TPU v7x, 512 devices: a whole 4x4x16 slice. The times are simulated.
512 devices in a mesh: section: 8 (over y, x_lo), dp: 64 (over z, x_hi, core).
Axes of the slice: x: 4 (x_hi: 2, x_lo: 2; x = x_hi * 2 + x_lo), y: 4, z: 16, core: 2. Of those that a mesh axis runs over, the one named last changes fastest.
Arguments:
- nodes: bfloat16 [256, 128, 512], P('dp'), may hold values from -120 to 120
- cotangent: bfloat16 [256, 128, 512], P('dp'), may hold values from -0.023925781 to 0.023925781
- w_qkv: bfloat16 [8, 512, 768], P('section'), may hold values from -0.25 to 0.25
- w_out: bfloat16 [8, 256, 512], P('section'), may hold values from -0.375 to 0.375
- tile_lists: int32 [256, 2, 2], P('dp'), may hold values from 0 to 1
- counts: int32 [256, 2], P('dp'), may hold values from 1 to 2
- virtual: int32 [256], P('dp'), may hold values from 0 to 1
Outputs:
- grad_qkv: bfloat16 [8, 512, 768], P('section')
- grad_out: bfloat16 [8, 256, 512], P('section')
Inputs may be any that keep to these rules, and one draw needn't show every extreme that they name: `tile_lists`: entries name row tiles of the same batch; entries at or beyond counts are padding.
All inputs are finite; a program needn't handle non-finite values.
Results may differ from a plain program's by a relative error of at most 0.022.
Values may be sent and summed in bfloat16 or wider, within the bound.
No kernel may reach another device: no remote copies, remote signals or barrier semaphores. Data moves between devices by JAX's collectives and lax.ppermute only.
A program may use at most 64 MiB of HBM per device.

v0:
```python
import jax
import jax.numpy as jnp
from jax import lax
from jax.sharding import PartitionSpec as P

HEADS = 4


EPSILON = 1e-06
TEMPER = 4.0


def shifted(value, axis, steps):
    count = lax.axis_size(axis)
    first, last = (max(0, -steps), min(count, count - steps))
    return lax.ppermute(value, axis, [(source, source + steps) for source in range(first, last)])


def unit_norm(values):
    return values * lax.rsqrt(jnp.mean(values * values, axis=-1, keepdims=True) + EPSILON)


def key_tables(tile_list, valid_count, virtual_tile):
    tile_count = tile_list.shape[0]
    first = jnp.broadcast_to(virtual_tile, (tile_count, 1))
    key_tiles = jnp.concatenate([first, tile_list], axis=1)
    slot_index = jnp.arange(tile_list.shape[1] + 1, dtype=jnp.int32)[None, :]
    key_valid = (slot_index == 0) | (slot_index - 1 < valid_count[:, None])
    return (key_tiles, key_valid)


def attend_layer(hidden_in, weight_qkv, weight_out, key_tiles, key_valid):
    row_count = hidden_in.shape[0]
    tile_count, listed = key_tiles.shape
    tile_rows = row_count // tile_count
    inner_width = weight_out.shape[0]
    head_size = inner_width // HEADS
    widened = hidden_in.astype(jnp.float32)
    normed = (
        widened * lax.rsqrt(jnp.mean(widened * widened, axis=-1, keepdims=True) + EPSILON)
    ).astype(jnp.bfloat16)
    projected = jnp.dot(normed, weight_qkv, preferred_element_type=jnp.float32)
    shaped = projected.reshape(tile_count, tile_rows, 3, HEADS, head_size)
    queries = (unit_norm(shaped[:, :, 0]) * (TEMPER / head_size)).astype(jnp.bfloat16)
    key_rows = unit_norm(shaped[:, :, 1]).astype(jnp.bfloat16)
    value_rows = shaped[:, :, 2].astype(jnp.bfloat16)
    gathered_keys = jnp.take(key_rows, key_tiles, axis=0).reshape(
        tile_count, listed * tile_rows, HEADS, head_size
    )
    gathered_values = jnp.take(value_rows, key_tiles, axis=0).reshape(
        tile_count, listed * tile_rows, HEADS, head_size
    )
    scores = jnp.einsum(
        "tqhd,tkhd->thqk", queries, gathered_keys, preferred_element_type=jnp.float32
    )
    open_keys = jnp.repeat(key_valid, tile_rows, axis=1)[:, None, None, :]
    exponent = jnp.where(open_keys, jnp.exp(scores), 0.0)
    attn = (exponent / jnp.sum(exponent, axis=-1, keepdims=True)).astype(jnp.bfloat16)
    mixed = jnp.einsum("thqk,tkhd->tqhd", attn, gathered_values, preferred_element_type=jnp.float32)
    mixed = mixed.astype(jnp.bfloat16).reshape(row_count, inner_width)
    return (widened + jnp.dot(mixed, weight_out, preferred_element_type=jnp.float32)).astype(
        jnp.bfloat16
    )


def per_device(nodes, cotangent, w_qkv, w_out, tile_lists, counts, virtual):
    sections = lax.axis_size("section")
    section_index = lax.axis_index("section")
    micro_count = nodes.shape[0]
    weight_qkv = w_qkv[0]
    weight_out = w_out[0]
    ticks = micro_count + sections - 1
    empty_rows = jnp.zeros(nodes.shape[1:], jnp.bfloat16)

    def tables(micro):
        return key_tables(tile_lists[micro], counts[micro], virtual[micro])

    def forward_tick(tick, state):
        received, stash = state
        micro = tick - section_index
        active = (micro >= 0) & (micro < micro_count)
        clipped = jnp.clip(micro, 0, micro_count - 1)
        incoming = jnp.where(section_index == 0, nodes[clipped], received)

        def compute():
            key_tiles, key_valid = tables(clipped)
            return attend_layer(incoming, weight_qkv, weight_out, key_tiles, key_valid)

        produced = lax.cond(active, compute, lambda: empty_rows)
        kept = jnp.where(active, incoming, stash[clipped])
        stash = stash.at[clipped].set(kept)
        received = shifted(produced, "section", 1)
        return (received, stash)

    ignored, stash = lax.fori_loop(0, ticks, forward_tick, (empty_rows, jnp.zeros_like(nodes)))

    def backward_tick(tick, state):
        received, sum_qkv, sum_out = state
        micro = tick - (sections - 1 - section_index)
        active = (micro >= 0) & (micro < micro_count)
        clipped = jnp.clip(micro, 0, micro_count - 1)
        incoming = jnp.where(section_index == sections - 1, cotangent[clipped], received)

        def pulled():
            key_tiles, key_valid = tables(clipped)

            def local_layer(hidden_in, weights_a, weights_b):
                return attend_layer(hidden_in, weights_a, weights_b, key_tiles, key_valid)

            unused, pullback = jax.vjp(local_layer, stash[clipped], weight_qkv, weight_out)
            return pullback(incoming)

        def skipped():
            return (empty_rows, jnp.zeros_like(weight_qkv), jnp.zeros_like(weight_out))

        grad_in, grad_first, grad_second = lax.cond(active, pulled, skipped)
        sum_qkv = sum_qkv + grad_first.astype(jnp.float32)
        sum_out = sum_out + grad_second.astype(jnp.float32)
        received = shifted(grad_in, "section", -1)
        return (received, sum_qkv, sum_out)

    start_state = (
        empty_rows,
        jnp.zeros(weight_qkv.shape, jnp.float32),
        jnp.zeros(weight_out.shape, jnp.float32),
    )
    ignored, sum_qkv, sum_out = lax.fori_loop(0, ticks, backward_tick, start_state)
    total_qkv, total_out = lax.psum((sum_qkv, sum_out), "dp")
    result_qkv = total_qkv.astype(jnp.bfloat16)
    result_out = total_out.astype(jnp.bfloat16)
    return (result_qkv[None], result_out[None])


def solution(mesh):
    in_specs = (
        P("dp", None, None),
        P("dp", None, None),
        P("section", None, None),
        P("section", None, None),
        P("dp", None, None),
        P("dp", None),
        P("dp"),
    )
    out_specs = (P("section", None, None), P("section", None, None))
    return jax.shard_map(
        per_device, mesh=mesh, in_specs=in_specs, out_specs=out_specs, check_vma=False
    )
```

profile of v0, /device:TPU:1, one launch (start us, length us, event | category | flops | bytes accessed | tf_op | source)
XLA Modules:
  0.0 936.7 jit_solution(1083721980510082463)
XLA Ops:
  4.2 183.1 %while.37 = (s32[]{:T(128)}, bf16[128,512]{1,0:T(8,128)(2,1)S(1)}, bf16[4,128,512]{2,1,0:T(8,128)(2,1)}, s32[]{:T(128)}, pred[]{:T(512)}, /*index=5*/bf16[4,128,...) while((s32[]{:T(128)}, bf16[128,512]{1,0:T(8,128)(2,1)S(1)}, ...), condition=%wide.region_8.10_spmd, body=%wide.region_0.9_spmd.sunk | while | flops 160992144 | bytes 10577601 | solution.py:95
  8.8 9.1 conditional.5
  25.7 9.2 conditional.5
  35.0 3.7 collective-permute-start
  45.2 9.2 conditional.5
  54.4 3.8 collective-permute-start
  64.7 9.2 conditional.5
  73.9 3.8 collective-permute-start
  84.2 13.0 %collective-permute-start = (bf16[128,512]{1,0:T(8,128)(2,1)S(1)}, bf16[128,512]{1,0:T(8,128)(2,1)S(1)}, u32[]{:S(2)}, u32[]{:S(2)}) collective-permute-start(bf16[128,512]{1,0:T(8,128)(2,1)S(1)} %get-tuple-element.1150), channel_id=1, source_target_pairs={{0,64},{64,128},{128,192},{192,256},{256,320},{320,384},{384,448},... | collective-permute-start | bytes 393224 | tf_op jit(solution)/shard_map/while/body/eval_jaxpr/ppermute | solution.py:16
  103.6 4.6 collective-permute-start
  115.7 12.9 %collective-permute-start = (bf16[128,512]{1,0:T(8,128)(2,1)S(1)}, bf16[128,512]{1,0:T(8,128)(2,1)S(1)}, u32[]{:S(2)}, u32[]{:S(2)}) collective-permute-start(bf16[128,512]{1,0:T(8,128)(2,1)S(1)} %get-tuple-element.1150), channel_id=1, source_target_pairs={{0,64},{64,128},{128,192},{192,256},{256,320},{320,384},{384,448},... | collective-permute-start | bytes 393224 | tf_op jit(solution)/shard_map/while/body/eval_jaxpr/ppermute | solution.py:16
  135.1 4.7 collective-permute-start
  146.3 10.2 %collective-permute-start = (bf16[128,512]{1,0:T(8,128)(2,1)S(1)}, bf16[128,512]{1,0:T(8,128)(2,1)S(1)}, u32[]{:S(2)}, u32[]{:S(2)}) collective-permute-start(bf16[128,512]{1,0:T(8,128)(2,1)S(1)} %get-tuple-element.1150), channel_id=1, source_target_pairs={{0,64},{64,128},{128,192},{192,256},{256,320},{320,384},{384,448},... | collective-permute-start | bytes 393224 | tf_op jit(solution)/shard_map/while/body/eval_jaxpr/ppermute | solution.py:16
  163.1 4.7 collective-permute-start
  174.3 11.1 %collective-permute-start = (bf16[128,512]{1,0:T(8,128)(2,1)S(1)}, bf16[128,512]{1,0:T(8,128)(2,1)S(1)}, u32[]{:S(2)}, u32[]{:S(2)}) collective-permute-start(bf16[128,512]{1,0:T(8,128)(2,1)S(1)} %get-tuple-element.1150), channel_id=1, source_target_pairs={{0,64},{64,128},{128,192},{192,256},{256,320},{320,384},{384,448},... | collective-permute-start | bytes 393224 | tf_op jit(solution)/shard_map/while/body/eval_jaxpr/ppermute | solution.py:16
  189.4 445.0 %while.38 = (s32[]{:T(128)}, bf16[128,512]{1,0:T(8,128)(2,1)}, f32[512,768]{1,0:T(8,128)}, f32[256,512]{1,0:T(8,128)}, s32[]{:T(128)}, /*index=5*/pred[]{:T(512)...) while((s32[]{:T(128)}, bf16[128,512]{1,0:T(8,128)(2,1)}, ...), condition=%wide.region_22.25_spmd.clone, body=%wide.region_9.24_spmd.clone.sunk | while | flops 451715904 | bytes 37956908 | solution.py:127
  193.1 4.4 collective-permute-done.1
  200.3 2.8 select_add_fusion.4
  203.3 9.3 collective-permute-done.1
  215.4 2.8 select_add_fusion.4
  218.4 3.3 collective-permute-done.1
  224.5 2.8 select_add_fusion.4
  227.5 8.1 collective-permute-done.1
  241.4 3.8 collective-permute-done.1
  251.0 7.6 collective-permute-done.1
  264.4 214.7 %collective-permute-done.1 = bf16[128,512]{1,0:T(8,128)(2,1)S(1)} collective-permute-done((bf16[128,512]{1,0:T(8,128)(2,1)}, bf16[128,512]{1,0:T(8,128)(2,1)S(1)}, u32[]{:S(2)}, u32[]{:S(2)}) %collective-permute-start.1) | collective-permute-done | bytes 131104 | tf_op jit(solution)/shard_map/while/body/eval_jaxpr/ppermute | solution.py:16
  479.7 31.3 %conditional.6 = (bf16[128,512]{1,0:T(8,128)(2,1)}, f32[512,768]{1,0:T(8,128)S(1)}, f32[256,512]{1,0:T(8,128)S(1)}) conditional(s32[]{:T(128)} %convert_element_type.356, () %tuple.148, (pred[]{:T(512)}, s32[]{:T(128)}, bf16[4,128,512]{2,1,0:T(8,128)(2,1)}, bf16[128,512]{1,0:T(8,128)(2,1)}, bf16[4,128,512]{2,1,0:T(8,128)(2,1)}, ...), branch_computations={%region_10.11_spmd, %region_11.23_spmd} | conditional | flops 450667328 | bytes 26422174 | solution.py:116
  515.3 2.9 collective-permute-done.1
  518.9 31.4 %conditional.6 = (bf16[128,512]{1,0:T(8,128)(2,1)}, f32[512,768]{1,0:T(8,128)S(1)}, f32[256,512]{1,0:T(8,128)S(1)}) conditional(s32[]{:T(128)} %convert_element_type.356, () %tuple.148, (pred[]{:T(512)}, s32[]{:T(128)}, bf16[4,128,512]{2,1,0:T(8,128)(2,1)}, bf16[128,512]{1,0:T(8,128)(2,1)}, bf16[4,128,512]{2,1,0:T(8,128)(2,1)}, ...), branch_computations={%region_10.11_spmd, %region_11.23_spmd} | conditional | flops 450667328 | bytes 26422174 | solution.py:116
  557.7 31.4 %conditional.6 = (bf16[128,512]{1,0:T(8,128)(2,1)}, f32[512,768]{1,0:T(8,128)S(1)}, f32[256,512]{1,0:T(8,128)S(1)}) conditional(s32[]{:T(128)} %convert_element_type.356, () %tuple.148, (pred[]{:T(512)}, s32[]{:T(128)}, bf16[4,128,512]{2,1,0:T(8,128)(2,1)}, bf16[128,512]{1,0:T(8,128)(2,1)}, bf16[4,128,512]{2,1,0:T(8,128)(2,1)}, ...), branch_computations={%region_10.11_spmd, %region_11.23_spmd} | conditional | flops 450667328 | bytes 26422174 | solution.py:116
  596.5 31.4 %conditional.6 = (bf16[128,512]{1,0:T(8,128)(2,1)}, f32[512,768]{1,0:T(8,128)S(1)}, f32[256,512]{1,0:T(8,128)S(1)}) conditional(s32[]{:T(128)} %convert_element_type.356, () %tuple.148, (pred[]{:T(512)}, s32[]{:T(128)}, bf16[4,128,512]{2,1,0:T(8,128)(2,1)}, bf16[128,512]{1,0:T(8,128)(2,1)}, bf16[4,128,512]{2,1,0:T(8,128)(2,1)}, ...), branch_computations={%region_10.11_spmd, %region_11.23_spmd} | conditional | flops 450667328 | bytes 26422174 | solution.py:116
  634.5 302.3 %all-reduce.7 = (bf16[512,768]{1,0:T(8,128)(2,1)}, bf16[256,512]{1,0:T(8,128)(2,1)}) all-reduce(f32[512,768]{1,0:T(8,128)} %get-tuple-element.666, f32[256,512]{1,0:T(8,128)} %get-tuple-element.667), channel_id=1, replica_groups=mesh['section'=8,'dp'=64] {'dp'}, use_global_device_ids=true, to_apply=%region_23.26 | all-reduce | flops 524288 | bytes 3145728 | tf_op jit(solution)/shard_map/psum | solution.py:128
  (726 shorter events, 301.9 us)
Async XLA Ops:
  17.9 3.2 collective-permute-start
  35.0 5.6 collective-permute-start
  54.4 5.7 collective-permute-start
  73.9 5.7 collective-permute-start
  84.2 14.9 %collective-permute-start = (bf16[128,512]{1,0:T(8,128)(2,1)S(1)}, bf16[128,512]{1,0:T(8,128)(2,1)S(1)}, u32[]{:S(2)}, u32[]{:S(2)}) collective-permute-start(bf16[128,512]{1,0:T(8,128)(2,1)S(1)} %get-tuple-element.1150), channel_id=1, source_target_pairs={{0,64},{64,128},{128,192},{192,256},{256,320},{320,384},{384,448},... | collective-permute-start | bytes 393224 | tf_op jit(solution)/shard_map/while/body/eval_jaxpr/ppermute | solution.py:16
  103.6 7.4 collective-permute-start
  115.7 14.9 %collective-permute-start = (bf16[128,512]{1,0:T(8,128)(2,1)S(1)}, bf16[128,512]{1,0:T(8,128)(2,1)S(1)}, u32[]{:S(2)}, u32[]{:S(2)}) collective-permute-start(bf16[128,512]{1,0:T(8,128)(2,1)S(1)} %get-tuple-element.1150), channel_id=1, source_target_pairs={{0,64},{64,128},{128,192},{192,256},{256,320},{320,384},{384,448},... | collective-permute-start | bytes 393224 | tf_op jit(solution)/shard_map/while/body/eval_jaxpr/ppermute | solution.py:16
  135.1 6.6 collective-permute-start
  146.3 12.1 %collective-permute-start = (bf16[128,512]{1,0:T(8,128)(2,1)S(1)}, bf16[128,512]{1,0:T(8,128)(2,1)S(1)}, u32[]{:S(2)}, u32[]{:S(2)}) collective-permute-start(bf16[128,512]{1,0:T(8,128)(2,1)S(1)} %get-tuple-element.1150), channel_id=1, source_target_pairs={{0,64},{64,128},{128,192},{192,256},{256,320},{320,384},{384,448},... | collective-permute-start | bytes 393224 | tf_op jit(solution)/shard_map/while/body/eval_jaxpr/ppermute | solution.py:16
  163.1 6.6 collective-permute-start
  174.3 13.1 %collective-permute-start = (bf16[128,512]{1,0:T(8,128)(2,1)S(1)}, bf16[128,512]{1,0:T(8,128)(2,1)S(1)}, u32[]{:S(2)}, u32[]{:S(2)}) collective-permute-start(bf16[128,512]{1,0:T(8,128)(2,1)S(1)} %get-tuple-element.1150), channel_id=1, source_target_pairs={{0,64},{64,128},{128,192},{192,256},{256,320},{320,384},{384,448},... | collective-permute-start | bytes 393224 | tf_op jit(solution)/shard_map/while/body/eval_jaxpr/ppermute | solution.py:16
  190.2 7.2 collective-permute-start.1
  199.0 13.7 %collective-permute-start.1 = (bf16[128,512]{1,0:T(8,128)(2,1)}, bf16[128,512]{1,0:T(8,128)(2,1)S(1)}, u32[]{:S(2)}, u32[]{:S(2)}) collective-permute-start(bf16[128,512]{1,0:T(8,128)(2,1)} %get-tuple-element.1042), channel_id=1, source_target_pairs={{64,0},{128,64},{192,128},{256,192},{320,256},{384,320},{448,384},... | collective-permute-start | bytes 393224 | tf_op jit(solution)/shard_map/while/body/eval_jaxpr/ppermute | solution.py:16
  203.3 9.4 copy-start.4
  214.1 7.6 collective-permute-start.1
  223.2 12.4 %collective-permute-start.1 = (bf16[128,512]{1,0:T(8,128)(2,1)}, bf16[128,512]{1,0:T(8,128)(2,1)S(1)}, u32[]{:S(2)}, u32[]{:S(2)}) collective-permute-start(bf16[128,512]{1,0:T(8,128)(2,1)} %get-tuple-element.1042), channel_id=1, source_target_pairs={{64,0},{128,64},{192,128},{256,192},{320,256},{384,320},{448,384},... | collective-permute-start | bytes 393224 | tf_op jit(solution)/shard_map/while/body/eval_jaxpr/ppermute | solution.py:16
  227.5 8.1 copy-start.4
  237.1 8.1 collective-permute-start.1
  246.7 11.9 %collective-permute-start.1 = (bf16[128,512]{1,0:T(8,128)(2,1)}, bf16[128,512]{1,0:T(8,128)(2,1)S(1)}, u32[]{:S(2)}, u32[]{:S(2)}) collective-permute-start(bf16[128,512]{1,0:T(8,128)(2,1)} %get-tuple-element.1042), channel_id=1, source_target_pairs={{64,0},{128,64},{192,128},{256,192},{320,256},{384,320},{448,384},... | collective-permute-start | bytes 393224 | tf_op jit(solution)/shard_map/while/body/eval_jaxpr/ppermute | solution.py:16
  251.0 7.6 copy-start.4
  260.0 219.0 %collective-permute-start.1 = (bf16[128,512]{1,0:T(8,128)(2,1)}, bf16[128,512]{1,0:T(8,128)(2,1)S(1)}, u32[]{:S(2)}, u32[]{:S(2)}) collective-permute-start(bf16[128,512]{1,0:T(8,128)(2,1)} %get-tuple-element.1042), channel_id=1, source_target_pairs={{64,0},{128,64},{192,128},{256,192},{320,256},{384,320},{448,384},... | collective-permute-start | bytes 393224 | tf_op jit(solution)/shard_map/while/body/eval_jaxpr/ppermute | solution.py:16
  264.4 214.7 %copy-start.4 = (f32[256,512]{1,0:T(8,128)}, f32[256,512]{1,0:T(8,128)S(1)}, u32[]{:S(2)}) copy-start(f32[256,512]{1,0:T(8,128)S(1)} %select_add_fusion.5) | copy-start | bytes 1572868 | tf_op jit(solution)/shard_map/while
  495.5 5.5 copy-start.13
  511.0 7.2 collective-permute-start.1
  534.8 5.5 copy-start.13
  550.2 6.8 collective-permute-start.1
  573.6 5.5 copy-start.10
  573.6 5.5 copy-start.13
  589.1 6.8 collective-permute-start.1
  612.4 5.5 copy-start.10
  612.4 5.5 copy-start.13
  627.9 5.9 collective-permute-start.1
  (107 other events, 215.2 us)
where the time goes:
time: 943 us; the launch traced here: 937 us
  blocking collectives  302 us (32%)
  waiting for transfers between devices  283 us (30%)
  other arithmetic  124 us (13%)
  local copies, waits for them, and re-layouts  90.9 us (10%)
  starting transfers between devices  87.8 us (9%)
  matrix products  45.8 us (5%)
    psum x1, blocking collectives, per_device(): total_qkv, total_out = lax.psum((sum_qkv, sum_out), 'dp')  302 us
    ppermute x22, waiting for transfers between devices, shifted(): lax.ppermute(value, axis, [(source, source + steps) for source in range(f...  283 us
    ppermute x22, starting transfers between devices, shifted(): lax.ppermute(value, axis, [(source, source + steps) for source in range(f...  87.8 us
    add x11, other arithmetic, backward_tick(): sum_qkv = sum_qkv + grad_first.astype(jnp.float32)  29.5 us
    scatter x11, other arithmetic, forward_tick(): stash = stash.at[clipped].set(kept)  24.8 us
  transfers between devices with their start and end apart: 22, of which 22 were waited for; matrix products, arithmetic and copies ran while one was open for 3% of the time, Pallas kernels for 0%

commit v1 on v0

v1 whole, which is shorter than its diff:
```python
import functools

import jax
import jax.numpy as jnp
from jax import lax
from jax.experimental import pallas as pl
from jax.experimental.pallas import tpu as pltpu
from jax.sharding import Mesh
from jax.sharding import PartitionSpec as P

HEADS = 4
EPSILON = 1e-06
TEMPER = 4.0
D = 512
INNER = 256
ROWS = 128
HEAD = INNER // HEADS
SCALE = TEMPER / HEAD
STAGE_LAYERS = 4
GROUP = ("yl", "xl")
STASH = ("normed", "inverse", "qkv", "scales", "attn", "mixed")
F32 = jnp.float32
BF16 = jnp.bfloat16


def stash_shapes():
    return {
        "normed": ((STAGE_LAYERS, ROWS, D), BF16),
        "inverse": ((STAGE_LAYERS, ROWS, 1), F32),
        "qkv": ((STAGE_LAYERS, 3, ROWS, INNER), BF16),
        "scales": ((STAGE_LAYERS, 2, ROWS, INNER), F32),
        "attn": ((STAGE_LAYERS, HEADS * ROWS, ROWS), BF16),
        "mixed": ((STAGE_LAYERS, ROWS, INNER), BF16),
    }


def dot(a, b, over_a=1, over_b=0):
    return lax.dot_general(a, b, (((over_a,), (over_b,)), ((), ())), preferred_element_type=F32)


def head_masks():
    lane = lax.broadcasted_iota(jnp.int32, (1, INNER), 1)
    return [jnp.where(lane // HEAD == h, 1.0, 0.0).astype(F32) for h in range(HEADS)]


def head_mean_matrix():
    row = lax.broadcasted_iota(jnp.int32, (INNER, INNER), 0) // HEAD
    col = lax.broadcasted_iota(jnp.int32, (INNER, INNER), 1) // HEAD
    return jnp.where(row == col, 1.0 / HEAD, 0.0).astype(BF16)


def spread(values, masks):
    return jnp.concatenate([values * m.astype(values.dtype) for m in masks], axis=0)


def gathered(stacked, masks):
    total = stacked[:ROWS] * masks[0]
    for h in range(1, HEADS):
        total = total + stacked[h * ROWS : (h + 1) * ROWS] * masks[h]
    return total


def multiplicities(batch, tile_lists, counts, virtual):
    def times(tile, key_tile):
        seen = (virtual[batch] == key_tile).astype(F32)
        for slot in range(2):
            named = tile_lists[batch, tile, slot] == key_tile
            seen = seen + (named & (slot < counts[batch, tile])).astype(F32)
        return seen

    row = lax.broadcasted_iota(jnp.int32, (ROWS, ROWS), 0) < ROWS // 2
    col = lax.broadcasted_iota(jnp.int32, (ROWS, ROWS), 1) < ROWS // 2
    one = jnp.where(
        row,
        jnp.where(col, times(0, 0), times(0, 1)),
        jnp.where(col, times(1, 0), times(1, 1)),
    )
    return jnp.concatenate([one] * HEADS, axis=0)


def forward_layer(layer, hidden, weight, times, masks, mean_matrix, stash):
    widened = hidden.astype(F32)
    inverse = lax.rsqrt(jnp.mean(widened * widened, axis=-1, keepdims=True) + EPSILON)
    normed = (widened * inverse).astype(BF16)
    q = dot(normed, weight(0))
    k = dot(normed, weight(1))
    v = dot(normed, weight(2)).astype(BF16)
    scale_q = lax.rsqrt(dot((q * q).astype(BF16), mean_matrix) + EPSILON) * SCALE
    scale_k = lax.rsqrt(dot((k * k).astype(BF16), mean_matrix) + EPSILON)
    qn = (q * scale_q).astype(BF16)
    kn = (k * scale_k).astype(BF16)
    scores = dot(spread(qn, masks), kn, 1, 1)
    exponent = jnp.exp(scores) * times
    attn = (exponent * (1.0 / jnp.sum(exponent, axis=-1, keepdims=True))).astype(BF16)
    mixed = gathered(dot(attn, v), masks).astype(BF16)
    stash["normed"][layer] = normed
    stash["inverse"][layer] = inverse
    stash["qkv"][layer, 0] = qn
    stash["qkv"][layer, 1] = kn
    stash["qkv"][layer, 2] = v
    stash["scales"][layer, 0] = scale_q
    stash["scales"][layer, 1] = scale_k
    stash["attn"][layer] = attn
    stash["mixed"][layer] = mixed
    out = weight(3)
    added = jnp.concatenate([dot(mixed, out[:INNER]), dot(mixed, out[INNER:])], axis=1)
    return (widened + added).astype(BF16)


def backward_layer(layer, grad, weight, masks, mean_matrix, stash, put):
    normed = stash["normed"][layer]
    inverse = stash["inverse"][layer]
    qn = stash["qkv"][layer, 0]
    kn = stash["qkv"][layer, 1]
    v = stash["qkv"][layer, 2]
    attn = stash["attn"][layer]
    mixed = stash["mixed"][layer]
    out = weight(3)
    low, high = grad[:, :INNER], grad[:, INNER:]
    grad_mixed = (dot(low, out[:INNER], 1, 1) + dot(high, out[INNER:], 1, 1)).astype(BF16)
    stacked = spread(grad_mixed, masks)
    grad_attn = dot(stacked, v, 1, 1)
    attn_wide = attn.astype(F32)
    inner = jnp.sum(attn_wide * grad_attn, axis=-1, keepdims=True)
    grad_scores = (attn_wide * (grad_attn - inner)).astype(BF16)
    grad_v = dot(attn, stacked, 0, 0).astype(BF16)
    grad_qn = gathered(dot(grad_scores, kn), masks)
    grad_kn = dot(grad_scores, spread(qn, masks), 0, 0)
    qw, kw = qn.astype(F32), kn.astype(F32)
    mean_q = dot((grad_qn * qw).astype(BF16), mean_matrix) * (1.0 / (SCALE * SCALE))
    mean_k = dot((grad_kn * kw).astype(BF16), mean_matrix)
    grad_q = (stash["scales"][layer, 0] * (grad_qn - qw * mean_q)).astype(BF16)
    grad_k = (stash["scales"][layer, 1] * (grad_kn - kw * mean_k)).astype(BF16)
    grad_normed = dot(grad_q, weight(0), 1, 1) + dot(grad_k, weight(1), 1, 1) + dot(grad_v, weight(2), 1, 1)
    wide = normed.astype(F32)
    mean = jnp.mean(grad_normed * wide, axis=-1, keepdims=True)
    result = (grad.astype(F32) + inverse * (grad_normed - wide * mean)).astype(BF16)
    put(0, dot(normed, grad_q, 0, 0).astype(BF16))
    put(1, dot(normed, grad_k, 0, 0).astype(BF16))
    put(2, dot(normed, grad_v, 0, 0).astype(BF16))
    put(3, jnp.concatenate([dot(mixed, low, 0, 0), dot(mixed, high, 0, 0)], axis=0).astype(BF16))
    return result


class Weights:
    def __init__(self, own, near, far, place, sems, me, core):
        self.place, self.me = place, me
        self.copies = []
        for r in range(STAGE_LAYERS):
            pair = []
            for side in range(2):
                if r == 0:
                    source, half = own.at[pl.ds(2 * side, 2)], side
                else:
                    source = near[r - 1] if side == 0 else far[r - 1]
                    half = core if side == 0 else 1 - core
                pair.append(pltpu.make_async_copy(source, place.at[r, half], sems.at[r, side]))
            self.copies.append(pair)

    def start(self):
        for pair in self.copies:
            for copy in pair:
                copy.start()

    def wait(self):
        for pair in self.copies:
            for copy in pair:
                copy.wait()

    def layer(self, index):
        r = index ^ self.me
        return lambda block: self.place[r, block // 2, block % 2]


class Gradients:
    def __init__(self, keep, send, place, sems, core):
        self.place, self.core, self.sems, self.outs = place, core, sems, (keep, send)
        self.copies = []

    def put(self, layer):
        def store(block, value):
            self.place[(block // 2) ^ self.core, layer, block % 2] = value

        return store

    def sent(self, layer):
        for side in range(2):
            copy = pltpu.make_async_copy(
                self.place.at[side, layer], self.outs[side].at[layer], self.sems.at[side, layer]
            )
            copy.start()
            self.copies.append(copy)

    def wait(self):
        for copy in self.copies:
            copy.wait()


def forward_kernel(info, tile_lists, counts, virtual, hidden_in, own, n1, n2, n3, f1, f2, f3, hidden_out, *rest):
    stash = dict(zip(STASH, rest[: len(STASH)]))
    place, sems = rest[len(STASH) :]
    batch, me, core = info[0], info[1], info[2]
    weights = Weights(own, (n1, n2, n3), (f1, f2, f3), place, sems, me, core)
    weights.start()
    masks, mean_matrix = head_masks(), head_mean_matrix()
    times = multiplicities(batch, tile_lists, counts, virtual)
    weights.wait()
    hidden = hidden_in[0]
    for layer in range(STAGE_LAYERS):
        hidden = forward_layer(layer, hidden, weights.layer(layer), times, masks, mean_matrix, stash)
    hidden_out[...] = hidden


def both_kernel(info, tile_lists, counts, virtual, hidden_in, grad_in, own, n1, n2, n3, f1, f2, f3, grad_out, keep, send, *rest):
    stash = dict(zip(STASH, rest[: len(STASH)]))
    place, sems, grads_place, grads_sems = rest[len(STASH) :]
    batch, me, core = info[0], info[1], info[2]
    weights = Weights(own, (n1, n2, n3), (f1, f2, f3), place, sems, me, core)
    weights.start()
    masks, mean_matrix = head_masks(), head_mean_matrix()
    times = multiplicities(batch, tile_lists, counts, virtual)
    grads = Gradients(keep, send, grads_place, grads_sems, core)
    weights.wait()
    hidden = hidden_in[...]
    for layer in range(STAGE_LAYERS):
        hidden = forward_layer(layer, hidden, weights.layer(layer), times, masks, mean_matrix, stash)
    grad = grad_in[0]
    for layer in reversed(range(STAGE_LAYERS)):
        grad = backward_layer(layer, grad, weights.layer(layer), masks, mean_matrix, stash, grads.put(layer))
        grads.sent(layer)
    grad_out[...] = grad
    grads.wait()


def backward_kernel(info, grad_in, *rest):
    stash = dict(zip(STASH, rest[: len(STASH)]))
    own, n1, n2, n3, f1, f2, f3, keep, send, place, sems, grads_place, grads_sems = rest[len(STASH) :]
    me, core = info[1], info[2]
    weights = Weights(own, (n1, n2, n3), (f1, f2, f3), place, sems, me, core)
    weights.start()
    masks, mean_matrix = head_masks(), head_mean_matrix()
    grads = Gradients(keep, send, grads_place, grads_sems, core)
    weights.wait()
    grad = grad_in[...]
    for layer in reversed(range(STAGE_LAYERS)):
        grad = backward_layer(layer, grad, weights.layer(layer), masks, mean_matrix, stash, grads.put(layer))
        grads.sent(layer)
    grads.wait()


def whole(shape):
    return pl.BlockSpec(shape, lambda *_: (0,) * len(shape))


def batch_block():
    return pl.BlockSpec((1, ROWS, D), lambda step, info, *_: (info[0], 0, 0))


ANYWHERE = pl.BlockSpec(memory_space=pl.ANY)
WEIGHT_SCRATCH = [
    pltpu.VMEM((STAGE_LAYERS, 2, 2, D, INNER), BF16),
    pltpu.SemaphoreType.DMA((STAGE_LAYERS, 2)),
]
GRAD_SCRATCH = [
    pltpu.VMEM((2, STAGE_LAYERS, 2, D, INNER), BF16),
    pltpu.SemaphoreType.DMA((2, STAGE_LAYERS)),
]
GRAD_HALF = jax.ShapeDtypeStruct((STAGE_LAYERS, 2, D, INNER), BF16)
HIDDEN = jax.ShapeDtypeStruct((ROWS, D), BF16)


def call(kernel, prefetched, in_specs, out_specs, out_shape, scratch, args):
    return pl.pallas_call(
        kernel,
        grid_spec=pltpu.PrefetchScalarGridSpec(
            num_scalar_prefetch=prefetched,
            grid=(1,),
            in_specs=in_specs,
            out_specs=out_specs,
            scratch_shapes=scratch,
        ),
        out_shape=out_shape,
        compiler_params=pltpu.CompilerParams(vmem_limit_bytes=48 * 2**20),
    )(*args)


def run_forward(info, tables, nodes, weights):
    shapes = stash_shapes()
    return call(
        forward_kernel,
        4,
        [batch_block()] + [ANYWHERE] * 7,
        [whole((ROWS, D))] + [whole(shapes[n][0]) for n in STASH],
        [HIDDEN] + [jax.ShapeDtypeStruct(*shapes[n]) for n in STASH],
        WEIGHT_SCRATCH,
        (info, *tables, nodes, *weights),
    )


def run_both(info, tables, hidden, cotangent, weights):
    shapes = stash_shapes()
    return call(
        both_kernel,
        4,
        [whole((ROWS, D)), batch_block()] + [ANYWHERE] * 7,
        [whole((ROWS, D)), ANYWHERE, ANYWHERE],
        [HIDDEN, GRAD_HALF, GRAD_HALF],
        [pltpu.VMEM(*shapes[n]) for n in STASH] + WEIGHT_SCRATCH + GRAD_SCRATCH,
        (info, *tables, hidden, cotangent, *weights),
    )


def run_backward(info, grad, stash, weights):
    shapes = stash_shapes()
    return call(
        backward_kernel,
        1,
        [whole((ROWS, D))] + [whole(shapes[n][0]) for n in STASH] + [ANYWHERE] * 7,
        [ANYWHERE, ANYWHERE],
        [GRAD_HALF, GRAD_HALF],
        WEIGHT_SCRATCH + GRAD_SCRATCH,
        (info, grad, *stash, *weights),
    )


def swapped(value, axis):
    return lax.ppermute(value, axis, [(0, 1), (1, 0)])


def fetched(half, flip_y, flip_x):
    axes = ("yl", "xl", "xh", "core")
    pairs = []
    for y in range(2):
        for x in range(2):
            for upper in range(2):
                for core in range(2):
                    there = upper ^ (core if flip_x else 0)
                    source = ((y * 2 + x) * 2 + upper) * 2 + core
                    target = (((y ^ flip_y) * 2 + (x ^ flip_x)) * 2 + there) * 2 + core
                    pairs.append((source, target))
    return lax.ppermute(half, axes, pairs)


def per_device(nodes, cotangent, w_qkv, w_out, tile_lists, counts, virtual):
    stage = lax.axis_index("yh")
    y, x, core = lax.axis_index("yl"), lax.axis_index("xl"), lax.axis_index("core")
    me = y * 2 + x
    batch = jnp.where(stage == 0, y, 1 - y) * 2 + x
    info = jnp.stack([batch, me, core]).astype(jnp.int32)
    tables = (tile_lists, counts, virtual)
    qkv, out = w_qkv[0], w_out[0]
    blocks = [qkv[:, i * INNER : (i + 1) * INNER] for i in range(3)]
    blocks.append(jnp.concatenate([out[:, :INNER], out[:, INNER:]], axis=0))
    own = jnp.stack(blocks)
    half = jnp.where(core == 0, own[:2], own[2:])
    near3 = fetched(half, 1, 1)
    near2 = fetched(half, 1, 0)
    near1 = fetched(half, 0, 1)
    near = (near1, near2, near3)
    far = tuple(swapped(value, "core") for value in near)
    weights = (own, *near, *far)

    hidden, *stash = run_forward(info, tables, nodes, weights)
    across = [(0, 3), (1, 2), (2, 1), (3, 0)]
    hidden = lax.ppermute(hidden, ("yh", "yl"), across)

    empty = jnp.zeros((STAGE_LAYERS, 2, D, INNER), BF16)
    grad, keep, send = lax.cond(
        stage == 1,
        lambda: tuple(run_both(info, tables, hidden, cotangent, weights)),
        lambda: (jnp.zeros((ROWS, D), BF16), empty, empty),
    )
    grad = lax.ppermute(grad, ("yh", "yl"), across)
    keep, send = lax.cond(
        stage == 0,
        lambda: tuple(run_backward(info, grad, stash, weights)),
        lambda: (keep, send),
    )

    def added(value, axis):
        return jnp.sum(value.astype(F32), axis=axis).astype(BF16)

    depth = lax.axis_size("z")
    total = (keep.astype(F32) + swapped(send, "core").astype(F32)).astype(BF16)
    total = lax.all_to_all(total.reshape(8, D, INNER), ("yl", "xl", "xh"), 0, 0, tiled=True)
    total = added(total, 0).reshape(depth, D // depth, INNER)
    total = added(lax.all_to_all(total, "z", 0, 0, tiled=True), 0)
    total = lax.all_to_all(jnp.broadcast_to(total, (depth, *total.shape)), "z", 0, 0, tiled=True)
    total = jnp.broadcast_to(total.reshape(1, D, INNER), (4, D, INNER))
    total = lax.all_to_all(total, ("core", "xh"), 0, 0, tiled=True)
    grad_qkv = jnp.concatenate([total[0], total[1], total[2]], axis=1)
    grad_out = jnp.concatenate([total[3, :INNER], total[3, INNER:]], axis=1)
    return (grad_qkv[None], grad_out[None])


def solution(mesh):
    depth = mesh.shape["dp"] // 4
    names = ("yh", "yl", "xl", "z", "xh", "core")
    cut = Mesh(mesh.devices.reshape(2, 2, 2, depth, 2, 2), names)
    section, dp = P(("yh", "yl", "xl")), P(("z", "xh", "core"))
    return jax.shard_map(
        per_device,
        mesh=cut,
        in_specs=(dp, dp, section, section, dp, dp, dp),
        out_specs=(section, section),
        check_vma=False,
    )
```

time: 943 us -> 207 us (0.22)
  waiting for transfers between devices: 283 us -> 24.3 us
  blocking collectives: 302 us -> 105 us
  other arithmetic: 124 us -> 5.2 us
  local copies, waits for them, and re-layouts: 90.9 us -> 3.67 us
  matrix products: 45.8 us -> 0 us
  starting transfers between devices: 87.8 us -> 48.1 us
  Pallas kernels: 0 us -> 18.9 us
    psum x1 -> x0, blocking collectives: 302 us -> none  [per_device(): total_qkv, total_out = lax.psum((sum_qkv, sum_out), 'dp')]
    ppermute x22 -> x9, waiting for transfers between devices: 283 us -> 24.3 us  [the longest x3 13.2 us: fetched(): return lax.ppermute(half, axes, pairs)]
    all_to_all x0 -> x4, blocking collectives: none -> 105 us  [the longest x1 29.9 us: per_device(): lax.all_to_all(total.reshape(8, D, INNER), ('yl', 'xl', 'xh'), 0, 0, tile...]
    dot_general x60 -> x0, matrix products: 45.8 us -> none  [the longest x16 17.3 us: attend_layer(): jnp.einsum('thqk,tkhd->tqhd', attn, gathered_values, preferred_element_ty...]
    ppermute x22 -> x9, starting transfers between devices: 87.8 us -> 48.1 us  [the longest x1 19 us: per_device(): grad = lax.ppermute(grad, ('yh', 'yl'), across)]
    add x22 -> x0, other arithmetic: 31.5 us -> none  [the longest x11 29.5 us: backward_tick(): sum_qkv = sum_qkv + grad_first.astype(jnp.float32)]
    scatter x11 -> x0, other arithmetic: 24.8 us -> none  [forward_tick(): stash = stash.at[clipped].set(kept)]
    dynamic_slice x19 -> x0, local copies, waits for them, and re-layouts: 20 us -> none  [the longest x11 10 us: forward_tick(): kept = jnp.where(active, incoming, stash[clipped])]
  transfers between devices with their start and end apart: 22 -> 9, of which waited for: 22 -> 6; matrix products, arithmetic and copies ran while one was open for 3% -> 1% of each run, Pallas kernels for 0% -> 0%
where the time goes in v1:
time: 207 us; the launch traced here: 206 us
  blocking collectives  105 us (51%)
  starting transfers between devices  48.1 us (23%)
  waiting for transfers between devices  24.3 us (12%)
  Pallas kernels  18.9 us (9%)
  other arithmetic  5.2 us (3%)
  local copies, waits for them, and re-layouts  3.67 us (2%)
    all_to_all x1, blocking collectives, per_device(): lax.all_to_all(total.reshape(8, D, INNER), ('yl', 'xl', 'xh'), 0, 0, tile...  29.9 us
    all_to_all x1, blocking collectives, per_device(): total = added(lax.all_to_all(total, 'z', 0, 0, tiled=True), 0)  27.5 us
    all_to_all x1, blocking collectives, per_device(): total = lax.all_to_all(total, ('core', 'xh'), 0, 0, tiled=True)  24.7 us
    all_to_all x1, blocking collectives, per_device(): lax.all_to_all(jnp.broadcast_to(total, (depth, *total.shape)), 'z', 0, 0,...  22.8 us
    ppermute x1, starting transfers between devices, per_device(): grad = lax.ppermute(grad, ('yh', 'yl'), across)  19 us
    pallas_call x2, Pallas kernels, call(): pl.pallas_call(kernel, grid_spec=pltpu.PrefetchScalarGridSpec(num_scalar_...  18.9 us
    ppermute x4, starting transfers between devices, swapped(): return lax.ppermute(value, axis, [(0, 1), (1, 0)])  14 us
    ppermute x3, waiting for transfers between devices, fetched(): return lax.ppermute(half, axes, pairs)  13.2 us
  transfers between devices with their start and end apart: 9, of which 6 were waited for; matrix products, arithmetic and copies ran while one was open for 1% of the time, Pallas kernels for 0%

profile of v1, /device:TPU:1, one launch (start us, length us, event | category | flops | bytes accessed | tf_op | source)
XLA Modules:
  0.0 206.0 jit_solution(13930389128960906784)
XLA Ops:
  0.7 1.0 fusion.1
  1.7 1.2 slice_bitcast_fusion.5
  3.0 6.4 %collective-permute-start.2 = (bf16[2,512,256]{2,1,0:T(8,128)(2,1)S(1)}, bf16[2,512,256]{2,1,0:T(8,128)(2,1)S(1)}, u32[]{:S(2)}, u32[]{:S(2)}) collective-permute-start(bf16[2,512,256]{2,1,0:T(8,128)(2,1)S(1)} %maximum_select_fusion), channel_id=1, source_target_pairs={{0,192},{1,195},{2,194},{3,193},{64,128},{65,131},{66,130},{67,129... | collective-permute-start | bytes 1572872 | tf_op jit(solution)/shard_map/ppermute | solution.py:341
  9.4 2.1 %collective-permute-start.1 = (bf16[2,512,256]{2,1,0:T(8,128)(2,1)S(1)}, bf16[2,512,256]{2,1,0:T(8,128)(2,1)S(1)}, u32[]{:S(2)}, u32[]{:S(2)}) collective-permute-start(bf16[2,512,256]{2,1,0:T(8,128)(2,1)S(1)} %maximum_select_fusion), channel_id=1, source_target_pairs={{0,128},{1,129},{2,130},{3,131},{64,192},{65,193},{66,194},{67,195... | collective-permute-start | bytes 1572872 | tf_op jit(solution)/shard_map/ppermute | solution.py:341
  11.5 2.0 collective-permute-start
  13.5 4.5 %collective-permute-done.2.n3 = bf16[2,512,256]{2,1,0:T(8,128)(2,1)S(1)} collective-permute-done((bf16[2,512,256]{2,1,0:T(8,128)(2,1)S(1)}, bf16[2,512,256]{2,1,0:T(8,128)(2,1)S(1)}, u32[]{:S(2)}, u32[]{:S(2)}) %collective-permute-start.2) | collective-permute-done | bytes 524320 | tf_op jit(solution)/shard_map/ppermute | solution.py:341
  18.0 6.3 %collective-permute-start.5 = (bf16[2,512,256]{2,1,0:T(8,128)(2,1)S(1)}, bf16[2,512,256]{2,1,0:T(8,128)(2,1)}, u32[]{:S(2)}, u32[]{:S(2)}) collective-permute-start(bf16[2,512,256]{2,1,0:T(8,128)(2,1)S(1)} %collective-permute-done.2.n3), channel_id=1, source_target_pairs={{0,1},{1,0},{2,3},{3,2},{4,5},{5,4},{6,7},{7,6},{8,9},{9,8},{10,11... | collective-permute-start | bytes 1572872 | tf_op jit(solution)/shard_map/ppermute | solution.py:327
  24.2 8.7 %collective-permute-done.1.n2 = bf16[2,512,256]{2,1,0:T(8,128)(2,1)S(1)} collective-permute-done((bf16[2,512,256]{2,1,0:T(8,128)(2,1)S(1)}, bf16[2,512,256]{2,1,0:T(8,128)(2,1)S(1)}, u32[]{:S(2)}, u32[]{:S(2)}) %collective-permute-start.1) | collective-permute-done | bytes 524320 | tf_op jit(solution)/shard_map/ppermute | solution.py:341
  33.0 2.4 %collective-permute-start.4 = (bf16[2,512,256]{2,1,0:T(8,128)(2,1)S(1)}, bf16[2,512,256]{2,1,0:T(8,128)(2,1)}, u32[]{:S(2)}, u32[]{:S(2)}) collective-permute-start(bf16[2,512,256]{2,1,0:T(8,128)(2,1)S(1)} %collective-permute-done.1.n2), channel_id=1, source_target_pairs={{0,1},{1,0},{2,3},{3,2},{4,5},{5,4},{6,7},{7,6},{8,9},{9,8},{10,11... | collective-permute-start | bytes 1572872 | tf_op jit(solution)/shard_map/ppermute | solution.py:327
  35.4 1.9 collective-permute-start.3
  37.6 1.2 pad_maximum_fusion.own
  38.9 0.4 collective-permute-done.3.f1
  39.4 7.7 %shard_map.87 = (bf16[128,512]{1,0:T(8,128)(2,1)S(1)}, bf16[4,128,512]{2,1,0:T(8,128)(2,1)}, f32[4,128,1]{2,1,0:T(8,128)S(1)}, bf16[4,3,128,256]{3,2,1,0:T(8,128...) custom-call(s32[3]{0:T(128)S(1)} %pad_add_fusion.info, ...), custom_call_target="tpu_custom_call" | custom-call | tf_op jit(solution)/shard_map/pallas_call | solution.py:273
  47.1 4.6 %collective-permute-start.6 = (bf16[128,512]{1,0:T(8,128)(2,1)S(1)}, bf16[128,512]{1,0:T(8,128)(2,1)S(1)}, u32[]{:S(2)}, u32[]{:S(2)}) collective-permute-start(bf16[128,512]{1,0:T(8,128)(2,1)S(1)} %get-tuple-element.111), channel_id=1, source_target_pairs={{0,384},{128,256},{256,128},{384,0},{1,385},{129,257},{257,129},{3... | collective-permute-start | bytes 393224 | tf_op jit(solution)/shard_map/ppermute | solution.py:365
  51.8 3.6 %collective-permute-done.6 = bf16[128,512]{1,0:T(8,128)(2,1)S(1)} collective-permute-done((bf16[128,512]{1,0:T(8,128)(2,1)S(1)}, bf16[128,512]{1,0:T(8,128)(2,1)S(1)}, u32[]{:S(2)}, u32[]{:S(2)}) %collective-permute-start.6) | collective-permute-done | bytes 131104 | tf_op jit(solution)/shard_map/ppermute | solution.py:365
  55.3 2.3 %conditional.2 = ((bf16[128,512]{1,0:T(8,128)(2,1)}, bf16[4,2,512,256]{3,2,1,0:T(8,128)(2,1)S(1)}, bf16[4,2,512,256]{3,2,1,0:T(8,128)(2,1)})) conditional(s32[]{:T(128)} %convert_element_type.23, () %tuple.27, (s32[3]{0:T(128)S(1)}, s32[4,2,2]{0,2,1:T(2,128)S(1)}, s32[4,2]{0,1:T(2,128)}, s32[4]{0:T(128)}, bf16[128,512]{1,0:T(8,128)(2,1)S(1)}, ...), branch_computations={%region_0.1_spmd, %region_1.2_spmd} | conditional | bytes 6816056 | solution.py:368
  55.3 0.7 broadcast.2
  56.0 1.5 broadcast_in_dim.6.clone
  57.6 19.0 %collective-permute-start.7 = (bf16[128,512]{1,0:T(8,128)(2,1)}, bf16[128,512]{1,0:T(8,128)(2,1)S(1)}, u32[]{:S(2)}, u32[]{:S(2)}) collective-permute-start(bf16[128,512]{1,0:T(8,128)(2,1)} %get-tuple-element.114), channel_id=1, source_target_pairs={{0,384},{128,256},{256,128},{384,0},{1,385},{129,257},{257,129},{3... | collective-permute-start | bytes 393224 | tf_op jit(solution)/shard_map/ppermute | solution.py:373
  76.7 3.1 %collective-permute-done.7 = bf16[128,512]{1,0:T(8,128)(2,1)S(1)} collective-permute-done((bf16[128,512]{1,0:T(8,128)(2,1)}, bf16[128,512]{1,0:T(8,128)(2,1)S(1)}, u32[]{:S(2)}, u32[]{:S(2)}) %collective-permute-start.7) | collective-permute-done | bytes 131104 | tf_op jit(solution)/shard_map/ppermute | solution.py:373
  79.8 11.2 %conditional.3 = ((bf16[4,2,512,256]{3,2,1,0:T(8,128)(2,1)}, bf16[4,2,512,256]{3,2,1,0:T(8,128)(2,1)S(1)})) conditional(s32[]{:T(128)} %convert_element_type.22, (bf16[4,2,512,256]{3,2,1,0:T(8,128)(2,1)}, bf16[4,2,512,256]{3,2,1,0:T(8,128)(2,1)S(1)}) %tuple.29, (s32[3]{0:T(128)S(1)}, bf16[128,512]{1,0:T(8,128)(2,1)S(1)}, ...), branch_computations={%region_2.3_spmd, %region_3.4_spmd} | conditional | bytes 24 | solution.py:374
  79.8 11.2 %branch_1_fun.3 = (bf16[4,2,512,256]{3,2,1,0:T(8,128)(2,1)S(1)}, bf16[4,2,512,256]{3,2,1,0:T(8,128)(2,1)}) custom-call(s32[3]{0:T(128)S(1)} %get-tuple-element.80.info, bf16[128,512]{1,0:T(8,128)(2,1)S(1)} %get-tuple-element.81.grad_in, bf16[4,128,512]{2,1,0:T(8,128)(2,1)} %get-tuple-element.82.rest_0_, f32[4,128,1]{2,1,0:T(8,128)S(1)} %get-tuple-element.83.rest_1_, ...), custom_call_target="tpu_custom_call" | custom-call | tf_op jit(solution)/shard_map/cond/branch_1_fun/pallas_call | solution.py:273
  91.0 3.4 %collective-permute-start.8 = (bf16[4,2,512,256]{3,2,1,0:T(8,128)(2,1)}, bf16[4,2,512,256]{3,2,1,0:T(8,128)(2,1)S(1)}, u32[]{:S(2)}, u32[]{:S(2)}) collective-permute-start(bf16[4,2,512,256]{3,2,1,0:T(8,128)(2,1)} %get-tuple-element.154), channel_id=1, source_target_pairs={{0,1},{1,0},{2,3},{3,2},{4,5},{5,4},{6,7},{7,6},{8,9},{9,8},{10,11... | collective-permute-start | bytes 6291464 | tf_op jit(solution)/shard_map/ppermute | solution.py:327
  94.4 4.0 %collective-permute-done.8 = bf16[4,2,512,256]{3,2,1,0:T(8,128)(2,1)S(1)} collective-permute-done((bf16[4,2,512,256]{3,2,1,0:T(8,128)(2,1)}, bf16[4,2,512,256]{3,2,1,0:T(8,128)(2,1)S(1)}, u32[]{:S(2)}, u32[]{:S(2)}) %collective-permute-start.8) | collective-permute-done | bytes 2097184 | tf_op jit(solution)/shard_map/ppermute | solution.py:327
  98.4 0.5 fusion
  98.9 29.9 %all_to_all.20 = bf16[8,512,256]{2,1,0:T(8,128)(2,1)S(1)} all-to-all(bf16[8,512,256]{2,1,0:T(8,128)(2,1)S(1)} %bitcast.30), channel_id=1, replica_groups=mesh['yh'=2,'yl'=2,'xl'=2,'z'=16,'xh'=2,'core'=2] {'yl','xl','xh'}, dimensions={0} | all-to-all | bytes 4194304 | tf_op jit(solution)/shard_map/all_to_all | solution.py:385
  128.8 0.4 reduce_sum.24
  129.2 27.5 %all_to_all.21 = bf16[16,32,256]{2,1,0:T(8,128)(2,1)S(1)} all-to-all(bf16[16,32,256]{2,1,0:T(8,128)(2,1)S(1)} %bitcast.31), channel_id=1, replica_groups=mesh['yh'=2,'yl'=2,'xl'=2,'z'=16,'xh'=2,'core'=2] {'z'}, dimensions={0} | all-to-all | bytes 524288 | tf_op jit(solution)/shard_map/all_to_all | solution.py:387
  156.7 22.8 %all_to_all.22 = bf16[16,32,256]{2,1,0:T(8,128)(2,1)S(1)} all-to-all(bf16[16,32,256]{2,1,0:T(8,128)(2,1)S(1)} %broadcast_in_dim.19), channel_id=1, replica_groups=mesh['yh'=2,'yl'=2,'xl'=2,'z'=16,'xh'=2,'core'=2] {'z'}, dimensions={0} | all-to-all | bytes 524288 | tf_op jit(solution)/shard_map/all_to_all | solution.py:388
  179.6 24.7 %all_to_all.23 = bf16[4,512,256]{2,1,0:T(8,128)(2,1)S(1)} all-to-all(bf16[4,512,256]{2,1,0:T(8,128)(2,1)S(1)} %broadcast_in_dim.21), channel_id=1, replica_groups=mesh['yh'=2,'yl'=2,'xl'=2,'z'=16,'xh'=2,'core'=2] {'core','xh'}, dimensions={0} | all-to-all | bytes 2097152 | tf_op jit(solution)/shard_map/all_to_all | solution.py:390
  204.3 0.7 maximum_bitcast_fusion.2
  205.1 0.9 maximum_bitcast_fusion
  (31 shorter events, 0.8 us)
Async XLA Ops:
  0.6 36.7 %copy-start.12 = (s32[4,2]{0,1:T(2,128)S(1)}, s32[4,2]{0,1:T(2,128)}, u32[]{:S(2)}) copy-start(s32[4,2]{0,1:T(2,128)} %param.16) | copy-start | bytes 100
  0.6 36.8 %copy-start.11 = (s32[4,2,2]{0,2,1:T(2,128)S(1)}, s32[4,2,2]{0,2,1:T(2,128)}, u32[]{:S(2)}) copy-start(s32[4,2,2]{0,2,1:T(2,128)} %param.15) | copy-start | bytes 196
  2.9 6.5 %copy-start.7 = (bf16[1,512,256]{2,1,0:T(8,128)(2,1)}, bf16[1,512,256]{2,1,0:T(8,128)(2,1)S(1)}, u32[]{:S(2)}) copy-start(bf16[1,512,256]{2,1,0:T(8,128)(2,1)S(1)} %get-tuple-element.162) | copy-start | bytes 786436
  2.9 6.5 %copy-start.8 = (bf16[1,512,256]{2,1,0:T(8,128)(2,1)}, bf16[1,512,256]{2,1,0:T(8,128)(2,1)S(1)}, u32[]{:S(2)}) copy-start(bf16[1,512,256]{2,1,0:T(8,128)(2,1)S(1)} %get-tuple-element.163) | copy-start | bytes 786436
  2.9 32.5 %copy-start.9 = (bf16[1,512,256]{2,1,0:T(8,128)(2,1)}, bf16[1,512,256]{2,1,0:T(8,128)(2,1)S(1)}, u32[]{:S(2)}) copy-start(bf16[1,512,256]{2,1,0:T(8,128)(2,1)S(1)} %get-tuple-element.166) | copy-start | bytes 786436
  2.9 36.5 %copy-start = (bf16[4,128,512]{2,1,0:T(8,128)(2,1)S(1)}, bf16[4,128,512]{2,1,0:T(8,128)(2,1)}, u32[]{:S(2)}) copy-start(bf16[4,128,512]{2,1,0:T(8,128)(2,1)} %hidden_in.1) | copy-start | bytes 1572868
  3.0 15.0 %collective-permute-start.2 = (bf16[2,512,256]{2,1,0:T(8,128)(2,1)S(1)}, bf16[2,512,256]{2,1,0:T(8,128)(2,1)S(1)}, u32[]{:S(2)}, u32[]{:S(2)}) collective-permute-start(bf16[2,512,256]{2,1,0:T(8,128)(2,1)S(1)} %maximum_select_fusion), channel_id=1, source_target_pairs={{0,192},{1,195},{2,194},{3,193},{64,128},{65,131},{66,130},{67,129... | collective-permute-start | bytes 1572872 | tf_op jit(solution)/shard_map/ppermute | solution.py:341
  9.4 23.6 %collective-permute-start.1 = (bf16[2,512,256]{2,1,0:T(8,128)(2,1)S(1)}, bf16[2,512,256]{2,1,0:T(8,128)(2,1)S(1)}, u32[]{:S(2)}, u32[]{:S(2)}) collective-permute-start(bf16[2,512,256]{2,1,0:T(8,128)(2,1)S(1)} %maximum_select_fusion), channel_id=1, source_target_pairs={{0,128},{1,129},{2,130},{3,131},{64,192},{65,193},{66,194},{67,195... | collective-permute-start | bytes 1572872 | tf_op jit(solution)/shard_map/ppermute | solution.py:341
  11.5 23.9 %collective-permute-start = (bf16[2,512,256]{2,1,0:T(8,128)(2,1)S(1)}, bf16[2,512,256]{2,1,0:T(8,128)(2,1)S(1)}, u32[]{:S(2)}, u32[]{:S(2)}) collective-permute-start(bf16[2,512,256]{2,1,0:T(8,128)(2,1)S(1)} %maximum_select_fusion), channel_id=1, source_target_pairs={{0,64},{1,67},{2,66},{3,65},{64,0},{65,3},{66,2},{67,1},{128,192},... | collective-permute-start | bytes 1572872 | tf_op jit(solution)/shard_map/ppermute | solution.py:341
  18.0 37.3 %copy-start.1 = (bf16[2,512,256]{2,1,0:T(8,128)(2,1)}, bf16[2,512,256]{2,1,0:T(8,128)(2,1)S(1)}, u32[]{:S(2)}) copy-start(bf16[2,512,256]{2,1,0:T(8,128)(2,1)S(1)} %collective-permute-done.2.n3) | copy-start | bytes 1572868
  18.0 20.9 %collective-permute-start.5 = (bf16[2,512,256]{2,1,0:T(8,128)(2,1)S(1)}, bf16[2,512,256]{2,1,0:T(8,128)(2,1)}, u32[]{:S(2)}, u32[]{:S(2)}) collective-permute-start(bf16[2,512,256]{2,1,0:T(8,128)(2,1)S(1)} %collective-permute-done.2.n3), channel_id=1, source_target_pairs={{0,1},{1,0},{2,3},{3,2},{4,5},{5,4},{6,7},{7,6},{8,9},{9,8},{10,11... | collective-permute-start | bytes 1572872 | tf_op jit(solution)/shard_map/ppermute | solution.py:327
  33.0 22.3 %copy-start.3 = (bf16[2,512,256]{2,1,0:T(8,128)(2,1)}, bf16[2,512,256]{2,1,0:T(8,128)(2,1)S(1)}, u32[]{:S(2)}) copy-start(bf16[2,512,256]{2,1,0:T(8,128)(2,1)S(1)} %collective-permute-done.1.n2) | copy-start | bytes 1572868
  33.0 5.9 %collective-permute-start.4 = (bf16[2,512,256]{2,1,0:T(8,128)(2,1)S(1)}, bf16[2,512,256]{2,1,0:T(8,128)(2,1)}, u32[]{:S(2)}, u32[]{:S(2)}) collective-permute-start(bf16[2,512,256]{2,1,0:T(8,128)(2,1)S(1)} %collective-permute-done.1.n2), channel_id=1, source_target_pairs={{0,1},{1,0},{2,3},{3,2},{4,5},{5,4},{6,7},{7,6},{8,9},{9,8},{10,11... | collective-permute-start | bytes 1572872 | tf_op jit(solution)/shard_map/ppermute | solution.py:327
  35.4 19.9 %copy-start.5 = (bf16[2,512,256]{2,1,0:T(8,128)(2,1)}, bf16[2,512,256]{2,1,0:T(8,128)(2,1)S(1)}, u32[]{:S(2)}) copy-start(bf16[2,512,256]{2,1,0:T(8,128)(2,1)S(1)} %collective-permute-done.n1) | copy-start | bytes 1572868
  35.4 3.9 %collective-permute-start.3 = (bf16[2,512,256]{2,1,0:T(8,128)(2,1)S(1)}, bf16[2,512,256]{2,1,0:T(8,128)(2,1)}, u32[]{:S(2)}, u32[]{:S(2)}) collective-permute-start(bf16[2,512,256]{2,1,0:T(8,128)(2,1)S(1)} %collective-permute-done.n1), channel_id=1, source_target_pairs={{0,1},{1,0},{2,3},{3,2},{4,5},{5,4},{6,7},{7,6},{8,9},{9,8},{10,11... | collective-permute-start | bytes 1572872 | tf_op jit(solution)/shard_map/ppermute | solution.py:327
  47.1 8.2 %collective-permute-start.6 = (bf16[128,512]{1,0:T(8,128)(2,1)S(1)}, bf16[128,512]{1,0:T(8,128)(2,1)S(1)}, u32[]{:S(2)}, u32[]{:S(2)}) collective-permute-start(bf16[128,512]{1,0:T(8,128)(2,1)S(1)} %get-tuple-element.111), channel_id=1, source_target_pairs={{0,384},{128,256},{256,128},{384,0},{1,385},{129,257},{257,129},{3... | collective-permute-start | bytes 393224 | tf_op jit(solution)/shard_map/ppermute | solution.py:365
  57.6 22.1 %collective-permute-start.7 = (bf16[128,512]{1,0:T(8,128)(2,1)}, bf16[128,512]{1,0:T(8,128)(2,1)S(1)}, u32[]{:S(2)}, u32[]{:S(2)}) collective-permute-start(bf16[128,512]{1,0:T(8,128)(2,1)} %get-tuple-element.114), channel_id=1, source_target_pairs={{0,384},{128,256},{256,128},{384,0},{1,385},{129,257},{257,129},{3... | collective-permute-start | bytes 393224 | tf_op jit(solution)/shard_map/ppermute | solution.py:373
  91.0 7.4 %collective-permute-start.8 = (bf16[4,2,512,256]{3,2,1,0:T(8,128)(2,1)}, bf16[4,2,512,256]{3,2,1,0:T(8,128)(2,1)S(1)}, u32[]{:S(2)}, u32[]{:S(2)}) collective-permute-start(bf16[4,2,512,256]{3,2,1,0:T(8,128)(2,1)} %get-tuple-element.154), channel_id=1, source_target_pairs={{0,1},{1,0},{2,3},{3,2},{4,5},{5,4},{6,7},{7,6},{8,9},{9,8},{10,11... | collective-permute-start | bytes 6291464 | tf_op jit(solution)/shard_map/ppermute | solution.py:327

commit v2 on v1

v2 whole, which is shorter than its diff:
```python
import jax
import jax.numpy as jnp
from jax import lax
from jax.experimental import pallas as pl
from jax.experimental.pallas import tpu as pltpu
from jax.sharding import Mesh
from jax.sharding import PartitionSpec as P

HEADS = 4
EPSILON = 1e-06
TEMPER = 4.0
D = 512
INNER = 256
ROWS = 128
HEAD = INNER // HEADS
SCALE = TEMPER / HEAD
STAGE_LAYERS = 4
F32 = jnp.float32
BF16 = jnp.bfloat16
STASH = {
    "normed": ((ROWS, D), BF16),
    "inverse": ((ROWS, ROWS), F32),
    "qkv": ((3, ROWS, INNER), BF16),
    "scales": ((2, ROWS, INNER), F32),
    "attn": ((HEADS * ROWS, ROWS), BF16),
    "mixed": ((ROWS, INNER), BF16),
}
TERMS = {
    "normed": ((ROWS, D), BF16),
    "mixed": ((ROWS, INNER), BF16),
    "grad_qkv": ((ROWS, 3 * INNER), BF16),
    "grad_out": ((ROWS, D), BF16),
}


def dot(a, b, over_a=1, over_b=0):
    return lax.dot_general(a, b, (((over_a,), (over_b,)), ((), ())), preferred_element_type=F32)


def head_masks():
    lane = lax.broadcasted_iota(jnp.int32, (1, INNER), 1)
    return [jnp.where(lane // HEAD == h, 1.0, 0.0).astype(F32) for h in range(HEADS)]


def head_mean_matrix():
    row = lax.broadcasted_iota(jnp.int32, (INNER, INNER), 0) // HEAD
    col = lax.broadcasted_iota(jnp.int32, (INNER, INNER), 1) // HEAD
    return jnp.where(row == col, 1.0 / HEAD, 0.0).astype(BF16)


def spread(values, masks):
    return jnp.concatenate([values * m.astype(values.dtype) for m in masks], axis=0)


def gathered(stacked, masks):
    total = stacked[:ROWS] * masks[0]
    for h in range(1, HEADS):
        total = total + stacked[h * ROWS : (h + 1) * ROWS] * masks[h]
    return total


def multiplicities(batch, tile_lists, counts, virtual):
    def times(tile, key_tile):
        seen = (virtual[batch] == key_tile).astype(F32)
        for slot in range(2):
            named = tile_lists[batch, tile, slot] == key_tile
            seen = seen + (named & (slot < counts[batch, tile])).astype(F32)
        return seen

    row = lax.broadcasted_iota(jnp.int32, (ROWS, ROWS), 0) < ROWS // 2
    col = lax.broadcasted_iota(jnp.int32, (ROWS, ROWS), 1) < ROWS // 2
    one = jnp.where(
        row,
        jnp.where(col, times(0, 0), times(0, 1)),
        jnp.where(col, times(1, 0), times(1, 1)),
    )
    return jnp.concatenate([one] * HEADS, axis=0)


def forward_layer(layer, hidden, weight, times, masks, mean_matrix, stash):
    widened = hidden.astype(F32)
    inverse = lax.rsqrt(jnp.mean(widened * widened, axis=-1, keepdims=True) + EPSILON)
    normed = (widened * inverse).astype(BF16)
    q = dot(normed, weight(0))
    k = dot(normed, weight(1))
    v = dot(normed, weight(2)).astype(BF16)
    scale_q = lax.rsqrt(dot((q * q).astype(BF16), mean_matrix) + EPSILON) * SCALE
    scale_k = lax.rsqrt(dot((k * k).astype(BF16), mean_matrix) + EPSILON)
    qn = (q * scale_q).astype(BF16)
    kn = (k * scale_k).astype(BF16)
    scores = dot(spread(qn, masks), kn, 1, 1)
    exponent = jnp.exp(scores) * times
    attn = (exponent * (1.0 / jnp.sum(exponent, axis=-1, keepdims=True))).astype(BF16)
    mixed = gathered(dot(attn, v), masks).astype(BF16)
    stash["normed"][layer] = normed
    stash["inverse"][layer] = jnp.broadcast_to(inverse, (ROWS, ROWS))
    stash["qkv"][layer, 0] = qn
    stash["qkv"][layer, 1] = kn
    stash["qkv"][layer, 2] = v
    stash["scales"][layer, 0] = scale_q
    stash["scales"][layer, 1] = scale_k
    stash["attn"][layer] = attn
    stash["mixed"][layer] = mixed
    out = weight(3)
    added = jnp.concatenate([dot(mixed, out[:INNER]), dot(mixed, out[INNER:])], axis=1)
    return (widened + added).astype(BF16)


def backward_layer(layer, grad, weight, masks, mean_matrix, stash):
    inverse = stash["inverse"][layer][:, :1]
    qn = stash["qkv"][layer, 0]
    kn = stash["qkv"][layer, 1]
    v = stash["qkv"][layer, 2]
    attn = stash["attn"][layer]
    out = weight(3)
    low, high = grad[:, :INNER], grad[:, INNER:]
    grad_mixed = (dot(low, out[:INNER], 1, 1) + dot(high, out[INNER:], 1, 1)).astype(BF16)
    stacked = spread(grad_mixed, masks)
    grad_attn = dot(stacked, v, 1, 1)
    attn_wide = attn.astype(F32)
    inner = jnp.sum(attn_wide * grad_attn, axis=-1, keepdims=True)
    grad_scores = (attn_wide * (grad_attn - inner)).astype(BF16)
    grad_v = dot(attn, stacked, 0, 0).astype(BF16)
    grad_qn = gathered(dot(grad_scores, kn), masks)
    grad_kn = dot(grad_scores, spread(qn, masks), 0, 0)
    qw, kw = qn.astype(F32), kn.astype(F32)
    mean_q = dot((grad_qn * qw).astype(BF16), mean_matrix) * (1.0 / (SCALE * SCALE))
    mean_k = dot((grad_kn * kw).astype(BF16), mean_matrix)
    grad_q = (stash["scales"][layer, 0] * (grad_qn - qw * mean_q)).astype(BF16)
    grad_k = (stash["scales"][layer, 1] * (grad_kn - kw * mean_k)).astype(BF16)
    grad_normed = dot(grad_q, weight(0), 1, 1) + dot(grad_k, weight(1), 1, 1) + dot(grad_v, weight(2), 1, 1)
    wide = stash["normed"][layer].astype(F32)
    mean = jnp.mean(grad_normed * wide, axis=-1, keepdims=True)
    result = (grad.astype(F32) + inverse * (grad_normed - wide * mean)).astype(BF16)
    return result, jnp.concatenate([grad_q, grad_k, grad_v], axis=1)


class Weights:
    def __init__(self, own, beside, near2, far2, near3, far3, place, sems, me, core, order):
        self.place, self.me, self.order = place, me, order

        def halves(r, near, far):
            return [(near, place.at[r, pl.ds(2 * core, 2)]), (far, place.at[r, pl.ds(2 * (1 - core), 2)])]

        pairs = [
            [(own, place.at[0])],
            [(beside, place.at[1])],
            halves(2, near2, far2),
            halves(3, near3, far3),
        ]
        self.copies = [
            [pltpu.make_async_copy(src, dst, sems.at[r, i]) for i, (src, dst) in enumerate(listed)]
            for r, listed in enumerate(pairs)
        ]

    def each(self, layer, act):
        for r in range(STAGE_LAYERS):

            @pl.when((layer ^ self.me) == r)
            def _(r=r):
                for copy in self.copies[r]:
                    act(copy)

    def start(self):
        for layer in self.order:
            self.each(layer, lambda copy: copy.start())

    def wait(self, layer):
        self.each(layer, lambda copy: copy.wait())

    def layer(self, index):
        r = index ^ self.me
        return lambda block: self.place[r, block]


class Sheets:
    def __init__(self, names, outside, inside, sems, inward):
        self.copies = []
        for layer in range(STAGE_LAYERS):
            listed = []
            for i in range(len(names)):
                a, b = outside[i].at[layer], inside[i].at[layer]
                listed.append(pltpu.make_async_copy(*((a, b) if inward else (b, a)), sems.at[i, layer]))
            self.copies.append(listed)
        self.refs = dict(zip(names, inside))

    def start(self, layer):
        for copy in self.copies[layer]:
            copy.start()

    def wait(self, layer):
        for copy in self.copies[layer]:
            copy.wait()


def weight_gradients(layer, normed, mixed, grad_qkv, grad_out, place, core):
    full = dot(normed, grad_qkv, 0, 0).astype(BF16)
    for block in range(3):
        place[(block // 2) ^ core, layer, block % 2] = full[:, block * INNER : (block + 1) * INNER]
    last = dot(mixed, grad_out, 0, 0).astype(BF16)
    place[1 ^ core, layer, 1, :INNER] = last[:, :INNER]
    place[1 ^ core, layer, 1, INNER:] = last[:, INNER:]


def pack_kernel(info, qkv, out, own, half, sems):
    blocks = [[(qkv.at[0, :, pl.ds(b * INNER, INNER)], slice(None))] for b in range(3)]
    blocks.append([(out.at[0, :, pl.ds(i * INNER, INNER)], pl.ds(i * INNER, INNER)) for i in range(2)])
    copies = []
    for block in range(4):
        for i, (source, rows) in enumerate(blocks[block]):
            copies.append(pltpu.make_async_copy(source, own.at[block, rows], sems.at[0, block + i]))
    for copy in copies:
        copy.start()
    for side in range(2):

        @pl.when(info[2] == side)
        def _(side=side):
            chosen = []
            for slot in range(2):
                for i, (source, rows) in enumerate(blocks[2 * side + slot]):
                    chosen.append(pltpu.make_async_copy(source, half.at[slot, rows], sems.at[1, slot + i]))
            for copy in chosen:
                copy.start()
            for copy in chosen:
                copy.wait()

    for copy in copies:
        copy.wait()


def forward_kernel(info, tile_lists, counts, virtual, hidden_in, *rest):
    weights = Weights(*rest[:6], *rest[-4:-2], info[1], info[2], range(STAGE_LAYERS))
    hidden_out, outside, inside = rest[6], rest[7 : 7 + len(STASH)], rest[7 + len(STASH) : 7 + 2 * len(STASH)]
    sheets = Sheets(STASH, outside, inside, rest[-2], False)
    weights.start()
    masks, mean_matrix = head_masks(), head_mean_matrix()
    times = rest[-1]
    times[...] = multiplicities(info[0], tile_lists, counts, virtual)
    hidden = hidden_in[0]
    for layer in range(STAGE_LAYERS):
        weights.wait(layer)
        hidden = forward_layer(layer, hidden, weights.layer(layer), times[...], masks, mean_matrix, sheets.refs)
        sheets.start(layer)
    hidden_out[...] = hidden
    for layer in range(STAGE_LAYERS):
        sheets.wait(layer)


def chain_kernel(info, tile_lists, counts, virtual, hidden_in, grad_in, *rest):
    weights = Weights(*rest[:6], *rest[-4:-2], info[1], info[2], range(STAGE_LAYERS))
    grad_out, outside = rest[6], rest[7 : 7 + len(TERMS)]
    stash = dict(zip(STASH, rest[7 + len(TERMS) :][: len(STASH)]))
    extra = rest[7 + len(TERMS) + len(STASH) :][:2]
    sheets = Sheets(TERMS, outside, (stash["normed"], stash["mixed"], *extra), rest[-2], False)
    weights.start()
    masks, mean_matrix = head_masks(), head_mean_matrix()
    times = rest[-1]
    times[...] = multiplicities(info[0], tile_lists, counts, virtual)
    hidden = hidden_in[...]
    for layer in range(STAGE_LAYERS):
        weights.wait(layer)
        hidden = forward_layer(layer, hidden, weights.layer(layer), times[...], masks, mean_matrix, stash)
    grad = grad_in[0]
    for layer in reversed(range(STAGE_LAYERS)):
        sheets.refs["grad_out"][layer] = grad
        grad, grad_qkv = backward_layer(layer, grad, weights.layer(layer), masks, mean_matrix, stash)
        sheets.refs["grad_qkv"][layer] = grad_qkv
        sheets.start(layer)
    grad_out[...] = grad
    for layer in range(STAGE_LAYERS):
        sheets.wait(layer)


def gradient_kernel(info, *rest):
    outside, (keep, send), inside = rest[: len(TERMS)], rest[len(TERMS) :][:2], rest[len(TERMS) + 2 : -3]
    place, in_sems, out_sems = rest[-3:]
    sheets = Sheets(TERMS, outside, inside, in_sems, True)
    results = Sheets(("keep", "send"), (keep, send), (place.at[0], place.at[1]), out_sems, False)
    for layer in range(STAGE_LAYERS):
        sheets.start(layer)
    for layer in range(STAGE_LAYERS):
        sheets.wait(layer)
        weight_gradients(layer, *(sheets.refs[n][layer] for n in TERMS), place, info[2])
        results.start(layer)
    for layer in range(STAGE_LAYERS):
        results.wait(layer)


def backward_kernel(info, grad_in, *rest):
    order = tuple(reversed(range(STAGE_LAYERS)))
    count = len(STASH)
    outside, given, (keep, send) = rest[:count], rest[count:][:6], rest[count + 6 :][:2]
    inside = rest[count + 8 :][:count]
    weight_place, weight_sems, place, in_sems, out_sems = rest[-5:]
    weights = Weights(*given, weight_place, weight_sems, info[1], info[2], order)
    sheets = Sheets(STASH, outside, inside, in_sems, True)
    results = Sheets(("keep", "send"), (keep, send), (place.at[0], place.at[1]), out_sems, False)
    for layer in order:
        sheets.start(layer)
        weights.each(layer, lambda copy: copy.start())
    masks, mean_matrix = head_masks(), head_mean_matrix()
    grad = grad_in[...]
    for layer in order:
        sheets.wait(layer)
        weights.wait(layer)
        before = grad
        grad, grad_qkv = backward_layer(layer, grad, weights.layer(layer), masks, mean_matrix, sheets.refs)
        weight_gradients(
            layer, sheets.refs["normed"][layer], sheets.refs["mixed"][layer], grad_qkv, before, place, info[2]
        )
        results.start(layer)
    for layer in order:
        results.wait(layer)


ANYWHERE = pl.BlockSpec(memory_space=pl.ANY)
HIDDEN = jax.ShapeDtypeStruct((ROWS, D), BF16)
HIDDEN_BLOCK = pl.BlockSpec((ROWS, D), lambda *_: (0, 0))
BATCH_BLOCK = pl.BlockSpec((1, ROWS, D), lambda step, info, *_: (info[0], 0, 0))
GRAD_HALF = jax.ShapeDtypeStruct((STAGE_LAYERS, 2, D, INNER), BF16)
WEIGHT_SCRATCH = [
    pltpu.VMEM((STAGE_LAYERS, 4, D, INNER), BF16),
    pltpu.SemaphoreType.DMA((STAGE_LAYERS, 2)),
]
GRAD_PLACE = pltpu.VMEM((2, STAGE_LAYERS, 2, D, INNER), BF16)
TIMES = pltpu.VMEM((HEADS * ROWS, ROWS), F32)


def layered(sizes, make):
    return [make((STAGE_LAYERS, *shape), kind) for shape, kind in sizes.values()]


def semaphores(count):
    return pltpu.SemaphoreType.DMA((count, STAGE_LAYERS))


def call(kernel, prefetched, in_specs, out_specs, out_shape, scratch, args):
    return pl.pallas_call(
        kernel,
        grid_spec=pltpu.PrefetchScalarGridSpec(
            num_scalar_prefetch=prefetched,
            grid=(1,),
            in_specs=in_specs,
            out_specs=out_specs,
            scratch_shapes=scratch,
        ),
        out_shape=out_shape,
        compiler_params=pltpu.CompilerParams(vmem_limit_bytes=48 * 2**20),
    )(*args)


def run_pack(info, w_qkv, w_out):
    shapes = [jax.ShapeDtypeStruct((blocks, D, INNER), BF16) for blocks in (4, 2)]
    sems = [pltpu.SemaphoreType.DMA((2, 5))]
    return call(pack_kernel, 1, [ANYWHERE] * 2, [ANYWHERE] * 2, shapes, sems, (info, w_qkv, w_out))


def run_forward(info, tables, nodes, weights):
    return call(
        forward_kernel,
        4,
        [BATCH_BLOCK] + [ANYWHERE] * 6,
        [HIDDEN_BLOCK] + [ANYWHERE] * len(STASH),
        [HIDDEN] + layered(STASH, jax.ShapeDtypeStruct),
        layered(STASH, pltpu.VMEM) + WEIGHT_SCRATCH + [semaphores(len(STASH)), TIMES],
        (info, *tables, nodes, *weights),
    )


def run_chain(info, tables, hidden, cotangent, weights):
    return call(
        chain_kernel,
        4,
        [HIDDEN_BLOCK, BATCH_BLOCK] + [ANYWHERE] * 6,
        [HIDDEN_BLOCK] + [ANYWHERE] * len(TERMS),
        [HIDDEN] + layered(TERMS, jax.ShapeDtypeStruct),
        layered(STASH, pltpu.VMEM) + layered(TERMS, pltpu.VMEM)[2:] + WEIGHT_SCRATCH + [semaphores(len(TERMS)), TIMES],
        (info, *tables, hidden, cotangent, *weights),
    )


def run_gradients(info, terms):
    return call(
        gradient_kernel,
        1,
        [ANYWHERE] * len(TERMS),
        [ANYWHERE] * 2,
        [GRAD_HALF] * 2,
        layered(TERMS, pltpu.VMEM) + [GRAD_PLACE, semaphores(len(TERMS)), semaphores(2)],
        (info, *terms),
    )


def run_backward(info, grad, stash, weights):
    return call(
        backward_kernel,
        1,
        [HIDDEN_BLOCK] + [ANYWHERE] * (len(STASH) + 6),
        [ANYWHERE] * 2,
        [GRAD_HALF] * 2,
        layered(STASH, pltpu.VMEM) + WEIGHT_SCRATCH + [GRAD_PLACE, semaphores(len(STASH)), semaphores(2)],
        (info, grad, *stash, *weights),
    )


def swapped(value, axis):
    return lax.ppermute(value, axis, [(0, 1), (1, 0)])


def fetched(value, flip_y, flip_x):
    axes = ("yl", "xl", "xh", "core")
    pairs = []
    for y in range(2):
        for x in range(2):
            for upper in range(2):
                for core in range(2):
                    there = upper ^ (core if flip_x else 0)
                    source = ((y * 2 + x) * 2 + upper) * 2 + core
                    target = (((y ^ flip_y) * 2 + (x ^ flip_x)) * 2 + there) * 2 + core
                    pairs.append((source, target))
    return lax.ppermute(value, axes, pairs)


def per_device(nodes, cotangent, w_qkv, w_out, tile_lists, counts, virtual):
    stage = lax.axis_index("yh")
    y, x, core = lax.axis_index("yl"), lax.axis_index("xl"), lax.axis_index("core")
    me = y * 2 + x
    batch = jnp.where(stage == 0, y, 1 - y) * 2 + x
    info = jnp.stack([batch, me, core]).astype(jnp.int32)
    tables = (tile_lists, counts, virtual)
    own, half = run_pack(info, w_qkv, w_out)
    near2 = fetched(half, 1, 0)
    near3 = fetched(half, 1, 1)
    beside = fetched(own, 0, 1)
    far2, far3 = swapped(near2, "core"), swapped(near3, "core")
    weights = (own, beside, near2, far2, near3, far3)

    hidden, *stash = run_forward(info, tables, nodes, weights)
    across = [(0, 3), (1, 2), (2, 1), (3, 0)]
    hidden = lax.ppermute(hidden, ("yh", "yl"), across)
    grad, *terms = run_chain(info, tables, hidden, cotangent, weights)
    grad = lax.ppermute(grad, ("yh", "yl"), across)
    keep, send = lax.cond(
        stage == 0,
        lambda: tuple(run_backward(info, grad, stash, weights)),
        lambda: tuple(run_gradients(info, terms)),
    )

    def added(value, axis):
        return jnp.sum(value.astype(F32), axis=axis).astype(BF16)

    def repeated(value, times):
        return jnp.broadcast_to(value, (times, *value.shape))

    far, near = lax.axis_size("zh"), lax.axis_size("zl")
    piece = D // (far * near)
    total = (keep.astype(F32) + swapped(send, "core").astype(F32)).astype(BF16)
    total = lax.all_to_all(total.reshape(8, D, INNER), ("yl", "xl", "xh"), 0, 0, tiled=True)
    total = added(total, 0).reshape(far * near, piece, INNER)
    total = added(lax.all_to_all(total, ("zl", "zh"), 0, 0, tiled=True), 0)
    total = lax.all_to_all(repeated(total, far), "zh", 0, 0, tiled=True)
    total = lax.all_to_all(repeated(total, 2 * near), ("xh", "zl"), 0, 0, tiled=True)
    mine = total.reshape(2, D, INNER)
    other = swapped(mine, "core")
    first, second = jnp.where(core == 0, mine, other), jnp.where(core == 0, other, mine)
    grad_qkv = jnp.concatenate([first[0], first[1], second[0]], axis=1)
    grad_out = jnp.concatenate([second[1, :INNER], second[1, INNER:]], axis=1)
    return (grad_qkv[None], grad_out[None])


def solution(mesh):
    depth = mesh.shape["dp"] // 4
    near = min(depth, 4)
    names = ("yh", "yl", "xl", "zh", "zl", "xh", "core")
    cut = Mesh(mesh.devices.reshape(2, 2, 2, depth // near, near, 2, 2), names)
    section, dp = P(("yh", "yl", "xl")), P(("zh", "zl", "xh", "core"))
    return jax.shard_map(
        per_device,
        mesh=cut,
        in_specs=(dp, dp, section, section, dp, dp, dp),
        out_specs=(section, section),
        check_vma=False,
    )
```

time: 207 us -> 199 us (0.961)
  starting transfers between devices: 48.1 us -> 39.4 us
  Pallas kernels: 18.9 us -> 27.2 us
  blocking collectives: 105 us -> 98.2 us
  other arithmetic: 5.2 us -> 2.75 us
    ppermute x1, starting transfers between devices: 19 us -> 5.01 us  [per_device(): grad = lax.ppermute(grad, ('yh', 'yl'), across)]
    pallas_call x2 -> x4, Pallas kernels: 18.9 us -> 27.2 us  [call(): pl.pallas_call(kernel, grid_spec=pltpu.PrefetchScalarGridSpec(num_scalar_...]
    all_to_all x3, blocking collectives: 75 us -> 68.3 us  [the longest x1 28.1 us: per_device(): total = added(lax.all_to_all(total, ('zl', 'zh'), 0, 0, tiled=True), 0)]
    unnamed x20 -> x12, local copies, waits for them, and re-layouts: 0.24 us -> 5.32 us
    ppermute x4, starting transfers between devices: 14 us -> 18.6 us  [swapped(): return lax.ppermute(value, axis, [(0, 1), (1, 0)])]
    another operation x2 -> x0, other arithmetic: 2.43 us -> none  [per_device(): own = jnp.stack(blocks)]
  transfers between devices with their start and end apart: 9 -> 9, of which waited for: 6 -> 7; matrix products, arithmetic and copies ran while one was open for 1% -> 1% of each run, Pallas kernels for 0% -> 0%
where the time goes in v2:
time: 199 us; the launch traced here: 198 us
  blocking collectives  98.2 us (49%)
  starting transfers between devices  39.4 us (20%)
  Pallas kernels  27.2 us (14%)
  waiting for transfers between devices  24.6 us (12%)
  local copies, waits for them, and re-layouts  5.45 us (3%)
  other arithmetic  2.75 us (1%)
    all_to_all x1, blocking collectives, per_device(): lax.all_to_all(total.reshape(8, D, INNER), ('yl', 'xl', 'xh'), 0, 0, tile...  29.9 us
    all_to_all x1, blocking collectives, per_device(): total = added(lax.all_to_all(total, ('zl', 'zh'), 0, 0, tiled=True), 0)  28.1 us
    pallas_call x4, Pallas kernels, call(): pl.pallas_call(kernel, grid_spec=pltpu.PrefetchScalarGridSpec(num_scalar_...  27.2 us
    all_to_all x1, blocking collectives, per_device(): total = lax.all_to_all(repeated(total, far), 'zh', 0, 0, tiled=True)  21.8 us
    ppermute x4, starting transfers between devices, swapped(): return lax.ppermute(value, axis, [(0, 1), (1, 0)])  18.6 us
    all_to_all x1, blocking collectives, per_device(): lax.all_to_all(repeated(total, 2 * near), ('xh', 'zl'), 0, 0, tiled=True)  18.4 us
    ppermute x3, waiting for transfers between devices, fetched(): return lax.ppermute(value, axes, pairs)  13.2 us
    ppermute x3, starting transfers between devices, fetched(): return lax.ppermute(value, axes, pairs)  10.3 us
  transfers between devices with their start and end apart: 9, of which 7 were waited for; matrix products, arithmetic and copies ran while one was open for 1% of the time, Pallas kernels for 0%

profile of v2, /device:TPU:1, one launch (start us, length us, event | category | flops | bytes accessed | tf_op | source)
XLA Modules:
  0.0 198.3 jit_solution(6672088170700658761)
XLA Ops:
  0.7 1.1 copy-done
  1.9 0.9 copy-done.3
  2.8 0.8 shard_map.86
  3.6 6.2 %collective-permute-start.3 = (bf16[2,512,256]{2,1,0:T(8,128)(2,1)S(1)}, bf16[2,512,256]{2,1,0:T(8,128)(2,1)S(1)}, u32[]{:S(2)}, u32[]{:S(2)}) collective-permute-start(bf16[2,512,256]{2,1,0:T(8,128)(2,1)S(1)} %get-tuple-element.88), channel_id=1, source_target_pairs={{0,192},{1,195},{2,194},{3,193},{64,128},{65,131},{66,130},{67,129... | collective-permute-start | bytes 1572872 | tf_op jit(solution)/shard_map/ppermute | solution.py:421
  9.8 2.1 %collective-permute-start.1 = (bf16[2,512,256]{2,1,0:T(8,128)(2,1)S(1)}, bf16[2,512,256]{2,1,0:T(8,128)(2,1)S(1)}, u32[]{:S(2)}, u32[]{:S(2)}) collective-permute-start(bf16[2,512,256]{2,1,0:T(8,128)(2,1)S(1)} %get-tuple-element.88), channel_id=1, source_target_pairs={{0,128},{1,129},{2,130},{3,131},{64,192},{65,193},{66,194},{67,195... | collective-permute-start | bytes 1572872 | tf_op jit(solution)/shard_map/ppermute | solution.py:421
  11.9 2.0 %collective-permute-start = (bf16[4,512,256]{2,1,0:T(8,128)(2,1)S(1)}, bf16[4,512,256]{2,1,0:T(8,128)(2,1)S(1)}, u32[]{:S(2)}, u32[]{:S(2)}) collective-permute-start(bf16[4,512,256]{2,1,0:T(8,128)(2,1)S(1)} %get-tuple-element.87.rest_0_), channel_id=1, source_target_pairs={{0,64},{1,67},{2,66},{3,65},{64,0},{65,3},{66,2},{67,1},{128,192},... | collective-permute-start | bytes 3145736 | tf_op jit(solution)/shard_map/ppermute | solution.py:421
  13.9 4.5 %collective-permute-done.3.rest_4_ = bf16[2,512,256]{2,1,0:T(8,128)(2,1)S(1)} collective-permute-done((bf16[2,512,256]{2,1,0:T(8,128)(2,1)S(1)}, bf16[2,512,256]{2,1,0:T(8,128)(2,1)S(1)}, u32[]{:S(2)}, u32[]{:S(2)}) %collective-permute-start.3) | collective-permute-done | bytes 524320 | tf_op jit(solution)/shard_map/ppermute | solution.py:421
  18.4 6.3 %collective-permute-start.4 = (bf16[2,512,256]{2,1,0:T(8,128)(2,1)S(1)}, bf16[2,512,256]{2,1,0:T(8,128)(2,1)}, u32[]{:S(2)}, u32[]{:S(2)}) collective-permute-start(bf16[2,512,256]{2,1,0:T(8,128)(2,1)S(1)} %collective-permute-done.3.rest_4_), channel_id=1, source_target_pairs={{0,1},{1,0},{2,3},{3,2},{4,5},{5,4},{6,7},{7,6},{8,9},{9,8},{10,11... | collective-permute-start | bytes 1572872 | tf_op jit(solution)/shard_map/ppermute | solution.py:407
  24.7 8.7 %collective-permute-done.1.rest_2_ = bf16[2,512,256]{2,1,0:T(8,128)(2,1)S(1)} collective-permute-done((bf16[2,512,256]{2,1,0:T(8,128)(2,1)S(1)}, bf16[2,512,256]{2,1,0:T(8,128)(2,1)S(1)}, u32[]{:S(2)}, u32[]{:S(2)}) %collective-permute-start.1) | collective-permute-done | bytes 524320 | tf_op jit(solution)/shard_map/ppermute | solution.py:421
  33.4 2.4 %collective-permute-start.2 = (bf16[2,512,256]{2,1,0:T(8,128)(2,1)S(1)}, bf16[2,512,256]{2,1,0:T(8,128)(2,1)}, u32[]{:S(2)}, u32[]{:S(2)}) collective-permute-start(bf16[2,512,256]{2,1,0:T(8,128)(2,1)S(1)} %collective-permute-done.1.rest_2_), channel_id=1, source_target_pairs={{0,1},{1,0},{2,3},{3,2},{4,5},{5,4},{6,7},{7,6},{8,9},{9,8},{10,11... | collective-permute-start | bytes 1572872 | tf_op jit(solution)/shard_map/ppermute | solution.py:407
  35.8 0.8 copy.16.counts
  36.6 0.8 copy.15.tile_lists
  37.5 1.0 copy-done.1
  38.5 0.7 copy-done.4
  39.2 6.7 %shard_map.87 = (bf16[128,512]{1,0:T(8,128)(2,1)S(1)}, bf16[4,128,512]{2,1,0:T(8,128)(2,1)}, f32[4,128,128]{2,1,0:T(8,128)S(1)}, bf16[4,3,128,256]{3,2,1,0:T(8,1...) custom-call(s32[3]{0:T(128)S(1)} %pad_add_fusion.info, ...), custom_call_target="tpu_custom_call" | custom-call | tf_op jit(solution)/shard_map/pallas_call | solution.py:338
  45.8 5.4 %collective-permute-start.5 = (bf16[128,512]{1,0:T(8,128)(2,1)S(1)}, bf16[128,512]{1,0:T(8,128)(2,1)S(1)}, u32[]{:S(2)}, u32[]{:S(2)}) collective-permute-start(bf16[128,512]{1,0:T(8,128)(2,1)S(1)} %get-tuple-element.89), channel_id=1, source_target_pairs={{0,384},{128,256},{256,128},{384,0},{1,385},{129,257},{257,129},{3... | collective-permute-start | bytes 393224 | tf_op jit(solution)/shard_map/ppermute | solution.py:440
  51.2 3.5 %collective-permute-done.5.hidden_in = bf16[128,512]{1,0:T(8,128)(2,1)S(1)} collective-permute-done((bf16[128,512]{1,0:T(8,128)(2,1)S(1)}, bf16[128,512]{1,0:T(8,128)(2,1)S(1)}, u32[]{:S(2)}, u32[]{:S(2)}) %collective-permute-start.5) | collective-permute-done | bytes 131104 | tf_op jit(solution)/shard_map/ppermute | solution.py:440
  54.8 10.4 %shard_map.88 = (bf16[128,512]{1,0:T(8,128)(2,1)S(1)}, bf16[4,128,512]{2,1,0:T(8,128)(2,1)}, bf16[4,128,256]{2,1,0:T(8,128)(2,1)}, bf16[4,128,768]{2,1,0:T(8,128)(2,1)}, bf16[4,128,512]{2,1,0:T(8,128)(2,1)}) custom-call(s32[3]{0:T(128)S(1)} %pad_add_fusion.info, s32[4,2,2]{2,1,0:T(2,128)S(1)} %copy.15.tile_lists, s32[4,2]{1,0:T(4,128)S(1)} %copy.16.counts, ...), custom_call_target="tpu_custom_call" | custom-call | tf_op jit(solution)/shard_map/pallas_call | solution.py:338
  65.2 5.0 %collective-permute-start.6 = (bf16[128,512]{1,0:T(8,128)(2,1)S(1)}, bf16[128,512]{1,0:T(8,128)(2,1)}, u32[]{:S(2)}, u32[]{:S(2)}) collective-permute-start(bf16[128,512]{1,0:T(8,128)(2,1)S(1)} %get-tuple-element.94), channel_id=1, source_target_pairs={{0,384},{128,256},{256,128},{384,0},{1,385},{129,257},{257,129},{3... | collective-permute-start | bytes 393224 | tf_op jit(solution)/shard_map/ppermute | solution.py:442
  70.2 2.4 %collective-permute-done.6 = bf16[128,512]{1,0:T(8,128)(2,1)} collective-permute-done((bf16[128,512]{1,0:T(8,128)(2,1)S(1)}, bf16[128,512]{1,0:T(8,128)(2,1)}, u32[]{:S(2)}, u32[]{:S(2)}) %collective-permute-start.6) | collective-permute-done | bytes 131104 | tf_op jit(solution)/shard_map/ppermute | solution.py:442
  72.7 9.3 %conditional.2 = (bf16[4,2,512,256]{3,2,1,0:T(8,128)(2,1)S(1)}, bf16[4,2,512,256]{3,2,1,0:T(8,128)(2,1)S(1)}) conditional(s32[]{:T(128)} %convert_element_type.19, (s32[3]{0:T(128)S(1)}, bf16[4,128,512]{2,1,0:T(8,128)(2,1)}, bf16[4,128,256]{2,1,0:T(8,128)(2,1)}, bf16[4,128,768]{2,1,0:T(8,128)(2,1)}, bf16[4,128,512]{2,1,0:T(8,128)(2,1)}) %tuple.21, ...), branch_computations={%region_0.1_spmd, %region_1.2_spmd} | conditional | bytes 16
  72.7 9.3 %branch_1_fun.1 = (bf16[4,2,512,256]{3,2,1,0:T(8,128)(2,1)S(1)}, bf16[4,2,512,256]{3,2,1,0:T(8,128)(2,1)S(1)}) custom-call(s32[3]{0:T(128)S(1)} %get-tuple-element.53.info, bf16[128,512]{1,0:T(8,128)(2,1)} %get-tuple-element.54.grad_in, bf16[4,128,512]{2,1,0:T(8,128)(2,1)} %get-tuple-element.55.rest_0_, f32[4,128,128]{2,1,0:T(8,128)S(1)} %get-tuple-element.56.rest_1_, ...), custom_call_target="tpu_custom_call" | custom-call | tf_op jit(solution)/shard_map/cond/branch_1_fun/pallas_call | solution.py:338
  82.0 4.0 %collective-permute-start.7 = (bf16[4,2,512,256]{3,2,1,0:T(8,128)(2,1)S(1)}, bf16[4,2,512,256]{3,2,1,0:T(8,128)(2,1)S(1)}, u32[]{:S(2)}, u32[]{:S(2)}) collective-permute-start(bf16[4,2,512,256]{3,2,1,0:T(8,128)(2,1)S(1)} %get-tuple-element.102), channel_id=1, source_target_pairs={{0,1},{1,0},{2,3},{3,2},{4,5},{5,4},{6,7},{7,6},{8,9},{9,8},{10,11... | collective-permute-start | bytes 6291464 | tf_op jit(solution)/shard_map/ppermute | solution.py:407
  86.0 3.8 %collective-permute-done.7 = bf16[4,2,512,256]{3,2,1,0:T(8,128)(2,1)S(1)} collective-permute-done((bf16[4,2,512,256]{3,2,1,0:T(8,128)(2,1)S(1)}, bf16[4,2,512,256]{3,2,1,0:T(8,128)(2,1)S(1)}, u32[]{:S(2)}, u32[]{:S(2)}) %collective-permute-start.7) | collective-permute-done | bytes 2097184 | tf_op jit(solution)/shard_map/ppermute | solution.py:407
  90.3 29.9 %all_to_all.20 = bf16[8,512,256]{2,1,0:T(8,128)(2,1)S(1)} all-to-all(bf16[8,512,256]{2,1,0:T(8,128)(2,1)S(1)} %bitcast.20), channel_id=1, replica_groups=mesh['yh'=2,'yl'=2,'xl'=2,'zh'=4,'zl'=4,'xh'=2,'core'=2] {'yl','xl','xh'}, dimensions={0} | all-to-all | bytes 4194304 | tf_op jit(solution)/shard_map/all_to_all | solution.py:458
  120.6 28.1 %all_to_all.21 = bf16[16,32,256]{2,1,0:T(8,128)(2,1)S(1)} all-to-all(bf16[16,32,256]{2,1,0:T(8,128)(2,1)S(1)} %bitcast.23), channel_id=1, replica_groups=mesh['yh'=2,'yl'=2,'xl'=2,'zh'=4,'zl'=4,'xh'=2,'core'=2] {'zl','zh'}, dimensions={0} | all-to-all | bytes 524288 | tf_op jit(solution)/shard_map/all_to_all | solution.py:460
  148.8 21.8 %all_to_all.22 = bf16[4,32,256]{2,1,0:T(8,128)(2,1)S(1)} all-to-all(bf16[4,32,256]{2,1,0:T(8,128)(2,1)S(1)} %broadcast_in_dim.12), channel_id=1, replica_groups=mesh['yh'=2,'yl'=2,'xl'=2,'zh'=4,'zl'=4,'xh'=2,'core'=2] {'zh'}, dimensions={0} | all-to-all | bytes 131072 | tf_op jit(solution)/shard_map/all_to_all | solution.py:461
  170.6 18.4 %all_to_all.23 = bf16[8,4,32,256]{3,2,1,0:T(8,128)(2,1)S(1)} all-to-all(bf16[8,4,32,256]{3,2,1,0:T(8,128)(2,1)S(1)} %broadcast_in_dim.13), channel_id=1, replica_groups=mesh['yh'=2,'yl'=2,'xl'=2,'zh'=4,'zl'=4,'xh'=2,'core'=2] {'xh','zl'}, dimensions={0} | all-to-all | bytes 1048576 | tf_op jit(solution)/shard_map/all_to_all | solution.py:462
  189.0 6.0 %collective-permute-start.8 = (bf16[2,512,256]{2,1,0:T(8,128)(2,1)S(1)}, bf16[2,512,256]{2,1,0:T(8,128)(2,1)S(1)}, u32[]{:S(2)}, u32[]{:S(2)}) collective-permute-start(bf16[2,512,256]{2,1,0:T(8,128)(2,1)S(1)} %bitcast.21), channel_id=1, source_target_pairs={{0,1},{1,0},{2,3},{3,2},{4,5},{5,4},{6,7},{7,6},{8,9},{9,8},{10,11... | collective-permute-start | bytes 1572872 | tf_op jit(solution)/shard_map/ppermute | solution.py:407
  195.0 1.5 collective-permute-done.8
  196.7 0.7 maximum_bitcast_fusion.1
  197.4 0.9 maximum_bitcast_fusion
  (18 shorter events, 1.3 us)
Async XLA Ops:
  0.7 1.1 copy-start
  1.9 0.9 copy-start.3
  3.6 14.8 %collective-permute-start.3 = (bf16[2,512,256]{2,1,0:T(8,128)(2,1)S(1)}, bf16[2,512,256]{2,1,0:T(8,128)(2,1)S(1)}, u32[]{:S(2)}, u32[]{:S(2)}) collective-permute-start(bf16[2,512,256]{2,1,0:T(8,128)(2,1)S(1)} %get-tuple-element.88), channel_id=1, source_target_pairs={{0,192},{1,195},{2,194},{3,193},{64,128},{65,131},{66,130},{67,129... | collective-permute-start | bytes 1572872 | tf_op jit(solution)/shard_map/ppermute | solution.py:421
  9.8 23.6 %collective-permute-start.1 = (bf16[2,512,256]{2,1,0:T(8,128)(2,1)S(1)}, bf16[2,512,256]{2,1,0:T(8,128)(2,1)S(1)}, u32[]{:S(2)}, u32[]{:S(2)}) collective-permute-start(bf16[2,512,256]{2,1,0:T(8,128)(2,1)S(1)} %get-tuple-element.88), channel_id=1, source_target_pairs={{0,128},{1,129},{2,130},{3,131},{64,192},{65,193},{66,194},{67,195... | collective-permute-start | bytes 1572872 | tf_op jit(solution)/shard_map/ppermute | solution.py:421
  11.9 25.6 %collective-permute-start = (bf16[4,512,256]{2,1,0:T(8,128)(2,1)S(1)}, bf16[4,512,256]{2,1,0:T(8,128)(2,1)S(1)}, u32[]{:S(2)}, u32[]{:S(2)}) collective-permute-start(bf16[4,512,256]{2,1,0:T(8,128)(2,1)S(1)} %get-tuple-element.87.rest_0_), channel_id=1, source_target_pairs={{0,64},{1,67},{2,66},{3,65},{64,0},{65,3},{66,2},{67,1},{128,192},... | collective-permute-start | bytes 3145736 | tf_op jit(solution)/shard_map/ppermute | solution.py:421
  18.4 18.9 %collective-permute-start.4 = (bf16[2,512,256]{2,1,0:T(8,128)(2,1)S(1)}, bf16[2,512,256]{2,1,0:T(8,128)(2,1)}, u32[]{:S(2)}, u32[]{:S(2)}) collective-permute-start(bf16[2,512,256]{2,1,0:T(8,128)(2,1)S(1)} %collective-permute-done.3.rest_4_), channel_id=1, source_target_pairs={{0,1},{1,0},{2,3},{3,2},{4,5},{5,4},{6,7},{7,6},{8,9},{9,8},{10,11... | collective-permute-start | bytes 1572872 | tf_op jit(solution)/shard_map/ppermute | solution.py:407
  33.4 4.0 %collective-permute-start.2 = (bf16[2,512,256]{2,1,0:T(8,128)(2,1)S(1)}, bf16[2,512,256]{2,1,0:T(8,128)(2,1)}, u32[]{:S(2)}, u32[]{:S(2)}) collective-permute-start(bf16[2,512,256]{2,1,0:T(8,128)(2,1)S(1)} %collective-permute-done.1.rest_2_), channel_id=1, source_target_pairs={{0,1},{1,0},{2,3},{3,2},{4,5},{5,4},{6,7},{7,6},{8,9},{9,8},{10,11... | collective-permute-start | bytes 1572872 | tf_op jit(solution)/shard_map/ppermute | solution.py:407
  37.5 1.0 copy-start.1
  38.5 0.7 copy-start.4
  39.2 15.6 %copy-start.2 = (bf16[4,128,512]{2,1,0:T(8,128)(2,1)S(1)}, bf16[4,128,512]{2,1,0:T(8,128)(2,1)}, u32[]{:S(2)}) copy-start(bf16[4,128,512]{2,1,0:T(8,128)(2,1)} %grad_in.1) | copy-start | bytes 1572868
  45.8 8.9 %collective-permute-start.5 = (bf16[128,512]{1,0:T(8,128)(2,1)S(1)}, bf16[128,512]{1,0:T(8,128)(2,1)S(1)}, u32[]{:S(2)}, u32[]{:S(2)}) collective-permute-start(bf16[128,512]{1,0:T(8,128)(2,1)S(1)} %get-tuple-element.89), channel_id=1, source_target_pairs={{0,384},{128,256},{256,128},{384,0},{1,385},{129,257},{257,129},{3... | collective-permute-start | bytes 393224 | tf_op jit(solution)/shard_map/ppermute | solution.py:440
  65.2 7.5 %collective-permute-start.6 = (bf16[128,512]{1,0:T(8,128)(2,1)S(1)}, bf16[128,512]{1,0:T(8,128)(2,1)}, u32[]{:S(2)}, u32[]{:S(2)}) collective-permute-start(bf16[128,512]{1,0:T(8,128)(2,1)S(1)} %get-tuple-element.94), channel_id=1, source_target_pairs={{0,384},{128,256},{256,128},{384,0},{1,385},{129,257},{257,129},{3... | collective-permute-start | bytes 393224 | tf_op jit(solution)/shard_map/ppermute | solution.py:442
  82.0 7.8 %collective-permute-start.7 = (bf16[4,2,512,256]{3,2,1,0:T(8,128)(2,1)S(1)}, bf16[4,2,512,256]{3,2,1,0:T(8,128)(2,1)S(1)}, u32[]{:S(2)}, u32[]{:S(2)}) collective-permute-start(bf16[4,2,512,256]{3,2,1,0:T(8,128)(2,1)S(1)} %get-tuple-element.102), channel_id=1, source_target_pairs={{0,1},{1,0},{2,3},{3,2},{4,5},{5,4},{6,7},{7,6},{8,9},{9,8},{10,11... | collective-permute-start | bytes 6291464 | tf_op jit(solution)/shard_map/ppermute | solution.py:407
  189.0 7.5 %collective-permute-start.8 = (bf16[2,512,256]{2,1,0:T(8,128)(2,1)S(1)}, bf16[2,512,256]{2,1,0:T(8,128)(2,1)S(1)}, u32[]{:S(2)}, u32[]{:S(2)}) collective-permute-start(bf16[2,512,256]{2,1,0:T(8,128)(2,1)S(1)} %bitcast.21), channel_id=1, source_target_pairs={{0,1},{1,0},{2,3},{3,2},{4,5},{5,4},{6,7},{7,6},{8,9},{9,8},{10,11... | collective-permute-start | bytes 1572872 | tf_op jit(solution)/shard_map/ppermute | solution.py:407

commit v3 on v2

--- a/solution.py
+++ b/solution.py
@@ -63,8 +63,8 @@
     def times(tile, key_tile):
         seen = (virtual[batch] == key_tile).astype(F32)
         for slot in range(2):
-            named = tile_lists[batch, tile, slot] == key_tile
-            seen = seen + (named & (slot < counts[batch, tile])).astype(F32)
+            named = tile_lists[tile, slot, batch] == key_tile
+            seen = seen + (named & (slot < counts[tile, batch])).astype(F32)
         return seen
 
     row = lax.broadcasted_iota(jnp.int32, (ROWS, ROWS), 0) < ROWS // 2
@@ -427,7 +427,7 @@
     me = y * 2 + x
     batch = jnp.where(stage == 0, y, 1 - y) * 2 + x
     info = jnp.stack([batch, me, core]).astype(jnp.int32)
-    tables = (tile_lists, counts, virtual)
+    tables = (tile_lists.transpose(1, 2, 0), counts.transpose(1, 0), virtual)
     own, half = run_pack(info, w_qkv, w_out)
     near2 = fetched(half, 1, 0)
     near3 = fetched(half, 1, 1)
@@ -453,12 +453,12 @@
         return jnp.broadcast_to(value, (times, *value.shape))
 
     far, near = lax.axis_size("zh"), lax.axis_size("zl")
-    piece = D // (far * near)
+    piece = D // near
     total = (keep.astype(F32) + swapped(send, "core").astype(F32)).astype(BF16)
     total = lax.all_to_all(total.reshape(8, D, INNER), ("yl", "xl", "xh"), 0, 0, tiled=True)
-    total = added(total, 0).reshape(far * near, piece, INNER)
-    total = added(lax.all_to_all(total, ("zl", "zh"), 0, 0, tiled=True), 0)
-    total = lax.all_to_all(repeated(total, far), "zh", 0, 0, tiled=True)
+    total = added(total, 0).reshape(near, piece, INNER)
+    total = added(lax.all_to_all(total, "zl", 0, 0, tiled=True), 0)
+    total = added(lax.all_to_all(repeated(total, far), "zh", 0, 0, tiled=True), 0)
     total = lax.all_to_all(repeated(total, 2 * near), ("xh", "zl"), 0, 0, tiled=True)
     mine = total.reshape(2, D, INNER)
     other = swapped(mine, "core")

time: 199 us -> 190 us (0.955)
  blocking collectives: 98.2 us -> 87.3 us
    all_to_all x2, blocking collectives: 49.9 us -> 40.1 us  [the longest x1 28.6 us: per_device(): lax.all_to_all(repeated(total, far), 'zh', 0, 0, tiled=True)]
    ppermute x4, starting transfers between devices: 18.6 us -> 20.7 us  [swapped(): return lax.ppermute(value, axis, [(0, 1), (1, 0)])]
    unnamed x12 -> x18, local copies, waits for them, and re-layouts: 5.32 us -> 5.34 us
  transfers between devices with their start and end apart: 9 -> 9, of which waited for: 7 -> 7; matrix products, arithmetic and copies ran while one was open for 1% -> 0% of each run, Pallas kernels for 0% -> 0%
where the time goes in v3:
time: 190 us
  blocking collectives  87.3 us (46%)
  starting transfers between devices  40.2 us (21%)
  Pallas kernels  27.2 us (14%)
  waiting for transfers between devices  25.8 us (14%)
  local copies, waits for them, and re-layouts  5.47 us (3%)
  other arithmetic  2.78 us (1%)
    all_to_all x1, blocking collectives, per_device(): lax.all_to_all(total.reshape(8, D, INNER), ('yl', 'xl', 'xh'), 0, 0, tile...  29.9 us
    all_to_all x1, blocking collectives, per_device(): lax.all_to_all(repeated(total, far), 'zh', 0, 0, tiled=True)  28.6 us
    pallas_call x4, Pallas kernels, call(): pl.pallas_call(kernel, grid_spec=pltpu.PrefetchScalarGridSpec(num_scalar_...  27.2 us
    ppermute x4, starting transfers between devices, swapped(): return lax.ppermute(value, axis, [(0, 1), (1, 0)])  20.7 us
    all_to_all x1, blocking collectives, per_device(): lax.all_to_all(repeated(total, 2 * near), ('xh', 'zl'), 0, 0, tiled=True)  17.3 us
    ppermute x3, waiting for transfers between devices, fetched(): return lax.ppermute(value, axes, pairs)  13.2 us
    all_to_all x1, blocking collectives, per_device(): total = added(lax.all_to_all(total, 'zl', 0, 0, tiled=True), 0)  11.5 us
    ppermute x3, starting transfers between devices, fetched(): return lax.ppermute(value, axes, pairs)  10.3 us
  transfers between devices with their start and end apart: 9, of which 7 were waited for; matrix products, arithmetic and copies ran while one was open for 0% of the time, Pallas kernels for 0%

profile of v3, /device:TPU:1, one launch (start us, length us, event | category | flops | bytes accessed | tf_op | source)
XLA Modules:
  0.0 189.6 jit_solution(11243192857740711827)
XLA Ops:
  0.7 1.1 copy-done
  1.9 0.9 copy-done.3
  2.8 0.8 shard_map.86
  3.6 6.2 %collective-permute-start.3 = (bf16[2,512,256]{2,1,0:T(8,128)(2,1)S(1)}, bf16[2,512,256]{2,1,0:T(8,128)(2,1)S(1)}, u32[]{:S(2)}, u32[]{:S(2)}) collective-permute-start(bf16[2,512,256]{2,1,0:T(8,128)(2,1)S(1)} %get-tuple-element.88), channel_id=1, source_target_pairs={{0,192},{1,195},{2,194},{3,193},{64,128},{65,131},{66,130},{67,129... | collective-permute-start | bytes 1572872 | tf_op jit(solution)/shard_map/ppermute | solution.py:421
  9.8 2.1 %collective-permute-start.1 = (bf16[2,512,256]{2,1,0:T(8,128)(2,1)S(1)}, bf16[2,512,256]{2,1,0:T(8,128)(2,1)S(1)}, u32[]{:S(2)}, u32[]{:S(2)}) collective-permute-start(bf16[2,512,256]{2,1,0:T(8,128)(2,1)S(1)} %get-tuple-element.88), channel_id=1, source_target_pairs={{0,128},{1,129},{2,130},{3,131},{64,192},{65,193},{66,194},{67,195... | collective-permute-start | bytes 1572872 | tf_op jit(solution)/shard_map/ppermute | solution.py:421
  11.9 2.0 %collective-permute-start = (bf16[4,512,256]{2,1,0:T(8,128)(2,1)S(1)}, bf16[4,512,256]{2,1,0:T(8,128)(2,1)S(1)}, u32[]{:S(2)}, u32[]{:S(2)}) collective-permute-start(bf16[4,512,256]{2,1,0:T(8,128)(2,1)S(1)} %get-tuple-element.87.rest_0_), channel_id=1, source_target_pairs={{0,64},{1,67},{2,66},{3,65},{64,0},{65,3},{66,2},{67,1},{128,192},... | collective-permute-start | bytes 3145736 | tf_op jit(solution)/shard_map/ppermute | solution.py:421
  13.9 4.5 %collective-permute-done.3.rest_4_ = bf16[2,512,256]{2,1,0:T(8,128)(2,1)S(1)} collective-permute-done((bf16[2,512,256]{2,1,0:T(8,128)(2,1)S(1)}, bf16[2,512,256]{2,1,0:T(8,128)(2,1)S(1)}, u32[]{:S(2)}, u32[]{:S(2)}) %collective-permute-start.3) | collective-permute-done | bytes 524320 | tf_op jit(solution)/shard_map/ppermute | solution.py:421
  18.4 6.3 %collective-permute-start.4 = (bf16[2,512,256]{2,1,0:T(8,128)(2,1)S(1)}, bf16[2,512,256]{2,1,0:T(8,128)(2,1)S(1)}, u32[]{:S(2)}, u32[]{:S(2)}) collective-permute-start(bf16[2,512,256]{2,1,0:T(8,128)(2,1)S(1)} %collective-permute-done.3.rest_4_), channel_id=1, source_target_pairs={{0,1},{1,0},{2,3},{3,2},{4,5},{5,4},{6,7},{7,6},{8,9},{9,8},{10,11... | collective-permute-start | bytes 1572872 | tf_op jit(solution)/shard_map/ppermute | solution.py:407
  24.7 8.7 %collective-permute-done.1.rest_2_ = bf16[2,512,256]{2,1,0:T(8,128)(2,1)S(1)} collective-permute-done((bf16[2,512,256]{2,1,0:T(8,128)(2,1)S(1)}, bf16[2,512,256]{2,1,0:T(8,128)(2,1)S(1)}, u32[]{:S(2)}, u32[]{:S(2)}) %collective-permute-start.1) | collective-permute-done | bytes 524320 | tf_op jit(solution)/shard_map/ppermute | solution.py:421
  33.4 2.4 %collective-permute-start.2 = (bf16[2,512,256]{2,1,0:T(8,128)(2,1)S(1)}, bf16[2,512,256]{2,1,0:T(8,128)(2,1)S(1)}, u32[]{:S(2)}, u32[]{:S(2)}) collective-permute-start(bf16[2,512,256]{2,1,0:T(8,128)(2,1)S(1)} %collective-permute-done.1.rest_2_), channel_id=1, source_target_pairs={{0,1},{1,0},{2,3},{3,2},{4,5},{5,4},{6,7},{7,6},{8,9},{9,8},{10,11... | collective-permute-start | bytes 1572872 | tf_op jit(solution)/shard_map/ppermute | solution.py:407
  35.8 1.5 collective-permute-done.2.rest_3_
  37.3 1.2 copy-done.1
  38.6 0.7 copy-done.4
  39.3 0.7 copy-done.5
  40.6 6.7 %shard_map.87 = (bf16[128,512]{1,0:T(8,128)(2,1)S(1)}, bf16[4,128,512]{2,1,0:T(8,128)(2,1)}, f32[4,128,128]{2,1,0:T(8,128)S(1)}, bf16[4,3,128,256]{3,2,1,0:T(8,1...) custom-call(s32[3]{0:T(128)S(1)} %pad_add_fusion.info, ...), custom_call_target="tpu_custom_call" | custom-call | tf_op jit(solution)/shard_map/pallas_call | solution.py:338
  47.3 4.6 %collective-permute-start.5 = (bf16[128,512]{1,0:T(8,128)(2,1)S(1)}, bf16[128,512]{1,0:T(8,128)(2,1)S(1)}, u32[]{:S(2)}, u32[]{:S(2)}) collective-permute-start(bf16[128,512]{1,0:T(8,128)(2,1)S(1)} %get-tuple-element.89), channel_id=1, source_target_pairs={{0,384},{128,256},{256,128},{384,0},{1,385},{129,257},{257,129},{3... | collective-permute-start | bytes 393224 | tf_op jit(solution)/shard_map/ppermute | solution.py:440
  51.9 3.3 %collective-permute-done.5.hidden_in = bf16[128,512]{1,0:T(8,128)(2,1)S(1)} collective-permute-done((bf16[128,512]{1,0:T(8,128)(2,1)S(1)}, bf16[128,512]{1,0:T(8,128)(2,1)S(1)}, u32[]{:S(2)}, u32[]{:S(2)}) %collective-permute-start.5) | collective-permute-done | bytes 131104 | tf_op jit(solution)/shard_map/ppermute | solution.py:440
  55.2 10.5 %shard_map.88 = (bf16[128,512]{1,0:T(8,128)(2,1)S(1)}, bf16[4,128,512]{2,1,0:T(8,128)(2,1)}, bf16[4,128,256]{2,1,0:T(8,128)(2,1)}, bf16[4,128,768]{2,1,0:T(8,128)(2,1)}, bf16[4,128,512]{2,1,0:T(8,128)(2,1)}) custom-call(s32[3]{0:T(128)S(1)} %pad_add_fusion.info, s32[2,2,4]{2,1,0:T(2,128)S(1)} %bitcast.26, s32[2,4]{1,0:T(2,128)S(1)} %bitcast.28, ...), custom_call_target="tpu_custom_call" | custom-call | tf_op jit(solution)/shard_map/pallas_call | solution.py:338
  65.7 4.5 %collective-permute-start.6 = (bf16[128,512]{1,0:T(8,128)(2,1)S(1)}, bf16[128,512]{1,0:T(8,128)(2,1)}, u32[]{:S(2)}, u32[]{:S(2)}) collective-permute-start(bf16[128,512]{1,0:T(8,128)(2,1)S(1)} %get-tuple-element.94), channel_id=1, source_target_pairs={{0,384},{128,256},{256,128},{384,0},{1,385},{129,257},{257,129},{3... | collective-permute-start | bytes 393224 | tf_op jit(solution)/shard_map/ppermute | solution.py:442
  70.2 2.5 %collective-permute-done.6 = bf16[128,512]{1,0:T(8,128)(2,1)} collective-permute-done((bf16[128,512]{1,0:T(8,128)(2,1)S(1)}, bf16[128,512]{1,0:T(8,128)(2,1)}, u32[]{:S(2)}, u32[]{:S(2)}) %collective-permute-start.6) | collective-permute-done | bytes 131104 | tf_op jit(solution)/shard_map/ppermute | solution.py:442
  72.7 9.3 %conditional.2 = (bf16[4,2,512,256]{3,2,1,0:T(8,128)(2,1)S(1)}, bf16[4,2,512,256]{3,2,1,0:T(8,128)(2,1)S(1)}) conditional(s32[]{:T(128)} %convert_element_type.21, (s32[3]{0:T(128)S(1)}, bf16[4,128,512]{2,1,0:T(8,128)(2,1)}, bf16[4,128,256]{2,1,0:T(8,128)(2,1)}, bf16[4,128,768]{2,1,0:T(8,128)(2,1)}, bf16[4,128,512]{2,1,0:T(8,128)(2,1)}) %tuple.21, ...), branch_computations={%region_0.1_spmd, %region_1.2_spmd} | conditional | bytes 16
  72.7 9.3 %branch_1_fun.1 = (bf16[4,2,512,256]{3,2,1,0:T(8,128)(2,1)S(1)}, bf16[4,2,512,256]{3,2,1,0:T(8,128)(2,1)S(1)}) custom-call(s32[3]{0:T(128)S(1)} %get-tuple-element.53.info, bf16[128,512]{1,0:T(8,128)(2,1)} %get-tuple-element.54.grad_in, bf16[4,128,512]{2,1,0:T(8,128)(2,1)} %get-tuple-element.55.rest_0_, f32[4,128,128]{2,1,0:T(8,128)S(1)} %get-tuple-element.56.rest_1_, ...), custom_call_target="tpu_custom_call" | custom-call | tf_op jit(solution)/shard_map/cond/branch_1_fun/pallas_call | solution.py:338
  82.1 4.2 %collective-permute-start.7 = (bf16[4,2,512,256]{3,2,1,0:T(8,128)(2,1)S(1)}, bf16[4,2,512,256]{3,2,1,0:T(8,128)(2,1)S(1)}, u32[]{:S(2)}, u32[]{:S(2)}) collective-permute-start(bf16[4,2,512,256]{3,2,1,0:T(8,128)(2,1)S(1)} %get-tuple-element.102), channel_id=1, source_target_pairs={{0,1},{1,0},{2,3},{3,2},{4,5},{5,4},{6,7},{7,6},{8,9},{9,8},{10,11... | collective-permute-start | bytes 6291464 | tf_op jit(solution)/shard_map/ppermute | solution.py:407
  86.3 3.8 %collective-permute-done.7 = bf16[4,2,512,256]{3,2,1,0:T(8,128)(2,1)S(1)} collective-permute-done((bf16[4,2,512,256]{3,2,1,0:T(8,128)(2,1)S(1)}, bf16[4,2,512,256]{3,2,1,0:T(8,128)(2,1)S(1)}, u32[]{:S(2)}, u32[]{:S(2)}) %collective-permute-start.7) | collective-permute-done | bytes 2097184 | tf_op jit(solution)/shard_map/ppermute | solution.py:407
  90.5 29.9 %all_to_all.20 = bf16[8,512,256]{2,1,0:T(8,128)(2,1)S(1)} all-to-all(bf16[8,512,256]{2,1,0:T(8,128)(2,1)S(1)} %bitcast.29), channel_id=1, replica_groups=mesh['yh'=2,'yl'=2,'xl'=2,'zh'=4,'zl'=4,'xh'=2,'core'=2] {'yl','xl','xh'}, dimensions={0} | all-to-all | bytes 4194304 | tf_op jit(solution)/shard_map/all_to_all | solution.py:458
  120.8 11.5 %all_to_all.21 = bf16[4,128,256]{2,1,0:T(8,128)(2,1)S(1)} all-to-all(bf16[4,128,256]{2,1,0:T(8,128)(2,1)S(1)} %bitcast.32), channel_id=1, replica_groups=mesh['yh'=2,'yl'=2,'xl'=2,'zh'=4,'zl'=4,'xh'=2,'core'=2] {'zl'}, dimensions={0} | all-to-all | bytes 524288 | tf_op jit(solution)/shard_map/all_to_all | solution.py:460
  132.4 28.6 %all_to_all.22 = bf16[4,128,256]{2,1,0:T(8,128)(2,1)S(1)} all-to-all(bf16[4,128,256]{2,1,0:T(8,128)(2,1)S(1)} %broadcast_in_dim.12), channel_id=1, replica_groups=mesh['yh'=2,'yl'=2,'xl'=2,'zh'=4,'zl'=4,'xh'=2,'core'=2] {'zh'}, dimensions={0} | all-to-all | bytes 524288 | tf_op jit(solution)/shard_map/all_to_all | solution.py:461
  161.1 17.3 %all_to_all.23 = bf16[8,128,256]{2,1,0:T(8,128)(2,1)S(1)} all-to-all(bf16[8,128,256]{2,1,0:T(8,128)(2,1)S(1)} %broadcast_in_dim.13), channel_id=1, replica_groups=mesh['yh'=2,'yl'=2,'xl'=2,'zh'=4,'zl'=4,'xh'=2,'core'=2] {'xh','zl'}, dimensions={0} | all-to-all | bytes 1048576 | tf_op jit(solution)/shard_map/all_to_all | solution.py:462
  178.4 7.9 %collective-permute-start.8 = (bf16[2,512,256]{2,1,0:T(8,128)(2,1)S(1)}, bf16[2,512,256]{2,1,0:T(8,128)(2,1)S(1)}, u32[]{:S(2)}, u32[]{:S(2)}) collective-permute-start(bf16[2,512,256]{2,1,0:T(8,128)(2,1)S(1)} %bitcast.30), channel_id=1, source_target_pairs={{0,1},{1,0},{2,3},{3,2},{4,5},{5,4},{6,7},{7,6},{8,9},{9,8},{10,11... | collective-permute-start | bytes 1572872 | tf_op jit(solution)/shard_map/ppermute | solution.py:407
  186.3 1.5 collective-permute-done.8
  188.0 0.7 maximum_bitcast_fusion.1
  188.7 0.9 maximum_bitcast_fusion
  (25 shorter events, 1.9 us)
Async XLA Ops:
  0.7 1.1 copy-start
  1.9 0.9 copy-start.3
  3.6 14.8 %collective-permute-start.3 = (bf16[2,512,256]{2,1,0:T(8,128)(2,1)S(1)}, bf16[2,512,256]{2,1,0:T(8,128)(2,1)S(1)}, u32[]{:S(2)}, u32[]{:S(2)}) collective-permute-start(bf16[2,512,256]{2,1,0:T(8,128)(2,1)S(1)} %get-tuple-element.88), channel_id=1, source_target_pairs={{0,192},{1,195},{2,194},{3,193},{64,128},{65,131},{66,130},{67,129... | collective-permute-start | bytes 1572872 | tf_op jit(solution)/shard_map/ppermute | solution.py:421
  9.8 23.6 %collective-permute-start.1 = (bf16[2,512,256]{2,1,0:T(8,128)(2,1)S(1)}, bf16[2,512,256]{2,1,0:T(8,128)(2,1)S(1)}, u32[]{:S(2)}, u32[]{:S(2)}) collective-permute-start(bf16[2,512,256]{2,1,0:T(8,128)(2,1)S(1)} %get-tuple-element.88), channel_id=1, source_target_pairs={{0,128},{1,129},{2,130},{3,131},{64,192},{65,193},{66,194},{67,195... | collective-permute-start | bytes 1572872 | tf_op jit(solution)/shard_map/ppermute | solution.py:421
  11.9 25.4 %collective-permute-start = (bf16[4,512,256]{2,1,0:T(8,128)(2,1)S(1)}, bf16[4,512,256]{2,1,0:T(8,128)(2,1)S(1)}, u32[]{:S(2)}, u32[]{:S(2)}) collective-permute-start(bf16[4,512,256]{2,1,0:T(8,128)(2,1)S(1)} %get-tuple-element.87.rest_0_), channel_id=1, source_target_pairs={{0,64},{1,67},{2,66},{3,65},{64,0},{65,3},{66,2},{67,1},{128,192},... | collective-permute-start | bytes 3145736 | tf_op jit(solution)/shard_map/ppermute | solution.py:421
  18.4 17.4 %collective-permute-start.4 = (bf16[2,512,256]{2,1,0:T(8,128)(2,1)S(1)}, bf16[2,512,256]{2,1,0:T(8,128)(2,1)S(1)}, u32[]{:S(2)}, u32[]{:S(2)}) collective-permute-start(bf16[2,512,256]{2,1,0:T(8,128)(2,1)S(1)} %collective-permute-done.3.rest_4_), channel_id=1, source_target_pairs={{0,1},{1,0},{2,3},{3,2},{4,5},{5,4},{6,7},{7,6},{8,9},{9,8},{10,11... | collective-permute-start | bytes 1572872 | tf_op jit(solution)/shard_map/ppermute | solution.py:407
  33.4 3.9 %collective-permute-start.2 = (bf16[2,512,256]{2,1,0:T(8,128)(2,1)S(1)}, bf16[2,512,256]{2,1,0:T(8,128)(2,1)S(1)}, u32[]{:S(2)}, u32[]{:S(2)}) collective-permute-start(bf16[2,512,256]{2,1,0:T(8,128)(2,1)S(1)} %collective-permute-done.1.rest_2_), channel_id=1, source_target_pairs={{0,1},{1,0},{2,3},{3,2},{4,5},{5,4},{6,7},{7,6},{8,9},{9,8},{10,11... | collective-permute-start | bytes 1572872 | tf_op jit(solution)/shard_map/ppermute | solution.py:407
  35.8 19.4 %copy-start.7 = (bf16[2,512,256]{2,1,0:T(8,128)(2,1)}, bf16[2,512,256]{2,1,0:T(8,128)(2,1)S(1)}, u32[]{:S(2)}) copy-start(bf16[2,512,256]{2,1,0:T(8,128)(2,1)S(1)} %collective-permute-done.4.rest_5_) | copy-start | bytes 1572868
  37.3 17.9 %copy-start.8 = (bf16[2,512,256]{2,1,0:T(8,128)(2,1)}, bf16[2,512,256]{2,1,0:T(8,128)(2,1)S(1)}, u32[]{:S(2)}) copy-start(bf16[2,512,256]{2,1,0:T(8,128)(2,1)S(1)} %collective-permute-done.2.rest_3_) | copy-start | bytes 1572868
  37.3 1.2 copy-start.1
  38.6 0.7 copy-start.4
  39.3 0.7 copy-start.5
  39.9 0.7 copy-start.6
  40.6 14.6 %copy-start.2 = (bf16[4,128,512]{2,1,0:T(8,128)(2,1)S(1)}, bf16[4,128,512]{2,1,0:T(8,128)(2,1)}, u32[]{:S(2)}) copy-start(bf16[4,128,512]{2,1,0:T(8,128)(2,1)} %grad_in.1) | copy-start | bytes 1572868
  47.3 8.0 %collective-permute-start.5 = (bf16[128,512]{1,0:T(8,128)(2,1)S(1)}, bf16[128,512]{1,0:T(8,128)(2,1)S(1)}, u32[]{:S(2)}, u32[]{:S(2)}) collective-permute-start(bf16[128,512]{1,0:T(8,128)(2,1)S(1)} %get-tuple-element.89), channel_id=1, source_target_pairs={{0,384},{128,256},{256,128},{384,0},{1,385},{129,257},{257,129},{3... | collective-permute-start | bytes 393224 | tf_op jit(solution)/shard_map/ppermute | solution.py:440
  65.7 7.0 %collective-permute-start.6 = (bf16[128,512]{1,0:T(8,128)(2,1)S(1)}, bf16[128,512]{1,0:T(8,128)(2,1)}, u32[]{:S(2)}, u32[]{:S(2)}) collective-permute-start(bf16[128,512]{1,0:T(8,128)(2,1)S(1)} %get-tuple-element.94), channel_id=1, source_target_pairs={{0,384},{128,256},{256,128},{384,0},{1,385},{129,257},{257,129},{3... | collective-permute-start | bytes 393224 | tf_op jit(solution)/shard_map/ppermute | solution.py:442
  82.1 8.0 %collective-permute-start.7 = (bf16[4,2,512,256]{3,2,1,0:T(8,128)(2,1)S(1)}, bf16[4,2,512,256]{3,2,1,0:T(8,128)(2,1)S(1)}, u32[]{:S(2)}, u32[]{:S(2)}) collective-permute-start(bf16[4,2,512,256]{3,2,1,0:T(8,128)(2,1)S(1)} %get-tuple-element.102), channel_id=1, source_target_pairs={{0,1},{1,0},{2,3},{3,2},{4,5},{5,4},{6,7},{7,6},{8,9},{9,8},{10,11... | collective-permute-start | bytes 6291464 | tf_op jit(solution)/shard_map/ppermute | solution.py:407
  178.4 9.4 %collective-permute-start.8 = (bf16[2,512,256]{2,1,0:T(8,128)(2,1)S(1)}, bf16[2,512,256]{2,1,0:T(8,128)(2,1)S(1)}, u32[]{:S(2)}, u32[]{:S(2)}) collective-permute-start(bf16[2,512,256]{2,1,0:T(8,128)(2,1)S(1)} %bitcast.30), channel_id=1, source_target_pairs={{0,1},{1,0},{2,3},{3,2},{4,5},{5,4},{6,7},{7,6},{8,9},{9,8},{10,11... | collective-permute-start | bytes 1572872 | tf_op jit(solution)/shard_map/ppermute | solution.py:407

commit v4 on v3

--- a/solution.py
+++ b/solution.py
@@ -228,6 +228,26 @@
         copy.wait()
 
 
+def unpack_kernel(info, mine, other, qkv, out, sems):
+    for side in range(2):
+
+        @pl.when(info[2] == side)
+        def _(side=side):
+            low, high = (mine, other) if side == 0 else (other, mine)
+            pairs = [
+                (low.at[0], qkv.at[0, :, pl.ds(0, INNER)]),
+                (low.at[1], qkv.at[0, :, pl.ds(INNER, INNER)]),
+                (high.at[0], qkv.at[0, :, pl.ds(2 * INNER, INNER)]),
+                (high.at[1, pl.ds(0, INNER)], out.at[0, :, pl.ds(0, INNER)]),
+                (high.at[1, pl.ds(INNER, INNER)], out.at[0, :, pl.ds(INNER, INNER)]),
+            ]
+            copies = [pltpu.make_async_copy(src, dst, sems.at[i]) for i, (src, dst) in enumerate(pairs)]
+            for copy in copies:
+                copy.start()
+            for copy in copies:
+                copy.wait()
+
+
 def forward_kernel(info, tile_lists, counts, virtual, hidden_in, *rest):
     weights = Weights(*rest[:6], *rest[-4:-2], info[1], info[2], range(STAGE_LAYERS))
     hidden_out, outside, inside = rest[6], rest[7 : 7 + len(STASH)], rest[7 + len(STASH) : 7 + 2 * len(STASH)]
@@ -314,6 +334,7 @@
 
 
 ANYWHERE = pl.BlockSpec(memory_space=pl.ANY)
+IN_HBM = pl.BlockSpec(memory_space=pltpu.HBM)
 HIDDEN = jax.ShapeDtypeStruct((ROWS, D), BF16)
 HIDDEN_BLOCK = pl.BlockSpec((ROWS, D), lambda *_: (0, 0))
 BATCH_BLOCK = pl.BlockSpec((1, ROWS, D), lambda step, info, *_: (info[0], 0, 0))
@@ -334,7 +355,7 @@
     return pltpu.SemaphoreType.DMA((count, STAGE_LAYERS))
 
 
-def call(kernel, prefetched, in_specs, out_specs, out_shape, scratch, args):
+def call(kernel, prefetched, in_specs, out_specs, out_shape, scratch, args, megabytes=20):
     return pl.pallas_call(
         kernel,
         grid_spec=pltpu.PrefetchScalarGridSpec(
@@ -345,14 +366,20 @@
             scratch_shapes=scratch,
         ),
         out_shape=out_shape,
-        compiler_params=pltpu.CompilerParams(vmem_limit_bytes=48 * 2**20),
+        compiler_params=pltpu.CompilerParams(vmem_limit_bytes=megabytes * 2**20),
     )(*args)
 
 
 def run_pack(info, w_qkv, w_out):
     shapes = [jax.ShapeDtypeStruct((blocks, D, INNER), BF16) for blocks in (4, 2)]
     sems = [pltpu.SemaphoreType.DMA((2, 5))]
-    return call(pack_kernel, 1, [ANYWHERE] * 2, [ANYWHERE] * 2, shapes, sems, (info, w_qkv, w_out))
+    return call(pack_kernel, 1, [IN_HBM] * 2, [ANYWHERE] * 2, shapes, sems, (info, w_qkv, w_out), 60)
+
+
+def run_unpack(info, mine, other):
+    shapes = [jax.ShapeDtypeStruct((1, *shape), BF16) for shape in ((D, 3 * INNER), (INNER, D))]
+    sems = [pltpu.SemaphoreType.DMA((5,))]
+    return call(unpack_kernel, 1, [ANYWHERE] * 2, [IN_HBM] * 2, shapes, sems, (info, mine, other), 1)
 
 
 def run_forward(info, tables, nodes, weights):
@@ -364,6 +391,7 @@
         [HIDDEN] + layered(STASH, jax.ShapeDtypeStruct),
         layered(STASH, pltpu.VMEM) + WEIGHT_SCRATCH + [semaphores(len(STASH)), TIMES],
         (info, *tables, nodes, *weights),
+        59,
     )
 
 
@@ -376,6 +404,7 @@
         [HIDDEN] + layered(TERMS, jax.ShapeDtypeStruct),
         layered(STASH, pltpu.VMEM) + layered(TERMS, pltpu.VMEM)[2:] + WEIGHT_SCRATCH + [semaphores(len(TERMS)), TIMES],
         (info, *tables, hidden, cotangent, *weights),
+        50,
     )
 
 
@@ -400,6 +429,7 @@
         [GRAD_HALF] * 2,
         layered(STASH, pltpu.VMEM) + WEIGHT_SCRATCH + [GRAD_PLACE, semaphores(len(STASH)), semaphores(2)],
         (info, grad, *stash, *weights),
+        20,
     )
 
 
@@ -461,11 +491,8 @@
     total = added(lax.all_to_all(repeated(total, far), "zh", 0, 0, tiled=True), 0)
     total = lax.all_to_all(repeated(total, 2 * near), ("xh", "zl"), 0, 0, tiled=True)
     mine = total.reshape(2, D, INNER)
-    other = swapped(mine, "core")
-    first, second = jnp.where(core == 0, mine, other), jnp.where(core == 0, other, mine)
-    grad_qkv = jnp.concatenate([first[0], first[1], second[0]], axis=1)
-    grad_out = jnp.concatenate([second[1, :INNER], second[1, INNER:]], axis=1)
-    return (grad_qkv[None], grad_out[None])
+    grad_qkv, grad_out = run_unpack(info, mine, swapped(mine, "core"))
+    return (grad_qkv, grad_out)
 
 
 def solution(mesh):

time: 190 us -> 206 us (1.084)
  Pallas kernels: 27.2 us -> 48 us
  local copies, waits for them, and re-layouts: 5.47 us -> 0.08 us
    pallas_call x4 -> x5, Pallas kernels: 27.2 us -> 48 us  [call(): pl.pallas_call(kernel, grid_spec=pltpu.PrefetchScalarGridSpec(num_scalar_...]
    unnamed x18 -> x12, local copies, waits for them, and re-layouts: 5.34 us -> 0.03 us
where the time goes in v4:
time: 206 us; the launch traced here: 205 us
  blocking collectives  86.8 us (42%)
  Pallas kernels  48 us (23%)
  starting transfers between devices  40.6 us (20%)
  waiting for transfers between devices  26.2 us (13%)
  other arithmetic  2.64 us (1%)
    pallas_call x5, Pallas kernels, call(): pl.pallas_call(kernel, grid_spec=pltpu.PrefetchScalarGridSpec(num_scalar_...  48 us
    all_to_all x1, blocking collectives, per_device(): lax.all_to_all(total.reshape(8, D, INNER), ('yl', 'xl', 'xh'), 0, 0, tile...  29.4 us
    all_to_all x1, blocking collectives, per_device(): lax.all_to_all(repeated(total, far), 'zh', 0, 0, tiled=True)  28.6 us
    ppermute x4, starting transfers between devices, swapped(): return lax.ppermute(value, axis, [(0, 1), (1, 0)])  20.4 us
    all_to_all x1, blocking collectives, per_device(): lax.all_to_all(repeated(total, 2 * near), ('xh', 'zl'), 0, 0, tiled=True)  17.3 us
    ppermute x3, waiting for transfers between devices, fetched(): return lax.ppermute(value, axes, pairs)  13.5 us
    all_to_all x1, blocking collectives, per_device(): total = added(lax.all_to_all(total, 'zl', 0, 0, tiled=True), 0)  11.5 us
    ppermute x3, starting transfers between devices, fetched(): return lax.ppermute(value, axes, pairs)  10.3 us
  transfers between devices with their start and end apart: 9, of which 7 were waited for; matrix products, arithmetic and copies ran while one was open for 0% of the time, Pallas kernels for 0%

profile of v4, /device:TPU:1, one launch (start us, length us, event | category | flops | bytes accessed | tf_op | source)
XLA Modules:
  0.0 205.4 jit_solution(12096113580805249087)
XLA Ops:
  0.6 0.1 pad_add_fusion.info
  0.7 17.6 %shard_map.86 = (bf16[4,512,256]{2,1,0:T(8,128)(2,1)S(1)}, bf16[2,512,256]{2,1,0:T(8,128)(2,1)}) custom-call(s32[3]{0:T(128)S(1)} %pad_add_fusion.info, bf16[1,512,768]{2,1,0:T(8,128)(2,1)} %qkv.1, bf16[1,256,512]{2,1,0:T(8,128)(2,1)} %out.1), custom_call_target="tpu_custom_call" | custom-call | tf_op jit(solution)/shard_map/pallas_call | solution.py:359
  18.4 6.2 %collective-permute-start.3 = (bf16[2,512,256]{2,1,0:T(8,128)(2,1)}, bf16[2,512,256]{2,1,0:T(8,128)(2,1)S(1)}, u32[]{:S(2)}, u32[]{:S(2)}) collective-permute-start(bf16[2,512,256]{2,1,0:T(8,128)(2,1)} %get-tuple-element.88), channel_id=1, source_target_pairs={{0,192},{1,195},{2,194},{3,193},{64,128},{65,131},{66,130},{67,129... | collective-permute-start | bytes 1572872 | tf_op jit(solution)/shard_map/ppermute | solution.py:451
  24.6 2.1 %collective-permute-start.1 = (bf16[2,512,256]{2,1,0:T(8,128)(2,1)}, bf16[2,512,256]{2,1,0:T(8,128)(2,1)S(1)}, u32[]{:S(2)}, u32[]{:S(2)}) collective-permute-start(bf16[2,512,256]{2,1,0:T(8,128)(2,1)} %get-tuple-element.88), channel_id=1, source_target_pairs={{0,128},{1,129},{2,130},{3,131},{64,192},{65,193},{66,194},{67,195... | collective-permute-start | bytes 1572872 | tf_op jit(solution)/shard_map/ppermute | solution.py:451
  26.7 2.0 collective-permute-start
  28.7 4.8 %collective-permute-done.3.rest_4_ = bf16[2,512,256]{2,1,0:T(8,128)(2,1)S(1)} collective-permute-done((bf16[2,512,256]{2,1,0:T(8,128)(2,1)}, bf16[2,512,256]{2,1,0:T(8,128)(2,1)S(1)}, u32[]{:S(2)}, u32[]{:S(2)}) %collective-permute-start.3) | collective-permute-done | bytes 524320 | tf_op jit(solution)/shard_map/ppermute | solution.py:451
  33.5 6.2 %collective-permute-start.4 = (bf16[2,512,256]{2,1,0:T(8,128)(2,1)S(1)}, bf16[2,512,256]{2,1,0:T(8,128)(2,1)S(1)}, u32[]{:S(2)}, u32[]{:S(2)}) collective-permute-start(bf16[2,512,256]{2,1,0:T(8,128)(2,1)S(1)} %collective-permute-done.3.rest_4_), channel_id=1, source_target_pairs={{0,1},{1,0},{2,3},{3,2},{4,5},{5,4},{6,7},{7,6},{8,9},{9,8},{10,11... | collective-permute-start | bytes 1572872 | tf_op jit(solution)/shard_map/ppermute | solution.py:437
  39.7 8.7 %collective-permute-done.1.rest_2_ = bf16[2,512,256]{2,1,0:T(8,128)(2,1)S(1)} collective-permute-done((bf16[2,512,256]{2,1,0:T(8,128)(2,1)}, bf16[2,512,256]{2,1,0:T(8,128)(2,1)S(1)}, u32[]{:S(2)}, u32[]{:S(2)}) %collective-permute-start.1) | collective-permute-done | bytes 524320 | tf_op jit(solution)/shard_map/ppermute | solution.py:451
  48.4 2.4 %collective-permute-start.2 = (bf16[2,512,256]{2,1,0:T(8,128)(2,1)S(1)}, bf16[2,512,256]{2,1,0:T(8,128)(2,1)S(1)}, u32[]{:S(2)}, u32[]{:S(2)}) collective-permute-start(bf16[2,512,256]{2,1,0:T(8,128)(2,1)S(1)} %collective-permute-done.1.rest_2_), channel_id=1, source_target_pairs={{0,1},{1,0},{2,3},{3,2},{4,5},{5,4},{6,7},{7,6},{8,9},{9,8},{10,11... | collective-permute-start | bytes 1572872 | tf_op jit(solution)/shard_map/ppermute | solution.py:437
  50.8 1.5 collective-permute-done.2.rest_3_
  52.3 0.0 collective-permute-done.rest_1_
  52.3 0.0 copy-start.2
  52.4 0.0 copy-start.3
  52.4 8.5 %shard_map.87 = (bf16[128,512]{1,0:T(8,128)(2,1)}, bf16[4,128,512]{2,1,0:T(8,128)(2,1)}, f32[4,128,128]{2,1,0:T(8,128)S(1)}, bf16[4,3,128,256]{3,2,1,0:T(8,128)(...) custom-call(s32[3]{0:T(128)S(1)} %pad_add_fusion.info, ...), custom_call_target="tpu_custom_call" | custom-call | tf_op jit(solution)/shard_map/pallas_call | solution.py:359
  60.9 4.6 %collective-permute-start.5 = (bf16[128,512]{1,0:T(8,128)(2,1)}, bf16[128,512]{1,0:T(8,128)(2,1)S(1)}, u32[]{:S(2)}, u32[]{:S(2)}) collective-permute-start(bf16[128,512]{1,0:T(8,128)(2,1)} %get-tuple-element.89), channel_id=1, source_target_pairs={{0,384},{128,256},{256,128},{384,0},{1,385},{129,257},{257,129},{3... | collective-permute-start | bytes 393224 | tf_op jit(solution)/shard_map/ppermute | solution.py:470
  65.5 3.5 %collective-permute-done.5.hidden_in = bf16[128,512]{1,0:T(8,128)(2,1)S(1)} collective-permute-done((bf16[128,512]{1,0:T(8,128)(2,1)}, bf16[128,512]{1,0:T(8,128)(2,1)S(1)}, u32[]{:S(2)}, u32[]{:S(2)}) %collective-permute-start.5) | collective-permute-done | bytes 131104 | tf_op jit(solution)/shard_map/ppermute | solution.py:470
  69.0 10.4 %shard_map.88 = (bf16[128,512]{1,0:T(8,128)(2,1)S(1)}, bf16[4,128,512]{2,1,0:T(8,128)(2,1)}, bf16[4,128,256]{2,1,0:T(8,128)(2,1)}, bf16[4,128,768]{2,1,0:T(8,128)(2,1)}, bf16[4,128,512]{2,1,0:T(8,128)(2,1)}) custom-call(s32[3]{0:T(128)S(1)} %pad_add_fusion.info, s32[2,2,4]{2,1,0:T(2,128)S(1)} %bitcast.11, s32[2,4]{1,0:T(2,128)S(1)} %bitcast.13, ...), custom_call_target="tpu_custom_call" | custom-call | tf_op jit(solution)/shard_map/pallas_call | solution.py:359
  79.5 5.2 %collective-permute-start.6 = (bf16[128,512]{1,0:T(8,128)(2,1)S(1)}, bf16[128,512]{1,0:T(8,128)(2,1)}, u32[]{:S(2)}, u32[]{:S(2)}) collective-permute-start(bf16[128,512]{1,0:T(8,128)(2,1)S(1)} %get-tuple-element.94), channel_id=1, source_target_pairs={{0,384},{128,256},{256,128},{384,0},{1,385},{129,257},{257,129},{3... | collective-permute-start | bytes 393224 | tf_op jit(solution)/shard_map/ppermute | solution.py:472
  84.7 2.4 %collective-permute-done.6 = bf16[128,512]{1,0:T(8,128)(2,1)} collective-permute-done((bf16[128,512]{1,0:T(8,128)(2,1)S(1)}, bf16[128,512]{1,0:T(8,128)(2,1)}, u32[]{:S(2)}, u32[]{:S(2)}) %collective-permute-start.6) | collective-permute-done | bytes 131104 | tf_op jit(solution)/shard_map/ppermute | solution.py:472
  87.2 9.9 %conditional.2 = (bf16[4,2,512,256]{3,2,1,0:T(8,128)(2,1)S(1)}, bf16[4,2,512,256]{3,2,1,0:T(8,128)(2,1)}) conditional(s32[]{:T(128)} %convert_element_type.21, (s32[3]{0:T(128)S(1)}, bf16[4,128,512]{2,1,0:T(8,128)(2,1)}, bf16[4,128,256]{2,1,0:T(8,128)(2,1)}, bf16[4,128,768]{2,1,0:T(8,128)(2,1)}, bf16[4,128,512]{2,1,0:T(8,128)(2,1)}) %tuple.20, ...), branch_computations={%region_0.1_spmd, %region_1.2_spmd} | conditional | bytes 16
  87.2 9.9 %branch_1_fun.1 = (bf16[4,2,512,256]{3,2,1,0:T(8,128)(2,1)}, bf16[4,2,512,256]{3,2,1,0:T(8,128)(2,1)S(1)}) custom-call(s32[3]{0:T(128)S(1)} %get-tuple-element.53.info, bf16[128,512]{1,0:T(8,128)(2,1)} %get-tuple-element.54.grad_in, bf16[4,128,512]{2,1,0:T(8,128)(2,1)} %get-tuple-element.55.rest_0_, f32[4,128,128]{2,1,0:T(8,128)S(1)} %get-tuple-element.56.rest_1_, ...), custom_call_target="tpu_custom_call" | custom-call | tf_op jit(solution)/shard_map/cond/branch_1_fun/pallas_call | solution.py:359
  97.1 4.0 %collective-permute-start.7 = (bf16[4,2,512,256]{3,2,1,0:T(8,128)(2,1)S(1)}, bf16[4,2,512,256]{3,2,1,0:T(8,128)(2,1)S(1)}, u32[]{:S(2)}, u32[]{:S(2)}) collective-permute-start(bf16[4,2,512,256]{3,2,1,0:T(8,128)(2,1)S(1)} %get-tuple-element.102), channel_id=1, source_target_pairs={{0,1},{1,0},{2,3},{3,2},{4,5},{5,4},{6,7},{7,6},{8,9},{9,8},{10,11... | collective-permute-start | bytes 6291464 | tf_op jit(solution)/shard_map/ppermute | solution.py:437
  101.1 3.8 %collective-permute-done.7 = bf16[4,2,512,256]{3,2,1,0:T(8,128)(2,1)S(1)} collective-permute-done((bf16[4,2,512,256]{3,2,1,0:T(8,128)(2,1)S(1)}, bf16[4,2,512,256]{3,2,1,0:T(8,128)(2,1)S(1)}, u32[]{:S(2)}, u32[]{:S(2)}) %collective-permute-start.7) | collective-permute-done | bytes 2097184 | tf_op jit(solution)/shard_map/ppermute | solution.py:437
  104.9 2.1 %add_convert_fusion = bf16[4,2,512,256]{3,2,1,0:T(8,128)(2,1)S(1)} fusion(bf16[4,2,512,256]{3,2,1,0:T(8,128)(2,1)S(1)} %collective-permute-done.7, bf16[4,2,512,256]{3,2,1,0:T(8,128)(2,1)} %get-tuple-element.101), kind=kLoop, calls=%fused_computation | loop fusion | flops 4194304 | bytes 6291456 | tf_op jit(solution)/shard_map/convert_element_type | solution.py:487
  107.0 29.4 %all_to_all.20 = bf16[8,512,256]{2,1,0:T(8,128)(2,1)S(1)} all-to-all(bf16[8,512,256]{2,1,0:T(8,128)(2,1)S(1)} %bitcast.14), channel_id=1, replica_groups=mesh['yh'=2,'yl'=2,'xl'=2,'zh'=4,'zl'=4,'xh'=2,'core'=2] {'yl','xl','xh'}, dimensions={0} | all-to-all | bytes 4194304 | tf_op jit(solution)/shard_map/all_to_all | solution.py:488
  136.4 0.4 reduce_sum.36
  136.8 11.5 %all_to_all.21 = bf16[4,128,256]{2,1,0:T(8,128)(2,1)S(1)} all-to-all(bf16[4,128,256]{2,1,0:T(8,128)(2,1)S(1)} %bitcast.15), channel_id=1, replica_groups=mesh['yh'=2,'yl'=2,'xl'=2,'zh'=4,'zl'=4,'xh'=2,'core'=2] {'zl'}, dimensions={0} | all-to-all | bytes 524288 | tf_op jit(solution)/shard_map/all_to_all | solution.py:490
  148.3 28.6 %all_to_all.22 = bf16[4,128,256]{2,1,0:T(8,128)(2,1)S(1)} all-to-all(bf16[4,128,256]{2,1,0:T(8,128)(2,1)S(1)} %broadcast_in_dim.6), channel_id=1, replica_groups=mesh['yh'=2,'yl'=2,'xl'=2,'zh'=4,'zl'=4,'xh'=2,'core'=2] {'zh'}, dimensions={0} | all-to-all | bytes 524288 | tf_op jit(solution)/shard_map/all_to_all | solution.py:491
  177.0 17.3 %all_to_all.23 = bf16[8,128,256]{2,1,0:T(8,128)(2,1)S(1)} all-to-all(bf16[8,128,256]{2,1,0:T(8,128)(2,1)S(1)} %broadcast_in_dim.7), channel_id=1, replica_groups=mesh['yh'=2,'yl'=2,'xl'=2,'zh'=4,'zl'=4,'xh'=2,'core'=2] {'xh','zl'}, dimensions={0} | all-to-all | bytes 1048576 | tf_op jit(solution)/shard_map/all_to_all | solution.py:492
  194.3 7.9 %collective-permute-start.8 = (bf16[2,512,256]{2,1,0:T(8,128)(2,1)S(1)}, bf16[2,512,256]{2,1,0:T(8,128)(2,1)S(1)}, u32[]{:S(2)}, u32[]{:S(2)}) collective-permute-start(bf16[2,512,256]{2,1,0:T(8,128)(2,1)S(1)} %bitcast.8), channel_id=1, source_target_pairs={{0,1},{1,0},{2,3},{3,2},{4,5},{5,4},{6,7},{7,6},{8,9},{9,8},{10,11... | collective-permute-start | bytes 1572872 | tf_op jit(solution)/shard_map/ppermute | solution.py:437
  202.2 1.5 collective-permute-done.8.other
  203.7 1.6 shard_map.89
  (15 shorter events, 0.2 us)
Async XLA Ops:
  18.4 15.2 %collective-permute-start.3 = (bf16[2,512,256]{2,1,0:T(8,128)(2,1)}, bf16[2,512,256]{2,1,0:T(8,128)(2,1)S(1)}, u32[]{:S(2)}, u32[]{:S(2)}) collective-permute-start(bf16[2,512,256]{2,1,0:T(8,128)(2,1)} %get-tuple-element.88), channel_id=1, source_target_pairs={{0,192},{1,195},{2,194},{3,193},{64,128},{65,131},{66,130},{67,129... | collective-permute-start | bytes 1572872 | tf_op jit(solution)/shard_map/ppermute | solution.py:451
  24.6 23.8 %collective-permute-start.1 = (bf16[2,512,256]{2,1,0:T(8,128)(2,1)}, bf16[2,512,256]{2,1,0:T(8,128)(2,1)S(1)}, u32[]{:S(2)}, u32[]{:S(2)}) collective-permute-start(bf16[2,512,256]{2,1,0:T(8,128)(2,1)} %get-tuple-element.88), channel_id=1, source_target_pairs={{0,128},{1,129},{2,130},{3,131},{64,192},{65,193},{66,194},{67,195... | collective-permute-start | bytes 1572872 | tf_op jit(solution)/shard_map/ppermute | solution.py:451
  26.7 25.6 %collective-permute-start = (bf16[4,512,256]{2,1,0:T(8,128)(2,1)S(1)}, bf16[4,512,256]{2,1,0:T(8,128)(2,1)S(1)}, u32[]{:S(2)}, u32[]{:S(2)}) collective-permute-start(bf16[4,512,256]{2,1,0:T(8,128)(2,1)S(1)} %get-tuple-element.87.rest_0_), channel_id=1, source_target_pairs={{0,64},{1,67},{2,66},{3,65},{64,0},{65,3},{66,2},{67,1},{128,192},... | collective-permute-start | bytes 3145736 | tf_op jit(solution)/shard_map/ppermute | solution.py:451
  33.5 17.3 %collective-permute-start.4 = (bf16[2,512,256]{2,1,0:T(8,128)(2,1)S(1)}, bf16[2,512,256]{2,1,0:T(8,128)(2,1)S(1)}, u32[]{:S(2)}, u32[]{:S(2)}) collective-permute-start(bf16[2,512,256]{2,1,0:T(8,128)(2,1)S(1)} %collective-permute-done.3.rest_4_), channel_id=1, source_target_pairs={{0,1},{1,0},{2,3},{3,2},{4,5},{5,4},{6,7},{7,6},{8,9},{9,8},{10,11... | collective-permute-start | bytes 1572872 | tf_op jit(solution)/shard_map/ppermute | solution.py:437
  48.4 3.9 %collective-permute-start.2 = (bf16[2,512,256]{2,1,0:T(8,128)(2,1)S(1)}, bf16[2,512,256]{2,1,0:T(8,128)(2,1)S(1)}, u32[]{:S(2)}, u32[]{:S(2)}) collective-permute-start(bf16[2,512,256]{2,1,0:T(8,128)(2,1)S(1)} %collective-permute-done.1.rest_2_), channel_id=1, source_target_pairs={{0,1},{1,0},{2,3},{3,2},{4,5},{5,4},{6,7},{7,6},{8,9},{9,8},{10,11... | collective-permute-start | bytes 1572872 | tf_op jit(solution)/shard_map/ppermute | solution.py:437
  50.8 18.2 %copy-start.4 = (bf16[2,512,256]{2,1,0:T(8,128)(2,1)}, bf16[2,512,256]{2,1,0:T(8,128)(2,1)S(1)}, u32[]{:S(2)}) copy-start(bf16[2,512,256]{2,1,0:T(8,128)(2,1)S(1)} %collective-permute-done.4.rest_5_) | copy-start | bytes 1572868
  52.3 8.6 %copy-start.5 = (bf16[2,512,256]{2,1,0:T(8,128)(2,1)}, bf16[2,512,256]{2,1,0:T(8,128)(2,1)S(1)}, u32[]{:S(2)}) copy-start(bf16[2,512,256]{2,1,0:T(8,128)(2,1)S(1)} %collective-permute-done.2.rest_3_) | copy-start | bytes 1572868
  52.3 16.7 %copy-start = (bf16[4,128,512]{2,1,0:T(8,128)(2,1)S(1)}, bf16[4,128,512]{2,1,0:T(8,128)(2,1)}, u32[]{:S(2)}) copy-start(bf16[4,128,512]{2,1,0:T(8,128)(2,1)} %grad_in.1) | copy-start | bytes 1572868
  52.3 16.7 %copy-start.1 = (s32[4,2,2]{0,2,1:T(2,128)S(1)}, s32[4,2,2]{0,2,1:T(2,128)}, u32[]{:S(2)}) copy-start(s32[4,2,2]{0,2,1:T(2,128)} %param.13) | copy-start | bytes 196
  52.3 16.7 %copy-start.2 = (s32[4,2]{0,1:T(2,128)S(1)}, s32[4,2]{0,1:T(2,128)}, u32[]{:S(2)}) copy-start(s32[4,2]{0,1:T(2,128)} %param.14) | copy-start | bytes 100
  52.4 16.7 %copy-start.3 = (s32[4]{0:T(128)S(1)}, s32[4]{0:T(128)}, u32[]{:S(2)}) copy-start(s32[4]{0:T(128)} %virtual.3) | copy-start | bytes 52
  60.9 8.1 %collective-permute-start.5 = (bf16[128,512]{1,0:T(8,128)(2,1)}, bf16[128,512]{1,0:T(8,128)(2,1)S(1)}, u32[]{:S(2)}, u32[]{:S(2)}) collective-permute-start(bf16[128,512]{1,0:T(8,128)(2,1)} %get-tuple-element.89), channel_id=1, source_target_pairs={{0,384},{128,256},{256,128},{384,0},{1,385},{129,257},{257,129},{3... | collective-permute-start | bytes 393224 | tf_op jit(solution)/shard_map/ppermute | solution.py:470
  79.5 7.7 %collective-permute-start.6 = (bf16[128,512]{1,0:T(8,128)(2,1)S(1)}, bf16[128,512]{1,0:T(8,128)(2,1)}, u32[]{:S(2)}, u32[]{:S(2)}) collective-permute-start(bf16[128,512]{1,0:T(8,128)(2,1)S(1)} %get-tuple-element.94), channel_id=1, source_target_pairs={{0,384},{128,256},{256,128},{384,0},{1,385},{129,257},{257,129},{3... | collective-permute-start | bytes 393224 | tf_op jit(solution)/shard_map/ppermute | solution.py:472
  97.1 7.8 %collective-permute-start.7 = (bf16[4,2,512,256]{3,2,1,0:T(8,128)(2,1)S(1)}, bf16[4,2,512,256]{3,2,1,0:T(8,128)(2,1)S(1)}, u32[]{:S(2)}, u32[]{:S(2)}) collective-permute-start(bf16[4,2,512,256]{3,2,1,0:T(8,128)(2,1)S(1)} %get-tuple-element.102), channel_id=1, source_target_pairs={{0,1},{1,0},{2,3},{3,2},{4,5},{5,4},{6,7},{7,6},{8,9},{9,8},{10,11... | collective-permute-start | bytes 6291464 | tf_op jit(solution)/shard_map/ppermute | solution.py:437
  194.3 9.4 %collective-permute-start.8 = (bf16[2,512,256]{2,1,0:T(8,128)(2,1)S(1)}, bf16[2,512,256]{2,1,0:T(8,128)(2,1)S(1)}, u32[]{:S(2)}, u32[]{:S(2)}) collective-permute-start(bf16[2,512,256]{2,1,0:T(8,128)(2,1)S(1)} %bitcast.8), channel_id=1, source_target_pairs={{0,1},{1,0},{2,3},{3,2},{4,5},{5,4},{6,7},{7,6},{8,9},{9,8},{10,11... | collective-permute-start | bytes 1572872 | tf_op jit(solution)/shard_map/ppermute | solution.py:437

commit v5 on v4

--- a/solution.py
+++ b/solution.py
@@ -1,3 +1,5 @@
+import functools
+
 import jax
 import jax.numpy as jnp
 from jax import lax
@@ -90,8 +92,9 @@
     kn = (k * scale_k).astype(BF16)
     scores = dot(spread(qn, masks), kn, 1, 1)
     exponent = jnp.exp(scores) * times
-    attn = (exponent * (1.0 / jnp.sum(exponent, axis=-1, keepdims=True))).astype(BF16)
-    mixed = gathered(dot(attn, v), masks).astype(BF16)
+    share = 1.0 / jnp.sum(exponent, axis=-1, keepdims=True)
+    mixed = gathered(dot(exponent.astype(BF16), v) * share, masks).astype(BF16)
+    attn = (exponent * share).astype(BF16)
     stash["normed"][layer] = normed
     stash["inverse"][layer] = jnp.broadcast_to(inverse, (ROWS, ROWS))
     stash["qkv"][layer, 0] = qn
@@ -118,7 +121,8 @@
     stacked = spread(grad_mixed, masks)
     grad_attn = dot(stacked, v, 1, 1)
     attn_wide = attn.astype(F32)
-    inner = jnp.sum(attn_wide * grad_attn, axis=-1, keepdims=True)
+    product = grad_mixed.astype(F32) * stash["mixed"][layer].astype(F32)
+    inner = jnp.concatenate([jnp.sum(product * m, axis=-1, keepdims=True) for m in masks], axis=0)
     grad_scores = (attn_wide * (grad_attn - inner)).astype(BF16)
     grad_v = dot(attn, stacked, 0, 0).astype(BF16)
     grad_qn = gathered(dot(grad_scores, kn), masks)
@@ -193,13 +197,19 @@
             copy.wait()
 
 
-def weight_gradients(layer, normed, mixed, grad_qkv, grad_out, place, core):
-    full = dot(normed, grad_qkv, 0, 0).astype(BF16)
-    for block in range(3):
-        place[(block // 2) ^ core, layer, block % 2] = full[:, block * INNER : (block + 1) * INNER]
-    last = dot(mixed, grad_out, 0, 0).astype(BF16)
-    place[1 ^ core, layer, 1, :INNER] = last[:, :INNER]
-    place[1 ^ core, layer, 1, INNER:] = last[:, INNER:]
+def half_gradients(layer, side, normed, mixed, grad_qkv, grad_out, place):
+    @pl.when(side == 0)
+    def _():
+        full = dot(normed, grad_qkv[:, : 2 * INNER], 0, 0).astype(BF16)
+        place[layer, 0] = full[:, :INNER]
+        place[layer, 1] = full[:, INNER:]
+
+    @pl.when(side == 1)
+    def _():
+        place[layer, 0] = dot(normed, grad_qkv[:, 2 * INNER :], 0, 0).astype(BF16)
+        last = dot(mixed, grad_out, 0, 0).astype(BF16)
+        place[layer, 1, :INNER] = last[:, :INNER]
+        place[layer, 1, INNER:] = last[:, INNER:]
 
 
 def pack_kernel(info, qkv, out, own, half, sems):
@@ -291,16 +301,27 @@
         sheets.wait(layer)
 
 
-def gradient_kernel(info, *rest):
-    outside, (keep, send), inside = rest[: len(TERMS)], rest[len(TERMS) :][:2], rest[len(TERMS) + 2 : -3]
+def gradient_kernel(keep, info, *rest):
+    count = len(TERMS)
+    given, result, inside = rest[: -count - 4], rest[-count - 4], rest[-count - 3 : -3]
     place, in_sems, out_sems = rest[-3:]
-    sheets = Sheets(TERMS, outside, inside, in_sems, True)
-    results = Sheets(("keep", "send"), (keep, send), (place.at[0], place.at[1]), out_sems, False)
-    for layer in range(STAGE_LAYERS):
-        sheets.start(layer)
-    for layer in range(STAGE_LAYERS):
-        sheets.wait(layer)
-        weight_gradients(layer, *(sheets.refs[n][layer] for n in TERMS), place, info[2])
+    side = info[2] if keep else 1 - info[2]
+    choices = [Sheets(TERMS, (*given[i : i + 2], *given[-2:]), inside, in_sems, True) for i in range(0, len(given) - 2, 2)]
+    results = Sheets(("half",), (result,), (place,), out_sems, False)
+
+    def each(act):
+        for i, sheets in enumerate(choices):
+            if len(choices) == 1:
+                act(sheets)
+            else:
+                pl.when(info[3] == i)(functools.partial(act, sheets))
+
+    refs = choices[0].refs
+    for layer in range(STAGE_LAYERS):
+        each(lambda sheets: sheets.start(layer))
+    for layer in range(STAGE_LAYERS):
+        each(lambda sheets: sheets.wait(layer))
+        half_gradients(layer, side, *(refs[n][layer] for n in TERMS), place)
         results.start(layer)
     for layer in range(STAGE_LAYERS):
         results.wait(layer)
@@ -309,12 +330,12 @@
 def backward_kernel(info, grad_in, *rest):
     order = tuple(reversed(range(STAGE_LAYERS)))
     count = len(STASH)
-    outside, given, (keep, send) = rest[:count], rest[count:][:6], rest[count + 6 :][:2]
-    inside = rest[count + 8 :][:count]
-    weight_place, weight_sems, place, in_sems, out_sems = rest[-5:]
+    outside, given, outputs = rest[:count], rest[count:][:6], rest[count + 6 :][:3]
+    inside = rest[count + 9 :][:count]
+    weight_place, weight_sems, place, terms_qkv, terms_out, in_sems, out_sems = rest[-7:]
     weights = Weights(*given, weight_place, weight_sems, info[1], info[2], order)
     sheets = Sheets(STASH, outside, inside, in_sems, True)
-    results = Sheets(("keep", "send"), (keep, send), (place.at[0], place.at[1]), out_sems, False)
+    results = Sheets(("send", "grad_qkv", "grad_out"), outputs, (place, terms_qkv, terms_out), out_sems, False)
     for layer in order:
         sheets.start(layer)
         weights.each(layer, lambda copy: copy.start())
@@ -325,8 +346,10 @@
         weights.wait(layer)
         before = grad
         grad, grad_qkv = backward_layer(layer, grad, weights.layer(layer), masks, mean_matrix, sheets.refs)
-        weight_gradients(
-            layer, sheets.refs["normed"][layer], sheets.refs["mixed"][layer], grad_qkv, before, place, info[2]
+        terms_qkv[layer] = grad_qkv
+        terms_out[layer] = before
+        half_gradients(
+            layer, 1 - info[2], sheets.refs["normed"][layer], sheets.refs["mixed"][layer], grad_qkv, before, place
         )
         results.start(layer)
     for layer in order:
@@ -343,7 +366,7 @@
     pltpu.VMEM((STAGE_LAYERS, 4, D, INNER), BF16),
     pltpu.SemaphoreType.DMA((STAGE_LAYERS, 2)),
 ]
-GRAD_PLACE = pltpu.VMEM((2, STAGE_LAYERS, 2, D, INNER), BF16)
+GRAD_PLACE = pltpu.VMEM((STAGE_LAYERS, 2, D, INNER), BF16)
 TIMES = pltpu.VMEM((HEADS * ROWS, ROWS), F32)
 
 
@@ -355,7 +378,7 @@
     return pltpu.SemaphoreType.DMA((count, STAGE_LAYERS))
 
 
-def call(kernel, prefetched, in_specs, out_specs, out_shape, scratch, args, megabytes=20):
+def call(kernel, prefetched, in_specs, out_specs, out_shape, scratch, args, megabytes=48):
     return pl.pallas_call(
         kernel,
         grid_spec=pltpu.PrefetchScalarGridSpec(
@@ -373,7 +396,7 @@
 def run_pack(info, w_qkv, w_out):
     shapes = [jax.ShapeDtypeStruct((blocks, D, INNER), BF16) for blocks in (4, 2)]
     sems = [pltpu.SemaphoreType.DMA((2, 5))]
-    return call(pack_kernel, 1, [IN_HBM] * 2, [ANYWHERE] * 2, shapes, sems, (info, w_qkv, w_out), 60)
+    return call(pack_kernel, 1, [IN_HBM] * 2, [ANYWHERE] * 2, shapes, sems, (info, w_qkv, w_out), 1)
 
 
 def run_unpack(info, mine, other):
@@ -391,7 +414,7 @@
         [HIDDEN] + layered(STASH, jax.ShapeDtypeStruct),
         layered(STASH, pltpu.VMEM) + WEIGHT_SCRATCH + [semaphores(len(STASH)), TIMES],
         (info, *tables, nodes, *weights),
-        59,
+        58,
     )
 
 
@@ -408,28 +431,33 @@
     )
 
 
-def run_gradients(info, terms):
+def run_gradients(info, terms, keep):
     return call(
-        gradient_kernel,
+        functools.partial(gradient_kernel, keep),
         1,
-        [ANYWHERE] * len(TERMS),
-        [ANYWHERE] * 2,
-        [GRAD_HALF] * 2,
-        layered(TERMS, pltpu.VMEM) + [GRAD_PLACE, semaphores(len(TERMS)), semaphores(2)],
+        [ANYWHERE] * len(terms),
+        ANYWHERE,
+        GRAD_HALF,
+        layered(TERMS, pltpu.VMEM) + [GRAD_PLACE, semaphores(len(TERMS)), semaphores(1)],
         (info, *terms),
     )
 
 
 def run_backward(info, grad, stash, weights):
+    terms = layered(TERMS, jax.ShapeDtypeStruct)[2:]
     return call(
         backward_kernel,
         1,
         [HIDDEN_BLOCK] + [ANYWHERE] * (len(STASH) + 6),
-        [ANYWHERE] * 2,
-        [GRAD_HALF] * 2,
-        layered(STASH, pltpu.VMEM) + WEIGHT_SCRATCH + [GRAD_PLACE, semaphores(len(STASH)), semaphores(2)],
+        [ANYWHERE] * 3,
+        [GRAD_HALF] + terms,
+        layered(STASH, pltpu.VMEM)
+        + WEIGHT_SCRATCH
+        + [GRAD_PLACE]
+        + layered(TERMS, pltpu.VMEM)[2:]
+        + [semaphores(len(STASH)), semaphores(3)],
         (info, grad, *stash, *weights),
-        20,
+        48,
     )
 
 
@@ -456,7 +484,7 @@
     y, x, core = lax.axis_index("yl"), lax.axis_index("xl"), lax.axis_index("core")
     me = y * 2 + x
     batch = jnp.where(stage == 0, y, 1 - y) * 2 + x
-    info = jnp.stack([batch, me, core]).astype(jnp.int32)
+    info = jnp.stack([batch, me, core, stage]).astype(jnp.int32)
     tables = (tile_lists.transpose(1, 2, 0), counts.transpose(1, 0), virtual)
     own, half = run_pack(info, w_qkv, w_out)
     near2 = fetched(half, 1, 0)
@@ -470,11 +498,13 @@
     hidden = lax.ppermute(hidden, ("yh", "yl"), across)
     grad, *terms = run_chain(info, tables, hidden, cotangent, weights)
     grad = lax.ppermute(grad, ("yh", "yl"), across)
-    keep, send = lax.cond(
+    send, grad_qkv, grad_out = lax.cond(
         stage == 0,
         lambda: tuple(run_backward(info, grad, stash, weights)),
-        lambda: tuple(run_gradients(info, terms)),
-    )
+        lambda: (run_gradients(info, terms, False), *terms[2:]),
+    )
+    first = dict(zip(STASH, stash))
+    keep = run_gradients(info, (first["normed"], first["mixed"], *terms[:2], grad_qkv, grad_out), True)
 
     def added(value, axis):
         return jnp.sum(value.astype(F32), axis=axis).astype(BF16)

time: 206 us -> 189 us (0.917)
  Pallas kernels: 48 us -> 33.6 us
  waiting for transfers between devices: 26.2 us -> 22.8 us
  local copies, waits for them, and re-layouts: 0.08 us -> 2.17 us
    pallas_call x5 -> x6, Pallas kernels: 48 us -> 33.6 us  [call(): pl.pallas_call(kernel, grid_spec=pltpu.PrefetchScalarGridSpec(num_scalar_...]
    ppermute x4, waiting for transfers between devices: 6.78 us -> 3.62 us  [swapped(): return lax.ppermute(value, axis, [(0, 1), (1, 0)])]
    unnamed x12 -> x16, local copies, waits for them, and re-layouts: 0.03 us -> 2.11 us
  transfers between devices with their start and end apart: 9 -> 9, of which waited for: 7 -> 7; matrix products, arithmetic and copies ran while one was open for 0% -> 0% of each run, Pallas kernels for 0% -> 2%
where the time goes in v5:
time: 189 us; the launch traced here: 188 us
  blocking collectives  87.3 us (46%)
  starting transfers between devices  40.2 us (21%)
  Pallas kernels  33.6 us (18%)
  waiting for transfers between devices  22.8 us (12%)
  local copies, waits for them, and re-layouts  2.17 us (1%)
    pallas_call x6, Pallas kernels, call(): pl.pallas_call(kernel, grid_spec=pltpu.PrefetchScalarGridSpec(num_scalar_...  33.6 us
    all_to_all x1, blocking collectives, per_device(): lax.all_to_all(total.reshape(8, D, INNER), ('yl', 'xl', 'xh'), 0, 0, tile...  29.9 us
    all_to_all x1, blocking collectives, per_device(): lax.all_to_all(repeated(total, far), 'zh', 0, 0, tiled=True)  28.6 us
    ppermute x4, starting transfers between devices, swapped(): return lax.ppermute(value, axis, [(0, 1), (1, 0)])  20.7 us
    all_to_all x1, blocking collectives, per_device(): lax.all_to_all(repeated(total, 2 * near), ('xh', 'zl'), 0, 0, tiled=True)  17.3 us
    ppermute x3, waiting for transfers between devices, fetched(): return lax.ppermute(value, axes, pairs)  13.2 us
    all_to_all x1, blocking collectives, per_device(): total = added(lax.all_to_all(total, 'zl', 0, 0, tiled=True), 0)  11.5 us
    ppermute x3, starting transfers between devices, fetched(): return lax.ppermute(value, axes, pairs)  10.3 us
  transfers between devices with their start and end apart: 9, of which 7 were waited for; matrix products, arithmetic and copies ran while one was open for 0% of the time, Pallas kernels for 2%

profile of v5, /device:TPU:1, one launch (start us, length us, event | category | flops | bytes accessed | tf_op | source)
XLA Modules:
  0.0 188.2 jit_solution(14308722784002881126)
XLA Ops:
  0.6 0.1 pad_add_fusion.info
  0.7 1.1 copy-done
  1.9 0.9 copy-done.2
  2.8 0.8 shard_map.86
  3.6 6.2 %collective-permute-start.3 = (bf16[2,512,256]{2,1,0:T(8,128)(2,1)S(1)}, bf16[2,512,256]{2,1,0:T(8,128)(2,1)S(1)}, u32[]{:S(2)}, u32[]{:S(2)}) collective-permute-start(bf16[2,512,256]{2,1,0:T(8,128)(2,1)S(1)} %get-tuple-element.77), channel_id=1, source_target_pairs={{0,192},{1,195},{2,194},{3,193},{64,128},{65,131},{66,130},{67,129... | collective-permute-start | bytes 1572872 | tf_op jit(solution)/shard_map/ppermute | solution.py:479
  9.8 2.1 %collective-permute-start.1 = (bf16[2,512,256]{2,1,0:T(8,128)(2,1)S(1)}, bf16[2,512,256]{2,1,0:T(8,128)(2,1)S(1)}, u32[]{:S(2)}, u32[]{:S(2)}) collective-permute-start(bf16[2,512,256]{2,1,0:T(8,128)(2,1)S(1)} %get-tuple-element.77), channel_id=1, source_target_pairs={{0,128},{1,129},{2,130},{3,131},{64,192},{65,193},{66,194},{67,195... | collective-permute-start | bytes 1572872 | tf_op jit(solution)/shard_map/ppermute | solution.py:479
  11.9 2.0 %collective-permute-start = (bf16[4,512,256]{2,1,0:T(8,128)(2,1)S(1)}, bf16[4,512,256]{2,1,0:T(8,128)(2,1)S(1)}, u32[]{:S(2)}, u32[]{:S(2)}) collective-permute-start(bf16[4,512,256]{2,1,0:T(8,128)(2,1)S(1)} %get-tuple-element.76.rest_0_), channel_id=1, source_target_pairs={{0,64},{1,67},{2,66},{3,65},{64,0},{65,3},{66,2},{67,1},{128,192},... | collective-permute-start | bytes 3145736 | tf_op jit(solution)/shard_map/ppermute | solution.py:479
  13.9 4.5 %collective-permute-done.3.rest_4_ = bf16[2,512,256]{2,1,0:T(8,128)(2,1)S(1)} collective-permute-done((bf16[2,512,256]{2,1,0:T(8,128)(2,1)S(1)}, bf16[2,512,256]{2,1,0:T(8,128)(2,1)S(1)}, u32[]{:S(2)}, u32[]{:S(2)}) %collective-permute-start.3) | collective-permute-done | bytes 524320 | tf_op jit(solution)/shard_map/ppermute | solution.py:479
  18.4 6.3 %collective-permute-start.4 = (bf16[2,512,256]{2,1,0:T(8,128)(2,1)S(1)}, bf16[2,512,256]{2,1,0:T(8,128)(2,1)S(1)}, u32[]{:S(2)}, u32[]{:S(2)}) collective-permute-start(bf16[2,512,256]{2,1,0:T(8,128)(2,1)S(1)} %collective-permute-done.3.rest_4_), channel_id=1, source_target_pairs={{0,1},{1,0},{2,3},{3,2},{4,5},{5,4},{6,7},{7,6},{8,9},{9,8},{10,11... | collective-permute-start | bytes 1572872 | tf_op jit(solution)/shard_map/ppermute | solution.py:465
  24.7 8.7 %collective-permute-done.1.rest_2_ = bf16[2,512,256]{2,1,0:T(8,128)(2,1)S(1)} collective-permute-done((bf16[2,512,256]{2,1,0:T(8,128)(2,1)S(1)}, bf16[2,512,256]{2,1,0:T(8,128)(2,1)S(1)}, u32[]{:S(2)}, u32[]{:S(2)}) %collective-permute-start.1) | collective-permute-done | bytes 524320 | tf_op jit(solution)/shard_map/ppermute | solution.py:479
  33.4 2.4 %collective-permute-start.2 = (bf16[2,512,256]{2,1,0:T(8,128)(2,1)S(1)}, bf16[2,512,256]{2,1,0:T(8,128)(2,1)S(1)}, u32[]{:S(2)}, u32[]{:S(2)}) collective-permute-start(bf16[2,512,256]{2,1,0:T(8,128)(2,1)S(1)} %collective-permute-done.1.rest_2_), channel_id=1, source_target_pairs={{0,1},{1,0},{2,3},{3,2},{4,5},{5,4},{6,7},{7,6},{8,9},{9,8},{10,11... | collective-permute-start | bytes 1572872 | tf_op jit(solution)/shard_map/ppermute | solution.py:465
  35.8 1.5 collective-permute-done.2.rest_3_
  37.4 7.7 %shard_map.87 = (bf16[128,512]{1,0:T(8,128)(2,1)}, bf16[4,128,512]{2,1,0:T(8,128)(2,1)}, f32[4,128,128]{2,1,0:T(8,128)}, bf16[4,3,128,256]{3,2,1,0:T(8,128)(2,1)...) custom-call(s32[4]{0:T(128)S(1)} %pad_add_fusion.info, ...), custom_call_target="tpu_custom_call" | custom-call | tf_op jit(solution)/shard_map/pallas_call | solution.py:382
  45.1 4.6 %collective-permute-start.5 = (bf16[128,512]{1,0:T(8,128)(2,1)}, bf16[128,512]{1,0:T(8,128)(2,1)S(1)}, u32[]{:S(2)}, u32[]{:S(2)}) collective-permute-start(bf16[128,512]{1,0:T(8,128)(2,1)} %get-tuple-element.80), channel_id=1, source_target_pairs={{0,384},{128,256},{256,128},{384,0},{1,385},{129,257},{257,129},{3... | collective-permute-start | bytes 393224 | tf_op jit(solution)/shard_map/ppermute | solution.py:498
  49.8 3.5 %collective-permute-done.5.hidden_in = bf16[128,512]{1,0:T(8,128)(2,1)S(1)} collective-permute-done((bf16[128,512]{1,0:T(8,128)(2,1)}, bf16[128,512]{1,0:T(8,128)(2,1)S(1)}, u32[]{:S(2)}, u32[]{:S(2)}) %collective-permute-start.5) | collective-permute-done | bytes 131104 | tf_op jit(solution)/shard_map/ppermute | solution.py:498
  53.3 10.1 %shard_map.88 = (bf16[128,512]{1,0:T(8,128)(2,1)S(1)}, bf16[4,128,512]{2,1,0:T(8,128)(2,1)}, bf16[4,128,256]{2,1,0:T(8,128)(2,1)}, bf16[4,128,768]{2,1,0:T(8,128)(2,1)}, bf16[4,128,512]{2,1,0:T(8,128)(2,1)}) custom-call(s32[4]{0:T(128)S(1)} %pad_add_fusion.info, s32[2,2,4]{2,1,0:T(2,128)S(1)} %bitcast.12, s32[2,4]{1,0:T(2,128)S(1)} %bitcast.14, ...), custom_call_target="tpu_custom_call" | custom-call | tf_op jit(solution)/shard_map/pallas_call | solution.py:382
  63.4 4.5 %collective-permute-start.6 = (bf16[128,512]{1,0:T(8,128)(2,1)S(1)}, bf16[128,512]{1,0:T(8,128)(2,1)}, u32[]{:S(2)}, u32[]{:S(2)}) collective-permute-start(bf16[128,512]{1,0:T(8,128)(2,1)S(1)} %get-tuple-element.85), channel_id=1, source_target_pairs={{0,384},{128,256},{256,128},{384,0},{1,385},{129,257},{257,129},{3... | collective-permute-start | bytes 393224 | tf_op jit(solution)/shard_map/ppermute | solution.py:500
  68.0 2.5 %collective-permute-done.6 = bf16[128,512]{1,0:T(8,128)(2,1)} collective-permute-done((bf16[128,512]{1,0:T(8,128)(2,1)S(1)}, bf16[128,512]{1,0:T(8,128)(2,1)}, u32[]{:S(2)}, u32[]{:S(2)}) %collective-permute-start.6) | collective-permute-done | bytes 131104 | tf_op jit(solution)/shard_map/ppermute | solution.py:500
  70.5 10.1 %conditional.1 = ((bf16[4,2,512,256]{3,2,1,0:T(8,128)(2,1)}, bf16[4,128,768]{2,1,0:T(8,128)(2,1)}, bf16[4,128,512]{2,1,0:T(8,128)(2,1)})) conditional(s32[]{:T(128)} %convert_element_type.8, (s32[4]{0:T(128)S(1)}, bf16[4,128,512]{2,1,0:T(8,128)(2,1)}, bf16[4,128,256]{2,1,0:T(8,128)(2,1)}, bf16[4,128,768]{2,1,0:T(8,128)(2,1)}, ...), branch_computations={%region_0.1_spmd, %region_1.2_spmd} | conditional | bytes 32 | solution.py:501
  70.5 10.1 %branch_1_fun.1 = (bf16[4,2,512,256]{3,2,1,0:T(8,128)(2,1)}, bf16[4,128,768]{2,1,0:T(8,128)(2,1)}, bf16[4,128,512]{2,1,0:T(8,128)(2,1)}) custom-call(s32[4]{0:T(128)S(1)} %get-tuple-element.43.info, bf16[128,512]{1,0:T(8,128)(2,1)} %get-tuple-element.44.grad_in, bf16[4,128,512]{2,1,0:T(8,128)(2,1)} %get-tuple-element.45.rest_0_, ...), custom_call_target="tpu_custom_call" | custom-call | tf_op jit(solution)/shard_map/cond/branch_1_fun/pallas_call | solution.py:382
  80.6 4.2 %collective-permute-start.7 = (bf16[4,2,512,256]{3,2,1,0:T(8,128)(2,1)}, bf16[4,2,512,256]{3,2,1,0:T(8,128)(2,1)S(1)}, u32[]{:S(2)}, u32[]{:S(2)}) collective-permute-start(bf16[4,2,512,256]{3,2,1,0:T(8,128)(2,1)} %get-tuple-element.92), channel_id=1, source_target_pairs={{0,1},{1,0},{2,3},{3,2},{4,5},{5,4},{6,7},{7,6},{8,9},{9,8},{10,11... | collective-permute-start | bytes 6291464 | tf_op jit(solution)/shard_map/ppermute | solution.py:465
  84.8 3.4 %shard_map.89 = bf16[4,2,512,256]{3,2,1,0:T(8,128)(2,1)S(1)} custom-call(s32[4]{0:T(128)S(1)} %pad_add_fusion.info, bf16[4,128,512]{2,1,0:T(8,128)(2,1)} %get-tuple-element.78.rest_0_, bf16[4,128,256]{2,1,0:T(8,128)(2,1)S(1)} %get-tuple-element.79.rest_1_, bf16[4,128,512]{2,1,0:T(8,128)(2,1)} %get-tuple-element.81.rest_2_, ...), custom_call_target="tpu_custom_call" | custom-call | tf_op jit(solution)/shard_map/pallas_call | solution.py:382
  88.1 0.6 collective-permute-done.7
  88.8 0.5 add_convert_fusion
  89.3 29.9 %all_to_all.20 = bf16[8,512,256]{2,1,0:T(8,128)(2,1)S(1)} all-to-all(bf16[8,512,256]{2,1,0:T(8,128)(2,1)S(1)} %bitcast.15), channel_id=1, replica_groups=mesh['yh'=2,'yl'=2,'xl'=2,'zh'=4,'zl'=4,'xh'=2,'core'=2] {'yl','xl','xh'}, dimensions={0} | all-to-all | bytes 4194304 | tf_op jit(solution)/shard_map/all_to_all | solution.py:518
  119.2 0.4 reduce_sum.36
  119.5 11.5 %all_to_all.21 = bf16[4,128,256]{2,1,0:T(8,128)(2,1)S(1)} all-to-all(bf16[4,128,256]{2,1,0:T(8,128)(2,1)S(1)} %bitcast.16), channel_id=1, replica_groups=mesh['yh'=2,'yl'=2,'xl'=2,'zh'=4,'zl'=4,'xh'=2,'core'=2] {'zl'}, dimensions={0} | all-to-all | bytes 524288 | tf_op jit(solution)/shard_map/all_to_all | solution.py:520
  131.1 28.6 %all_to_all.22 = bf16[4,128,256]{2,1,0:T(8,128)(2,1)S(1)} all-to-all(bf16[4,128,256]{2,1,0:T(8,128)(2,1)S(1)} %broadcast_in_dim.6), channel_id=1, replica_groups=mesh['yh'=2,'yl'=2,'xl'=2,'zh'=4,'zl'=4,'xh'=2,'core'=2] {'zh'}, dimensions={0} | all-to-all | bytes 524288 | tf_op jit(solution)/shard_map/all_to_all | solution.py:521
  159.8 17.3 %all_to_all.23 = bf16[8,128,256]{2,1,0:T(8,128)(2,1)S(1)} all-to-all(bf16[8,128,256]{2,1,0:T(8,128)(2,1)S(1)} %broadcast_in_dim.7), channel_id=1, replica_groups=mesh['yh'=2,'yl'=2,'xl'=2,'zh'=4,'zl'=4,'xh'=2,'core'=2] {'xh','zl'}, dimensions={0} | all-to-all | bytes 1048576 | tf_op jit(solution)/shard_map/all_to_all | solution.py:522
  177.1 7.9 %collective-permute-start.8 = (bf16[2,512,256]{2,1,0:T(8,128)(2,1)S(1)}, bf16[2,512,256]{2,1,0:T(8,128)(2,1)S(1)}, u32[]{:S(2)}, u32[]{:S(2)}) collective-permute-start(bf16[2,512,256]{2,1,0:T(8,128)(2,1)S(1)} %bitcast.9), channel_id=1, source_target_pairs={{0,1},{1,0},{2,3},{3,2},{4,5},{5,4},{6,7},{7,6},{8,9},{9,8},{10,11... | collective-permute-start | bytes 1572872 | tf_op jit(solution)/shard_map/ppermute | solution.py:465
  185.0 1.5 collective-permute-done.8.other
  186.5 1.6 shard_map.90
  (20 shorter events, 0.2 us)
Async XLA Ops:
  0.7 1.1 copy-start
  1.9 0.9 copy-start.2
  3.6 14.8 %collective-permute-start.3 = (bf16[2,512,256]{2,1,0:T(8,128)(2,1)S(1)}, bf16[2,512,256]{2,1,0:T(8,128)(2,1)S(1)}, u32[]{:S(2)}, u32[]{:S(2)}) collective-permute-start(bf16[2,512,256]{2,1,0:T(8,128)(2,1)S(1)} %get-tuple-element.77), channel_id=1, source_target_pairs={{0,192},{1,195},{2,194},{3,193},{64,128},{65,131},{66,130},{67,129... | collective-permute-start | bytes 1572872 | tf_op jit(solution)/shard_map/ppermute | solution.py:479
  9.8 23.6 %collective-permute-start.1 = (bf16[2,512,256]{2,1,0:T(8,128)(2,1)S(1)}, bf16[2,512,256]{2,1,0:T(8,128)(2,1)S(1)}, u32[]{:S(2)}, u32[]{:S(2)}) collective-permute-start(bf16[2,512,256]{2,1,0:T(8,128)(2,1)S(1)} %get-tuple-element.77), channel_id=1, source_target_pairs={{0,128},{1,129},{2,130},{3,131},{64,192},{65,193},{66,194},{67,195... | collective-permute-start | bytes 1572872 | tf_op jit(solution)/shard_map/ppermute | solution.py:479
  11.9 25.4 %collective-permute-start = (bf16[4,512,256]{2,1,0:T(8,128)(2,1)S(1)}, bf16[4,512,256]{2,1,0:T(8,128)(2,1)S(1)}, u32[]{:S(2)}, u32[]{:S(2)}) collective-permute-start(bf16[4,512,256]{2,1,0:T(8,128)(2,1)S(1)} %get-tuple-element.76.rest_0_), channel_id=1, source_target_pairs={{0,64},{1,67},{2,66},{3,65},{64,0},{65,3},{66,2},{67,1},{128,192},... | collective-permute-start | bytes 3145736 | tf_op jit(solution)/shard_map/ppermute | solution.py:479
  18.4 17.4 %collective-permute-start.4 = (bf16[2,512,256]{2,1,0:T(8,128)(2,1)S(1)}, bf16[2,512,256]{2,1,0:T(8,128)(2,1)S(1)}, u32[]{:S(2)}, u32[]{:S(2)}) collective-permute-start(bf16[2,512,256]{2,1,0:T(8,128)(2,1)S(1)} %collective-permute-done.3.rest_4_), channel_id=1, source_target_pairs={{0,1},{1,0},{2,3},{3,2},{4,5},{5,4},{6,7},{7,6},{8,9},{9,8},{10,11... | collective-permute-start | bytes 1572872 | tf_op jit(solution)/shard_map/ppermute | solution.py:465
  33.4 3.9 %collective-permute-start.2 = (bf16[2,512,256]{2,1,0:T(8,128)(2,1)S(1)}, bf16[2,512,256]{2,1,0:T(8,128)(2,1)S(1)}, u32[]{:S(2)}, u32[]{:S(2)}) collective-permute-start(bf16[2,512,256]{2,1,0:T(8,128)(2,1)S(1)} %collective-permute-done.1.rest_2_), channel_id=1, source_target_pairs={{0,1},{1,0},{2,3},{3,2},{4,5},{5,4},{6,7},{7,6},{8,9},{9,8},{10,11... | collective-permute-start | bytes 1572872 | tf_op jit(solution)/shard_map/ppermute | solution.py:465
  35.8 17.4 %copy-start.6 = (bf16[2,512,256]{2,1,0:T(8,128)(2,1)}, bf16[2,512,256]{2,1,0:T(8,128)(2,1)S(1)}, u32[]{:S(2)}) copy-start(bf16[2,512,256]{2,1,0:T(8,128)(2,1)S(1)} %collective-permute-done.4.rest_5_) | copy-start | bytes 1572868
  37.3 15.9 %copy-start.7 = (bf16[2,512,256]{2,1,0:T(8,128)(2,1)}, bf16[2,512,256]{2,1,0:T(8,128)(2,1)S(1)}, u32[]{:S(2)}) copy-start(bf16[2,512,256]{2,1,0:T(8,128)(2,1)S(1)} %collective-permute-done.2.rest_3_) | copy-start | bytes 1572868
  37.3 15.9 %copy-start.1 = (bf16[4,128,512]{2,1,0:T(8,128)(2,1)S(1)}, bf16[4,128,512]{2,1,0:T(8,128)(2,1)}, u32[]{:S(2)}) copy-start(bf16[4,128,512]{2,1,0:T(8,128)(2,1)} %grad_in.1) | copy-start | bytes 1572868
  37.3 15.9 %copy-start.3 = (s32[4,2,2]{0,2,1:T(2,128)S(1)}, s32[4,2,2]{0,2,1:T(2,128)}, u32[]{:S(2)}) copy-start(s32[4,2,2]{0,2,1:T(2,128)} %param.13) | copy-start | bytes 196
  37.4 15.9 %copy-start.4 = (s32[4,2]{0,1:T(2,128)S(1)}, s32[4,2]{0,1:T(2,128)}, u32[]{:S(2)}) copy-start(s32[4,2]{0,1:T(2,128)} %param.14) | copy-start | bytes 100
  37.4 15.9 %copy-start.5 = (s32[4]{0:T(128)S(1)}, s32[4]{0:T(128)}, u32[]{:S(2)}) copy-start(s32[4]{0:T(128)} %virtual.3) | copy-start | bytes 52
  45.1 8.1 %collective-permute-start.5 = (bf16[128,512]{1,0:T(8,128)(2,1)}, bf16[128,512]{1,0:T(8,128)(2,1)S(1)}, u32[]{:S(2)}, u32[]{:S(2)}) collective-permute-start(bf16[128,512]{1,0:T(8,128)(2,1)} %get-tuple-element.80), channel_id=1, source_target_pairs={{0,384},{128,256},{256,128},{384,0},{1,385},{129,257},{257,129},{3... | collective-permute-start | bytes 393224 | tf_op jit(solution)/shard_map/ppermute | solution.py:498
  63.4 7.0 %collective-permute-start.6 = (bf16[128,512]{1,0:T(8,128)(2,1)S(1)}, bf16[128,512]{1,0:T(8,128)(2,1)}, u32[]{:S(2)}, u32[]{:S(2)}) collective-permute-start(bf16[128,512]{1,0:T(8,128)(2,1)S(1)} %get-tuple-element.85), channel_id=1, source_target_pairs={{0,384},{128,256},{256,128},{384,0},{1,385},{129,257},{257,129},{3... | collective-permute-start | bytes 393224 | tf_op jit(solution)/shard_map/ppermute | solution.py:500
  80.6 8.2 %collective-permute-start.7 = (bf16[4,2,512,256]{3,2,1,0:T(8,128)(2,1)}, bf16[4,2,512,256]{3,2,1,0:T(8,128)(2,1)S(1)}, u32[]{:S(2)}, u32[]{:S(2)}) collective-permute-start(bf16[4,2,512,256]{3,2,1,0:T(8,128)(2,1)} %get-tuple-element.92), channel_id=1, source_target_pairs={{0,1},{1,0},{2,3},{3,2},{4,5},{5,4},{6,7},{7,6},{8,9},{9,8},{10,11... | collective-permute-start | bytes 6291464 | tf_op jit(solution)/shard_map/ppermute | solution.py:465
  177.1 9.4 %collective-permute-start.8 = (bf16[2,512,256]{2,1,0:T(8,128)(2,1)S(1)}, bf16[2,512,256]{2,1,0:T(8,128)(2,1)S(1)}, u32[]{:S(2)}, u32[]{:S(2)}) collective-permute-start(bf16[2,512,256]{2,1,0:T(8,128)(2,1)S(1)} %bitcast.9), channel_id=1, source_target_pairs={{0,1},{1,0},{2,3},{3,2},{4,5},{5,4},{6,7},{7,6},{8,9},{9,8},{10,11... | collective-permute-start | bytes 1572872 | tf_op jit(solution)/shard_map/ppermute | solution.py:465

commit v6 on v4

--- a/solution.py
+++ b/solution.py
@@ -1,3 +1,5 @@
+import functools
+
 import jax
 import jax.numpy as jnp
 from jax import lax
@@ -90,8 +92,9 @@
     kn = (k * scale_k).astype(BF16)
     scores = dot(spread(qn, masks), kn, 1, 1)
     exponent = jnp.exp(scores) * times
-    attn = (exponent * (1.0 / jnp.sum(exponent, axis=-1, keepdims=True))).astype(BF16)
-    mixed = gathered(dot(attn, v), masks).astype(BF16)
+    share = 1.0 / jnp.sum(exponent, axis=-1, keepdims=True)
+    mixed = gathered(dot(exponent.astype(BF16), v) * share, masks).astype(BF16)
+    attn = (exponent * share).astype(BF16)
     stash["normed"][layer] = normed
     stash["inverse"][layer] = jnp.broadcast_to(inverse, (ROWS, ROWS))
     stash["qkv"][layer, 0] = qn
@@ -118,7 +121,8 @@
     stacked = spread(grad_mixed, masks)
     grad_attn = dot(stacked, v, 1, 1)
     attn_wide = attn.astype(F32)
-    inner = jnp.sum(attn_wide * grad_attn, axis=-1, keepdims=True)
+    product = grad_mixed.astype(F32) * stash["mixed"][layer].astype(F32)
+    inner = jnp.concatenate([jnp.sum(product * m, axis=-1, keepdims=True) for m in masks], axis=0)
     grad_scores = (attn_wide * (grad_attn - inner)).astype(BF16)
     grad_v = dot(attn, stacked, 0, 0).astype(BF16)
     grad_qn = gathered(dot(grad_scores, kn), masks)
@@ -193,13 +197,33 @@
             copy.wait()
 
 
-def weight_gradients(layer, normed, mixed, grad_qkv, grad_out, place, core):
+def weight_gradients(slot, normed, mixed, grad_qkv, grad_out, place, core):
     full = dot(normed, grad_qkv, 0, 0).astype(BF16)
     for block in range(3):
-        place[(block // 2) ^ core, layer, block % 2] = full[:, block * INNER : (block + 1) * INNER]
+        place[(block // 2) ^ core, slot, block % 2] = full[:, block * INNER : (block + 1) * INNER]
     last = dot(mixed, grad_out, 0, 0).astype(BF16)
-    place[1 ^ core, layer, 1, :INNER] = last[:, :INNER]
-    place[1 ^ core, layer, 1, INNER:] = last[:, INNER:]
+    place[1 ^ core, slot, 1, :INNER] = last[:, :INNER]
+    place[1 ^ core, slot, 1, INNER:] = last[:, INNER:]
+
+
+def both(a, b):
+    return jnp.concatenate([a, b], axis=0)
+
+
+class Results:
+    def __init__(self, outs, place, sems):
+        self.copies = [
+            [pltpu.make_async_copy(place.at[side, slot], outs[side].at[slot], sems.at[side, slot]) for side in range(2)]
+            for slot in range(2)
+        ]
+
+    def start(self, slot):
+        for copy in self.copies[slot]:
+            copy.start()
+
+    def wait(self, slot):
+        for copy in self.copies[slot]:
+            copy.wait()
 
 
 def pack_kernel(info, qkv, out, own, half, sems):
@@ -266,71 +290,139 @@
         sheets.wait(layer)
 
 
-def chain_kernel(info, tile_lists, counts, virtual, hidden_in, grad_in, *rest):
-    weights = Weights(*rest[:6], *rest[-4:-2], info[1], info[2], range(STAGE_LAYERS))
-    grad_out, outside = rest[6], rest[7 : 7 + len(TERMS)]
-    stash = dict(zip(STASH, rest[7 + len(TERMS) :][: len(STASH)]))
-    extra = rest[7 + len(TERMS) + len(STASH) :][:2]
-    sheets = Sheets(TERMS, outside, (stash["normed"], stash["mixed"], *extra), rest[-2], False)
-    weights.start()
-    masks, mean_matrix = head_masks(), head_mean_matrix()
-    times = rest[-1]
-    times[...] = multiplicities(info[0], tile_lists, counts, virtual)
-    hidden = hidden_in[...]
+def run_chain(hidden, grad, weights, times, masks, mean_matrix, stash, terms_qkv, terms_out, done):
     for layer in range(STAGE_LAYERS):
         weights.wait(layer)
         hidden = forward_layer(layer, hidden, weights.layer(layer), times[...], masks, mean_matrix, stash)
-    grad = grad_in[0]
     for layer in reversed(range(STAGE_LAYERS)):
-        sheets.refs["grad_out"][layer] = grad
+        terms_out[layer] = grad
         grad, grad_qkv = backward_layer(layer, grad, weights.layer(layer), masks, mean_matrix, stash)
-        sheets.refs["grad_qkv"][layer] = grad_qkv
-        sheets.start(layer)
-    grad_out[...] = grad
-    for layer in range(STAGE_LAYERS):
-        sheets.wait(layer)
-
-
-def gradient_kernel(info, *rest):
-    outside, (keep, send), inside = rest[: len(TERMS)], rest[len(TERMS) :][:2], rest[len(TERMS) + 2 : -3]
-    place, in_sems, out_sems = rest[-3:]
-    sheets = Sheets(TERMS, outside, inside, in_sems, True)
-    results = Sheets(("keep", "send"), (keep, send), (place.at[0], place.at[1]), out_sems, False)
-    for layer in range(STAGE_LAYERS):
-        sheets.start(layer)
-    for layer in range(STAGE_LAYERS):
-        sheets.wait(layer)
-        weight_gradients(layer, *(sheets.refs[n][layer] for n in TERMS), place, info[2])
-        results.start(layer)
-    for layer in range(STAGE_LAYERS):
-        results.wait(layer)
-
-
-def backward_kernel(info, grad_in, *rest):
+        terms_qkv[layer] = grad_qkv
+        done(layer)
+    return grad
+
+
+def middle_kernel(info, tile_lists, counts, virtual, hidden_in, grad_in, nodes_in, *rest):
+    given, grad_out, rest = rest[:6], rest[6], rest[7:]
+    terms_outside, stash_outside, inside = rest[: len(TERMS)], rest[len(TERMS) :][: len(STASH)], rest[len(TERMS) + len(STASH) :]
+    stash_inside, (terms_qkv, terms_out) = inside[: len(STASH)], inside[len(STASH) :][:2]
+    place, weight_sems, terms_sems, stash_sems, times = inside[len(STASH) + 2 :]
+    weights = Weights(*given, place, weight_sems, info[1], info[2], range(STAGE_LAYERS))
+    stash = dict(zip(STASH, stash_inside))
+    weights.start()
+    masks, mean_matrix = head_masks(), head_mean_matrix()
+
+    @pl.when(info[3] == 1)
+    def _():
+        times[...] = multiplicities(info[0], tile_lists, counts, virtual)
+        sheets = Sheets(TERMS, terms_outside, (stash["normed"], stash["mixed"], terms_qkv, terms_out), terms_sems, False)
+        grad_out[...] = run_chain(
+            hidden_in[...], grad_in[0], weights, times, masks, mean_matrix, stash, terms_qkv, terms_out, sheets.start
+        )
+        for layer in range(STAGE_LAYERS):
+            sheets.wait(layer)
+
+    @pl.when(info[3] == 0)
+    def _():
+        times[...] = multiplicities(info[4], tile_lists, counts, virtual)
+        sheets = Sheets(STASH, stash_outside, stash_inside, stash_sems, False)
+        hidden = nodes_in[0]
+        for layer in range(STAGE_LAYERS):
+            weights.wait(layer)
+            hidden = forward_layer(layer, hidden, weights.layer(layer), times[...], masks, mean_matrix, stash)
+            sheets.start(layer)
+        for layer in range(STAGE_LAYERS):
+            sheets.wait(layer)
+
+
+def later_kernel(info, tile_lists, counts, virtual, hidden_in, grad_in, *rest):
+    given, outside, outs, inside = rest[:6], rest[6:10], rest[10:12], rest[12:]
+    stash = dict(zip(STASH, inside[: len(STASH)]))
+    terms_qkv, terms_out, *first = inside[len(STASH) :][:6]
+    weight_place, weight_sems, place, terms_sems, out_sems, times = inside[len(STASH) + 6 :]
+    low = 2 * info[5]
+    copies = [
+        pltpu.make_async_copy(outside[i].at[low + slot], first[i].at[slot], terms_sems.at[i, slot])
+        for i in range(len(TERMS))
+        for slot in range(2)
+    ]
+    weights = Weights(*given, weight_place, weight_sems, info[1], info[2], range(STAGE_LAYERS))
+    weights.start()
+    for copy in copies:
+        copy.start()
+    masks, mean_matrix = head_masks(), head_mean_matrix()
+    times[...] = multiplicities(info[4], tile_lists, counts, virtual)
+    run_chain(
+        hidden_in[...], grad_in[0], weights, times, masks, mean_matrix, stash, terms_qkv, terms_out, lambda layer: None
+    )
+    for copy in copies:
+        copy.wait()
+    results = Results(outs, place, out_sems)
+    second = (stash["normed"], stash["mixed"], terms_qkv, terms_out)
+    for slot in range(2):
+        weight_gradients(slot, *(both(first[i][slot], second[i][low + slot]) for i in range(len(TERMS))), place, info[2])
+        results.start(slot)
+    for slot in range(2):
+        results.wait(slot)
+
+
+def backward_kernel(info, grad_in, grad_in2, *rest):
     order = tuple(reversed(range(STAGE_LAYERS)))
     count = len(STASH)
-    outside, given, (keep, send) = rest[:count], rest[count:][:6], rest[count + 6 :][:2]
-    inside = rest[count + 8 :][:count]
-    weight_place, weight_sems, place, in_sems, out_sems = rest[-5:]
+    outside, outside2, given, outs = rest[:count], rest[count:][:count], rest[2 * count :][:6], rest[2 * count + 6 :][:2]
+    inside = rest[2 * count + 8 :]
+    weight_place, weight_sems, place, kept_qkv, kept_out, sems, sems2, out_sems = inside[2 * count :]
     weights = Weights(*given, weight_place, weight_sems, info[1], info[2], order)
-    sheets = Sheets(STASH, outside, inside, in_sems, True)
-    results = Sheets(("keep", "send"), (keep, send), (place.at[0], place.at[1]), out_sems, False)
+    sheets = [
+        Sheets(STASH, outside, inside[:count], sems, True),
+        Sheets(STASH, outside2, inside[count:][:count], sems2, True),
+    ]
+    results = Results(outs, place, out_sems)
     for layer in order:
-        sheets.start(layer)
+        for one in sheets:
+            one.start(layer)
         weights.each(layer, lambda copy: copy.start())
     masks, mean_matrix = head_masks(), head_mean_matrix()
-    grad = grad_in[...]
-    for layer in order:
-        sheets.wait(layer)
+
+    def step(layer, grads):
+        for one in sheets:
+            one.wait(layer)
         weights.wait(layer)
-        before = grad
-        grad, grad_qkv = backward_layer(layer, grad, weights.layer(layer), masks, mean_matrix, sheets.refs)
-        weight_gradients(
-            layer, sheets.refs["normed"][layer], sheets.refs["mixed"][layer], grad_qkv, before, place, info[2]
+        return tuple(
+            zip(*(backward_layer(layer, g, weights.layer(layer), masks, mean_matrix, one.refs) for g, one in zip(grads, sheets)))
         )
-        results.start(layer)
-    for layer in order:
-        results.wait(layer)
+
+    def finish(layer, grad_qkv, grad_out):
+        normed, mixed = (both(*(one.refs[n][layer] for one in sheets)) for n in ("normed", "mixed"))
+        weight_gradients(layer % 2, normed, mixed, grad_qkv, grad_out, place, info[2])
+        results.start(layer % 2)
+
+    grads = (grad_in[...], grad_in2[...])
+    for layer in (3, 2):
+        kept_out[layer - 2] = both(*grads)
+        grads, terms = step(layer, grads)
+        kept_qkv[layer - 2] = both(*terms)
+    kept_out[2] = both(*grads)
+
+    @pl.when(info[5] == 1)
+    def _():
+        for layer in (3, 2):
+            finish(layer, kept_qkv[layer - 2], kept_out[layer - 2])
+        for layer in (1, 0):
+            for one in sheets:
+                one.wait(layer)
+            weights.wait(layer)
+
+    @pl.when(info[5] == 0)
+    def _():
+        now = (kept_out[2, :ROWS], kept_out[2, ROWS:])
+        for layer in (1, 0):
+            before = both(*now)
+            now, terms = step(layer, now)
+            finish(layer, both(*terms), before)
+
+    for slot in range(2):
+        results.wait(slot)
 
 
 ANYWHERE = pl.BlockSpec(memory_space=pl.ANY)
@@ -338,12 +430,13 @@
 HIDDEN = jax.ShapeDtypeStruct((ROWS, D), BF16)
 HIDDEN_BLOCK = pl.BlockSpec((ROWS, D), lambda *_: (0, 0))
 BATCH_BLOCK = pl.BlockSpec((1, ROWS, D), lambda step, info, *_: (info[0], 0, 0))
-GRAD_HALF = jax.ShapeDtypeStruct((STAGE_LAYERS, 2, D, INNER), BF16)
+SECOND_BLOCK = pl.BlockSpec((1, ROWS, D), lambda step, info, *_: (info[4], 0, 0))
+GRAD_HALF = jax.ShapeDtypeStruct((2, 2, D, INNER), BF16)
 WEIGHT_SCRATCH = [
     pltpu.VMEM((STAGE_LAYERS, 4, D, INNER), BF16),
     pltpu.SemaphoreType.DMA((STAGE_LAYERS, 2)),
 ]
-GRAD_PLACE = pltpu.VMEM((2, STAGE_LAYERS, 2, D, INNER), BF16)
+GRAD_PLACE = pltpu.VMEM((2, 2, 2, D, INNER), BF16)
 TIMES = pltpu.VMEM((HEADS * ROWS, ROWS), F32)
 
 
@@ -355,7 +448,7 @@
     return pltpu.SemaphoreType.DMA((count, STAGE_LAYERS))
 
 
-def call(kernel, prefetched, in_specs, out_specs, out_shape, scratch, args, megabytes=20):
+def call(kernel, prefetched, in_specs, out_specs, out_shape, scratch, args, megabytes=48):
     return pl.pallas_call(
         kernel,
         grid_spec=pltpu.PrefetchScalarGridSpec(
@@ -373,7 +466,7 @@
 def run_pack(info, w_qkv, w_out):
     shapes = [jax.ShapeDtypeStruct((blocks, D, INNER), BF16) for blocks in (4, 2)]
     sems = [pltpu.SemaphoreType.DMA((2, 5))]
-    return call(pack_kernel, 1, [IN_HBM] * 2, [ANYWHERE] * 2, shapes, sems, (info, w_qkv, w_out), 60)
+    return call(pack_kernel, 1, [IN_HBM] * 2, [ANYWHERE] * 2, shapes, sems, (info, w_qkv, w_out), 1)
 
 
 def run_unpack(info, mine, other):
@@ -391,45 +484,54 @@
         [HIDDEN] + layered(STASH, jax.ShapeDtypeStruct),
         layered(STASH, pltpu.VMEM) + WEIGHT_SCRATCH + [semaphores(len(STASH)), TIMES],
         (info, *tables, nodes, *weights),
-        59,
-    )
-
-
-def run_chain(info, tables, hidden, cotangent, weights):
+        58,
+    )
+
+
+def run_middle(info, tables, hidden, cotangent, nodes, weights):
     return call(
-        chain_kernel,
+        middle_kernel,
         4,
-        [HIDDEN_BLOCK, BATCH_BLOCK] + [ANYWHERE] * 6,
-        [HIDDEN_BLOCK] + [ANYWHERE] * len(TERMS),
-        [HIDDEN] + layered(TERMS, jax.ShapeDtypeStruct),
-        layered(STASH, pltpu.VMEM) + layered(TERMS, pltpu.VMEM)[2:] + WEIGHT_SCRATCH + [semaphores(len(TERMS)), TIMES],
-        (info, *tables, hidden, cotangent, *weights),
+        [HIDDEN_BLOCK, BATCH_BLOCK, SECOND_BLOCK] + [ANYWHERE] * 6,
+        [HIDDEN_BLOCK] + [ANYWHERE] * (len(TERMS) + len(STASH)),
+        [HIDDEN] + layered(TERMS, jax.ShapeDtypeStruct) + layered(STASH, jax.ShapeDtypeStruct),
+        layered(STASH, pltpu.VMEM)
+        + layered(TERMS, pltpu.VMEM)[2:]
+        + WEIGHT_SCRATCH
+        + [semaphores(len(TERMS)), semaphores(len(STASH)), TIMES],
+        (info, *tables, hidden, cotangent, nodes, *weights),
         50,
     )
 
 
-def run_gradients(info, terms):
+def run_later(info, tables, hidden, cotangent, weights, terms):
     return call(
-        gradient_kernel,
-        1,
-        [ANYWHERE] * len(TERMS),
+        later_kernel,
+        4,
+        [HIDDEN_BLOCK, SECOND_BLOCK] + [ANYWHERE] * (6 + len(TERMS)),
         [ANYWHERE] * 2,
         [GRAD_HALF] * 2,
-        layered(TERMS, pltpu.VMEM) + [GRAD_PLACE, semaphores(len(TERMS)), semaphores(2)],
-        (info, *terms),
-    )
-
-
-def run_backward(info, grad, stash, weights):
+        layered(STASH, pltpu.VMEM)
+        + layered(TERMS, pltpu.VMEM)[2:]
+        + [pltpu.VMEM((2, *shape), kind) for shape, kind in TERMS.values()]
+        + WEIGHT_SCRATCH
+        + [GRAD_PLACE, pltpu.SemaphoreType.DMA((len(TERMS), 2)), pltpu.SemaphoreType.DMA((2, 2)), TIMES],
+        (info, *tables, hidden, cotangent, *weights, *terms),
+    )
+
+
+def run_backward(info, grads, stash, stash2, weights):
     return call(
         backward_kernel,
         1,
-        [HIDDEN_BLOCK] + [ANYWHERE] * (len(STASH) + 6),
+        [HIDDEN_BLOCK] * 2 + [ANYWHERE] * (2 * len(STASH) + 6),
         [ANYWHERE] * 2,
         [GRAD_HALF] * 2,
-        layered(STASH, pltpu.VMEM) + WEIGHT_SCRATCH + [GRAD_PLACE, semaphores(len(STASH)), semaphores(2)],
-        (info, grad, *stash, *weights),
-        20,
+        layered(STASH, pltpu.VMEM) * 2
+        + WEIGHT_SCRATCH
+        + [GRAD_PLACE, pltpu.VMEM((2, 2 * ROWS, 3 * INNER), BF16), pltpu.VMEM((3, 2 * ROWS, D), BF16)]
+        + [semaphores(len(STASH)), semaphores(len(STASH)), pltpu.SemaphoreType.DMA((2, 2))],
+        (info, *grads, *stash, *stash2, *weights),
     )
 
 
@@ -456,7 +558,7 @@
     y, x, core = lax.axis_index("yl"), lax.axis_index("xl"), lax.axis_index("core")
     me = y * 2 + x
     batch = jnp.where(stage == 0, y, 1 - y) * 2 + x
-    info = jnp.stack([batch, me, core]).astype(jnp.int32)
+    info = jnp.stack([batch, me, core, stage, batch ^ 2, y]).astype(jnp.int32)
     tables = (tile_lists.transpose(1, 2, 0), counts.transpose(1, 0), virtual)
     own, half = run_pack(info, w_qkv, w_out)
     near2 = fetched(half, 1, 0)
@@ -466,14 +568,16 @@
     weights = (own, beside, near2, far2, near3, far3)
 
     hidden, *stash = run_forward(info, tables, nodes, weights)
-    across = [(0, 3), (1, 2), (2, 1), (3, 0)]
-    hidden = lax.ppermute(hidden, ("yh", "yl"), across)
-    grad, *terms = run_chain(info, tables, hidden, cotangent, weights)
-    grad = lax.ppermute(grad, ("yh", "yl"), across)
+    pair = ("yh", "yl")
+    across, crossed = [(0, 3), (1, 2), (2, 1), (3, 0)], [(0, 2), (1, 3), (2, 0), (3, 1)]
+    first, second = lax.ppermute(hidden, pair, across), lax.ppermute(hidden, pair, crossed)
+    grad, *rest = run_middle(info, tables, first, cotangent, nodes, weights)
+    terms, stash2 = rest[: len(TERMS)], rest[len(TERMS) :]
+    grads = (lax.ppermute(grad, pair, across), lax.ppermute(grad, pair, crossed))
     keep, send = lax.cond(
         stage == 0,
-        lambda: tuple(run_backward(info, grad, stash, weights)),
-        lambda: tuple(run_gradients(info, terms)),
+        lambda: tuple(run_backward(info, grads, stash, stash2, weights)),
+        lambda: tuple(run_later(info, tables, second, cotangent, weights, terms)),
     )
 
     def added(value, axis):
@@ -485,7 +589,7 @@
     far, near = lax.axis_size("zh"), lax.axis_size("zl")
     piece = D // near
     total = (keep.astype(F32) + swapped(send, "core").astype(F32)).astype(BF16)
-    total = lax.all_to_all(total.reshape(8, D, INNER), ("yl", "xl", "xh"), 0, 0, tiled=True)
+    total = lax.all_to_all(total.reshape(4, D, INNER), ("xl", "xh"), 0, 0, tiled=True)
     total = added(total, 0).reshape(near, piece, INNER)
     total = added(lax.all_to_all(total, "zl", 0, 0, tiled=True), 0)
     total = added(lax.all_to_all(repeated(total, far), "zh", 0, 0, tiled=True), 0)

time: 206 us -> 182 us (0.88)
  Pallas kernels: 48 us -> 29.1 us
  blocking collectives: 86.8 us -> 75.1 us
  starting transfers between devices: 40.6 us -> 49.8 us
  waiting for transfers between devices: 26.2 us -> 23.8 us
  local copies, waits for them, and re-layouts: 0.08 us -> 2.26 us
    pallas_call x5, Pallas kernels: 48 us -> 29.1 us  [call(): pl.pallas_call(kernel, grid_spec=pltpu.PrefetchScalarGridSpec(num_scalar_...]
    all_to_all x1, blocking collectives: 29.4 us -> 17.5 us  [per_device(): lax.all_to_all(total.reshape(4, D, INNER), ('xl', 'xh'), 0, 0, tiled=True)]
    ppermute x2 -> x4, starting transfers between devices: 9.85 us -> 17.8 us  [the longest x1 7.98 us: per_device(): lax.ppermute(grad, pair, crossed)]
    unnamed x12 -> x18, local copies, waits for them, and re-layouts: 0.03 us -> 2.12 us
    ppermute x2 -> x4, waiting for transfers between devices: 5.94 us -> 5.29 us  [the longest x1 4.06 us: per_device(): lax.ppermute(grad, pair, across)]
  transfers between devices with their start and end apart: 9 -> 11, of which waited for: 7 -> 7; matrix products, arithmetic and copies ran while one was open for 0% -> 0% of each run, Pallas kernels for 0% -> 3%
where the time goes in v6:
time: 182 us
  blocking collectives  75.1 us (41%)
  starting transfers between devices  49.8 us (27%)
  Pallas kernels  29.1 us (16%)
  waiting for transfers between devices  23.8 us (13%)
  local copies, waits for them, and re-layouts  2.26 us (1%)
    all_to_all x1, blocking collectives, per_device(): lax.all_to_all(repeated(total, far), 'zh', 0, 0, tiled=True)  29.2 us
    pallas_call x5, Pallas kernels, call(): pl.pallas_call(kernel, grid_spec=pltpu.PrefetchScalarGridSpec(num_scalar_...  29.1 us
    ppermute x4, starting transfers between devices, swapped(): return lax.ppermute(value, axis, [(0, 1), (1, 0)])  21.7 us
    all_to_all x1, blocking collectives, per_device(): lax.all_to_all(total.reshape(4, D, INNER), ('xl', 'xh'), 0, 0, tiled=True)  17.5 us
    all_to_all x1, blocking collectives, per_device(): lax.all_to_all(repeated(total, 2 * near), ('xh', 'zl'), 0, 0, tiled=True)  16.9 us
    ppermute x3, waiting for transfers between devices, fetched(): return lax.ppermute(value, axes, pairs)  13.2 us
    all_to_all x1, blocking collectives, per_device(): total = added(lax.all_to_all(total, 'zl', 0, 0, tiled=True), 0)  11.5 us
    ppermute x3, starting transfers between devices, fetched(): return lax.ppermute(value, axes, pairs)  10.3 us
  transfers between devices with their start and end apart: 11, of which 7 were waited for; matrix products, arithmetic and copies ran while one was open for 0% of the time, Pallas kernels for 3%

profile of v6, /device:TPU:1, one launch (start us, length us, event | category | flops | bytes accessed | tf_op | source)
XLA Modules:
  0.0 181.7 jit_solution(5574334358689185400)
XLA Ops:
  0.8 1.1 copy-done.1
  1.9 0.9 copy-done.2
  2.8 0.8 shard_map.86
  3.6 6.2 %collective-permute-start.3 = (bf16[2,512,256]{2,1,0:T(8,128)(2,1)S(1)}, bf16[2,512,256]{2,1,0:T(8,128)(2,1)S(1)}, u32[]{:S(2)}, u32[]{:S(2)}) collective-permute-start(bf16[2,512,256]{2,1,0:T(8,128)(2,1)S(1)} %get-tuple-element.148), channel_id=1, source_target_pairs={{0,192},{1,195},{2,194},{3,193},{64,128},{65,131},{66,130},{67,129... | collective-permute-start | bytes 1572872 | tf_op jit(solution)/shard_map/ppermute | solution.py:553
  9.9 2.1 %collective-permute-start.1 = (bf16[2,512,256]{2,1,0:T(8,128)(2,1)S(1)}, bf16[2,512,256]{2,1,0:T(8,128)(2,1)S(1)}, u32[]{:S(2)}, u32[]{:S(2)}) collective-permute-start(bf16[2,512,256]{2,1,0:T(8,128)(2,1)S(1)} %get-tuple-element.148), channel_id=1, source_target_pairs={{0,128},{1,129},{2,130},{3,131},{64,192},{65,193},{66,194},{67,195... | collective-permute-start | bytes 1572872 | tf_op jit(solution)/shard_map/ppermute | solution.py:553
  11.9 2.0 %collective-permute-start = (bf16[4,512,256]{2,1,0:T(8,128)(2,1)S(1)}, bf16[4,512,256]{2,1,0:T(8,128)(2,1)S(1)}, u32[]{:S(2)}, u32[]{:S(2)}) collective-permute-start(bf16[4,512,256]{2,1,0:T(8,128)(2,1)S(1)} %get-tuple-element.147.rest_0_), channel_id=1, source_target_pairs={{0,64},{1,67},{2,66},{3,65},{64,0},{65,3},{66,2},{67,1},{128,192},... | collective-permute-start | bytes 3145736 | tf_op jit(solution)/shard_map/ppermute | solution.py:553
  14.0 4.5 %collective-permute-done.3.rest_4_ = bf16[2,512,256]{2,1,0:T(8,128)(2,1)S(1)} collective-permute-done((bf16[2,512,256]{2,1,0:T(8,128)(2,1)S(1)}, bf16[2,512,256]{2,1,0:T(8,128)(2,1)S(1)}, u32[]{:S(2)}, u32[]{:S(2)}) %collective-permute-start.3) | collective-permute-done | bytes 524320 | tf_op jit(solution)/shard_map/ppermute | solution.py:553
  18.5 6.3 %collective-permute-start.4 = (bf16[2,512,256]{2,1,0:T(8,128)(2,1)S(1)}, bf16[2,512,256]{2,1,0:T(8,128)(2,1)S(1)}, u32[]{:S(2)}, u32[]{:S(2)}) collective-permute-start(bf16[2,512,256]{2,1,0:T(8,128)(2,1)S(1)} %collective-permute-done.3.rest_4_), channel_id=1, source_target_pairs={{0,1},{1,0},{2,3},{3,2},{4,5},{5,4},{6,7},{7,6},{8,9},{9,8},{10,11... | collective-permute-start | bytes 1572872 | tf_op jit(solution)/shard_map/ppermute | solution.py:539
  24.7 8.7 %collective-permute-done.1.rest_2_ = bf16[2,512,256]{2,1,0:T(8,128)(2,1)S(1)} collective-permute-done((bf16[2,512,256]{2,1,0:T(8,128)(2,1)S(1)}, bf16[2,512,256]{2,1,0:T(8,128)(2,1)S(1)}, u32[]{:S(2)}, u32[]{:S(2)}) %collective-permute-start.1) | collective-permute-done | bytes 524320 | tf_op jit(solution)/shard_map/ppermute | solution.py:553
  33.5 2.4 %collective-permute-start.2 = (bf16[2,512,256]{2,1,0:T(8,128)(2,1)S(1)}, bf16[2,512,256]{2,1,0:T(8,128)(2,1)S(1)}, u32[]{:S(2)}, u32[]{:S(2)}) collective-permute-start(bf16[2,512,256]{2,1,0:T(8,128)(2,1)S(1)} %collective-permute-done.1.rest_2_), channel_id=1, source_target_pairs={{0,1},{1,0},{2,3},{3,2},{4,5},{5,4},{6,7},{7,6},{8,9},{9,8},{10,11... | collective-permute-start | bytes 1572872 | tf_op jit(solution)/shard_map/ppermute | solution.py:539
  35.9 1.5 collective-permute-done.2.rest_3_
  37.4 7.9 %shard_map.87 = (bf16[128,512]{1,0:T(8,128)(2,1)}, bf16[4,128,512]{2,1,0:T(8,128)(2,1)}, f32[4,128,128]{2,1,0:T(8,128)S(1)}, bf16[4,3,128,256]{3,2,1,0:T(8,128)(...) custom-call(s32[6]{0:T(128)S(1)} %stack.27.info, ...), custom_call_target="tpu_custom_call" | custom-call | tf_op jit(solution)/shard_map/pallas_call | solution.py:452
  45.3 4.6 %collective-permute-start.6 = (bf16[128,512]{1,0:T(8,128)(2,1)}, bf16[128,512]{1,0:T(8,128)(2,1)S(1)}, u32[]{:S(2)}, u32[]{:S(2)}) collective-permute-start(bf16[128,512]{1,0:T(8,128)(2,1)} %get-tuple-element.149), channel_id=1, source_target_pairs={{0,384},{128,256},{256,128},{384,0},{1,385},{129,257},{257,129},{3... | collective-permute-start | bytes 393224 | tf_op jit(solution)/shard_map/ppermute | solution.py:573
  50.0 2.3 %collective-permute-start.5 = (bf16[128,512]{1,0:T(8,128)(2,1)}, bf16[128,512]{1,0:T(8,128)(2,1)}, u32[]{:S(2)}, u32[]{:S(2)}) collective-permute-start(bf16[128,512]{1,0:T(8,128)(2,1)} %get-tuple-element.149), channel_id=1, source_target_pairs={{0,256},{128,384},{256,0},{384,128},{1,257},{129,385},{257,1},{385... | collective-permute-start | bytes 393224 | tf_op jit(solution)/shard_map/ppermute | solution.py:573
  52.2 1.2 collective-permute-done.6.hidden_in
  53.5 6.1 %shard_map.88 = (bf16[128,512]{1,0:T(8,128)(2,1)S(1)}, bf16[4,128,512]{2,1,0:T(8,128)(2,1)}, bf16[4,128,256]{2,1,0:T(8,128)(2,1)}, bf16[4,128,768]{2,1,0:T(8,128...) custom-call(s32[6]{0:T(128)S(1)} %stack.27.info, ...), custom_call_target="tpu_custom_call" | custom-call | tf_op jit(solution)/shard_map/pallas_call | solution.py:452
  59.5 8.0 %collective-permute-start.8 = (bf16[128,512]{1,0:T(8,128)(2,1)S(1)}, bf16[128,512]{1,0:T(8,128)(2,1)}, u32[]{:S(2)}, u32[]{:S(2)}) collective-permute-start(bf16[128,512]{1,0:T(8,128)(2,1)S(1)} %get-tuple-element.154), channel_id=1, source_target_pairs={{0,256},{128,384},{256,0},{384,128},{1,257},{129,385},{257,1},{385... | collective-permute-start | bytes 393224 | tf_op jit(solution)/shard_map/ppermute | solution.py:576
  67.5 2.9 %collective-permute-start.7 = (bf16[128,512]{1,0:T(8,128)(2,1)S(1)}, bf16[128,512]{1,0:T(8,128)(2,1)}, u32[]{:S(2)}, u32[]{:S(2)}) collective-permute-start(bf16[128,512]{1,0:T(8,128)(2,1)S(1)} %get-tuple-element.154), channel_id=1, source_target_pairs={{0,384},{128,256},{256,128},{384,0},{1,385},{129,257},{257,129},{3... | collective-permute-start | bytes 393224 | tf_op jit(solution)/shard_map/ppermute | solution.py:576
  70.5 4.1 %collective-permute-done.7 = bf16[128,512]{1,0:T(8,128)(2,1)} collective-permute-done((bf16[128,512]{1,0:T(8,128)(2,1)S(1)}, bf16[128,512]{1,0:T(8,128)(2,1)}, u32[]{:S(2)}, u32[]{:S(2)}) %collective-permute-start.7) | collective-permute-done | bytes 131104 | tf_op jit(solution)/shard_map/ppermute | solution.py:576
  74.5 12.8 %conditional.2 = (bf16[2,2,512,256]{3,2,1,0:T(8,128)(2,1)S(1)}, bf16[2,2,512,256]{3,2,1,0:T(8,128)(2,1)S(1)}) conditional(s32[]{:T(128)} %convert_element_type.21, (s32[6]{0:T(128)S(1)}, s32[2,2,4]{2,1,0:T(2,128)S(1)}, s32[2,4]{1,0:T(2,128)S(1)}, s32[4]{0:T(128)S(1)}, bf16[128,512]{1,0:T(8,128)(2,1)}, /*index=5*/bf16[4,128,512]{2,1,0:T(8,128)(2,1)}, ...), branch_computations={%region_0.1_spmd, %region_1.2_spmd} | conditional | bytes 16
  74.5 12.8 %branch_1_fun.1 = (bf16[2,2,512,256]{3,2,1,0:T(8,128)(2,1)S(1)}, bf16[2,2,512,256]{3,2,1,0:T(8,128)(2,1)S(1)}) custom-call(s32[6]{0:T(128)S(1)} %get-tuple-element.100.info, bf16[128,512]{1,0:T(8,128)(2,1)} %get-tuple-element.101.grad_in, bf16[128,512]{1,0:T(8,128)(2,1)} %get-tuple-element.102.grad_in2, bf16[4,128,512]{2,1,0:T(8,128)(2,1)} %get-tuple-element.103.rest_0_, ...), custom_call_target="tpu_custom_call" | custom-call | tf_op jit(solution)/shard_map/cond/branch_1_fun/pallas_call | solution.py:452
  87.4 5.2 %collective-permute-start.9 = (bf16[2,2,512,256]{3,2,1,0:T(8,128)(2,1)S(1)}, bf16[2,2,512,256]{3,2,1,0:T(8,128)(2,1)S(1)}, u32[]{:S(2)}, u32[]{:S(2)}) collective-permute-start(bf16[2,2,512,256]{3,2,1,0:T(8,128)(2,1)S(1)} %get-tuple-element.168), channel_id=1, source_target_pairs={{0,1},{1,0},{2,3},{3,2},{4,5},{5,4},{6,7},{7,6},{8,9},{9,8},{10,11... | collective-permute-start | bytes 3145736 | tf_op jit(solution)/shard_map/ppermute | solution.py:539
  92.5 2.3 %collective-permute-done.9 = bf16[2,2,512,256]{3,2,1,0:T(8,128)(2,1)S(1)} collective-permute-done((bf16[2,2,512,256]{3,2,1,0:T(8,128)(2,1)S(1)}, bf16[2,2,512,256]{3,2,1,0:T(8,128)(2,1)S(1)}, u32[]{:S(2)}, u32[]{:S(2)}) %collective-permute-start.9) | collective-permute-done | bytes 1048608 | tf_op jit(solution)/shard_map/ppermute | solution.py:539
  94.8 0.3 add_convert_fusion
  95.1 17.5 %all_to_all.20 = bf16[4,512,256]{2,1,0:T(8,128)(2,1)S(1)} all-to-all(bf16[4,512,256]{2,1,0:T(8,128)(2,1)S(1)} %bitcast.13), channel_id=1, replica_groups=mesh['yh'=2,'yl'=2,'xl'=2,'zh'=4,'zl'=4,'xh'=2,'core'=2] {'xl','xh'}, dimensions={0} | all-to-all | bytes 2097152 | tf_op jit(solution)/shard_map/all_to_all | solution.py:592
  112.6 0.3 reduce_sum.36
  112.9 11.5 %all_to_all.21 = bf16[4,128,256]{2,1,0:T(8,128)(2,1)S(1)} all-to-all(bf16[4,128,256]{2,1,0:T(8,128)(2,1)S(1)} %bitcast.14), channel_id=1, replica_groups=mesh['yh'=2,'yl'=2,'xl'=2,'zh'=4,'zl'=4,'xh'=2,'core'=2] {'zl'}, dimensions={0} | all-to-all | bytes 524288 | tf_op jit(solution)/shard_map/all_to_all | solution.py:594
  124.4 29.2 %all_to_all.22 = bf16[4,128,256]{2,1,0:T(8,128)(2,1)S(1)} all-to-all(bf16[4,128,256]{2,1,0:T(8,128)(2,1)S(1)} %broadcast_in_dim.6), channel_id=1, replica_groups=mesh['yh'=2,'yl'=2,'xl'=2,'zh'=4,'zl'=4,'xh'=2,'core'=2] {'zh'}, dimensions={0} | all-to-all | bytes 524288 | tf_op jit(solution)/shard_map/all_to_all | solution.py:595
  153.7 16.9 %all_to_all.23 = bf16[8,128,256]{2,1,0:T(8,128)(2,1)S(1)} all-to-all(bf16[8,128,256]{2,1,0:T(8,128)(2,1)S(1)} %broadcast_in_dim.7), channel_id=1, replica_groups=mesh['yh'=2,'yl'=2,'xl'=2,'zh'=4,'zl'=4,'xh'=2,'core'=2] {'xh','zl'}, dimensions={0} | all-to-all | bytes 1048576 | tf_op jit(solution)/shard_map/all_to_all | solution.py:596
  170.6 7.9 %collective-permute-start.10 = (bf16[2,512,256]{2,1,0:T(8,128)(2,1)S(1)}, bf16[2,512,256]{2,1,0:T(8,128)(2,1)S(1)}, u32[]{:S(2)}, u32[]{:S(2)}) collective-permute-start(bf16[2,512,256]{2,1,0:T(8,128)(2,1)S(1)} %bitcast.11), channel_id=1, source_target_pairs={{0,1},{1,0},{2,3},{3,2},{4,5},{5,4},{6,7},{7,6},{8,9},{9,8},{10,11... | collective-permute-start | bytes 1572872 | tf_op jit(solution)/shard_map/ppermute | solution.py:539
  178.5 1.5 collective-permute-done.10.other
  180.0 1.6 shard_map.89
  (25 shorter events, 0.3 us)
Async XLA Ops:
  0.6 36.8 %copy-start.8 = (s32[4]{0:T(128)S(1)}, s32[4]{0:T(128)}, u32[]{:S(2)}) copy-start(s32[4]{0:T(128)} %virtual.3) | copy-start | bytes 52
  0.6 36.7 %copy-start.7 = (s32[4,2]{0,1:T(2,128)S(1)}, s32[4,2]{0,1:T(2,128)}, u32[]{:S(2)}) copy-start(s32[4,2]{0,1:T(2,128)} %param.14) | copy-start | bytes 100
  0.7 36.7 %copy-start.6 = (s32[4,2,2]{0,2,1:T(2,128)S(1)}, s32[4,2,2]{0,2,1:T(2,128)}, u32[]{:S(2)}) copy-start(s32[4,2,2]{0,2,1:T(2,128)} %param.13) | copy-start | bytes 196
  0.8 1.1 copy-start.1
  1.9 0.9 copy-start.2
  3.6 14.8 %collective-permute-start.3 = (bf16[2,512,256]{2,1,0:T(8,128)(2,1)S(1)}, bf16[2,512,256]{2,1,0:T(8,128)(2,1)S(1)}, u32[]{:S(2)}, u32[]{:S(2)}) collective-permute-start(bf16[2,512,256]{2,1,0:T(8,128)(2,1)S(1)} %get-tuple-element.148), channel_id=1, source_target_pairs={{0,192},{1,195},{2,194},{3,193},{64,128},{65,131},{66,130},{67,129... | collective-permute-start | bytes 1572872 | tf_op jit(solution)/shard_map/ppermute | solution.py:553
  9.9 23.6 %collective-permute-start.1 = (bf16[2,512,256]{2,1,0:T(8,128)(2,1)S(1)}, bf16[2,512,256]{2,1,0:T(8,128)(2,1)S(1)}, u32[]{:S(2)}, u32[]{:S(2)}) collective-permute-start(bf16[2,512,256]{2,1,0:T(8,128)(2,1)S(1)} %get-tuple-element.148), channel_id=1, source_target_pairs={{0,128},{1,129},{2,130},{3,131},{64,192},{65,193},{66,194},{67,195... | collective-permute-start | bytes 1572872 | tf_op jit(solution)/shard_map/ppermute | solution.py:553
  11.9 25.4 %collective-permute-start = (bf16[4,512,256]{2,1,0:T(8,128)(2,1)S(1)}, bf16[4,512,256]{2,1,0:T(8,128)(2,1)S(1)}, u32[]{:S(2)}, u32[]{:S(2)}) collective-permute-start(bf16[4,512,256]{2,1,0:T(8,128)(2,1)S(1)} %get-tuple-element.147.rest_0_), channel_id=1, source_target_pairs={{0,64},{1,67},{2,66},{3,65},{64,0},{65,3},{66,2},{67,1},{128,192},... | collective-permute-start | bytes 3145736 | tf_op jit(solution)/shard_map/ppermute | solution.py:553
  18.5 17.4 %collective-permute-start.4 = (bf16[2,512,256]{2,1,0:T(8,128)(2,1)S(1)}, bf16[2,512,256]{2,1,0:T(8,128)(2,1)S(1)}, u32[]{:S(2)}, u32[]{:S(2)}) collective-permute-start(bf16[2,512,256]{2,1,0:T(8,128)(2,1)S(1)} %collective-permute-done.3.rest_4_), channel_id=1, source_target_pairs={{0,1},{1,0},{2,3},{3,2},{4,5},{5,4},{6,7},{7,6},{8,9},{9,8},{10,11... | collective-permute-start | bytes 1572872 | tf_op jit(solution)/shard_map/ppermute | solution.py:539
  33.5 3.9 %collective-permute-start.2 = (bf16[2,512,256]{2,1,0:T(8,128)(2,1)S(1)}, bf16[2,512,256]{2,1,0:T(8,128)(2,1)S(1)}, u32[]{:S(2)}, u32[]{:S(2)}) collective-permute-start(bf16[2,512,256]{2,1,0:T(8,128)(2,1)S(1)} %collective-permute-done.1.rest_2_), channel_id=1, source_target_pairs={{0,1},{1,0},{2,3},{3,2},{4,5},{5,4},{6,7},{7,6},{8,9},{9,8},{10,11... | collective-permute-start | bytes 1572872 | tf_op jit(solution)/shard_map/ppermute | solution.py:539
  35.9 17.6 %copy-start.3 = (bf16[2,512,256]{2,1,0:T(8,128)(2,1)}, bf16[2,512,256]{2,1,0:T(8,128)(2,1)S(1)}, u32[]{:S(2)}) copy-start(bf16[2,512,256]{2,1,0:T(8,128)(2,1)S(1)} %collective-permute-done.4.rest_5_) | copy-start | bytes 1572868
  37.4 16.1 %copy-start.4 = (bf16[2,512,256]{2,1,0:T(8,128)(2,1)}, bf16[2,512,256]{2,1,0:T(8,128)(2,1)S(1)}, u32[]{:S(2)}) copy-start(bf16[2,512,256]{2,1,0:T(8,128)(2,1)S(1)} %collective-permute-done.2.rest_3_) | copy-start | bytes 1572868
  37.4 16.1 %copy-start = (bf16[4,128,512]{2,1,0:T(8,128)(2,1)S(1)}, bf16[4,128,512]{2,1,0:T(8,128)(2,1)}, u32[]{:S(2)}) copy-start(bf16[4,128,512]{2,1,0:T(8,128)(2,1)} %nodes_in.1) | copy-start | bytes 1572868
  37.4 16.0 %copy-start.5 = (bf16[4,128,512]{2,1,0:T(8,128)(2,1)S(1)}, bf16[4,128,512]{2,1,0:T(8,128)(2,1)}, u32[]{:S(2)}) copy-start(bf16[4,128,512]{2,1,0:T(8,128)(2,1)} %grad_in.1) | copy-start | bytes 1572868
  45.3 8.1 %collective-permute-start.6 = (bf16[128,512]{1,0:T(8,128)(2,1)}, bf16[128,512]{1,0:T(8,128)(2,1)S(1)}, u32[]{:S(2)}, u32[]{:S(2)}) collective-permute-start(bf16[128,512]{1,0:T(8,128)(2,1)} %get-tuple-element.149), channel_id=1, source_target_pairs={{0,384},{128,256},{256,128},{384,0},{1,385},{129,257},{257,129},{3... | collective-permute-start | bytes 393224 | tf_op jit(solution)/shard_map/ppermute | solution.py:573
  50.0 20.5 %collective-permute-start.5 = (bf16[128,512]{1,0:T(8,128)(2,1)}, bf16[128,512]{1,0:T(8,128)(2,1)}, u32[]{:S(2)}, u32[]{:S(2)}) collective-permute-start(bf16[128,512]{1,0:T(8,128)(2,1)} %get-tuple-element.149), channel_id=1, source_target_pairs={{0,256},{128,384},{256,0},{384,128},{1,257},{129,385},{257,1},{385... | collective-permute-start | bytes 393224 | tf_op jit(solution)/shard_map/ppermute | solution.py:573
  59.5 10.9 %collective-permute-start.8 = (bf16[128,512]{1,0:T(8,128)(2,1)S(1)}, bf16[128,512]{1,0:T(8,128)(2,1)}, u32[]{:S(2)}, u32[]{:S(2)}) collective-permute-start(bf16[128,512]{1,0:T(8,128)(2,1)S(1)} %get-tuple-element.154), channel_id=1, source_target_pairs={{0,256},{128,384},{256,0},{384,128},{1,257},{129,385},{257,1},{385... | collective-permute-start | bytes 393224 | tf_op jit(solution)/shard_map/ppermute | solution.py:576
  67.5 7.0 %collective-permute-start.7 = (bf16[128,512]{1,0:T(8,128)(2,1)S(1)}, bf16[128,512]{1,0:T(8,128)(2,1)}, u32[]{:S(2)}, u32[]{:S(2)}) collective-permute-start(bf16[128,512]{1,0:T(8,128)(2,1)S(1)} %get-tuple-element.154), channel_id=1, source_target_pairs={{0,384},{128,256},{256,128},{384,0},{1,385},{129,257},{257,129},{3... | collective-permute-start | bytes 393224 | tf_op jit(solution)/shard_map/ppermute | solution.py:576
  87.4 7.4 %collective-permute-start.9 = (bf16[2,2,512,256]{3,2,1,0:T(8,128)(2,1)S(1)}, bf16[2,2,512,256]{3,2,1,0:T(8,128)(2,1)S(1)}, u32[]{:S(2)}, u32[]{:S(2)}) collective-permute-start(bf16[2,2,512,256]{3,2,1,0:T(8,128)(2,1)S(1)} %get-tuple-element.168), channel_id=1, source_target_pairs={{0,1},{1,0},{2,3},{3,2},{4,5},{5,4},{6,7},{7,6},{8,9},{9,8},{10,11... | collective-permute-start | bytes 3145736 | tf_op jit(solution)/shard_map/ppermute | solution.py:539
  170.6 9.4 %collective-permute-start.10 = (bf16[2,512,256]{2,1,0:T(8,128)(2,1)S(1)}, bf16[2,512,256]{2,1,0:T(8,128)(2,1)S(1)}, u32[]{:S(2)}, u32[]{:S(2)}) collective-permute-start(bf16[2,512,256]{2,1,0:T(8,128)(2,1)S(1)} %bitcast.11), channel_id=1, source_target_pairs={{0,1},{1,0},{2,3},{3,2},{4,5},{5,4},{6,7},{7,6},{8,9},{9,8},{10,11... | collective-permute-start | bytes 1572872 | tf_op jit(solution)/shard_map/ppermute | solution.py:539

commit v7 on v6

--- a/solution.py
+++ b/solution.py
@@ -302,7 +302,7 @@
     return grad
 
 
-def middle_kernel(info, tile_lists, counts, virtual, hidden_in, grad_in, nodes_in, *rest):
+def middle_kernel(info, tile_lists, counts, virtual, hidden_in, sent, grad_in, nodes_in, *rest):
     given, grad_out, rest = rest[:6], rest[6], rest[7:]
     terms_outside, stash_outside, inside = rest[: len(TERMS)], rest[len(TERMS) :][: len(STASH)], rest[len(TERMS) + len(STASH) :]
     stash_inside, (terms_qkv, terms_out) = inside[: len(STASH)], inside[len(STASH) :][:2]
@@ -326,6 +326,7 @@
     def _():
         times[...] = multiplicities(info[4], tile_lists, counts, virtual)
         sheets = Sheets(STASH, stash_outside, stash_inside, stash_sems, False)
+        grad_out[...] = sent[...]
         hidden = nodes_in[0]
         for layer in range(STAGE_LAYERS):
             weights.wait(layer)
@@ -488,18 +489,18 @@
     )
 
 
-def run_middle(info, tables, hidden, cotangent, nodes, weights):
+def run_middle(info, tables, hidden, sent, cotangent, nodes, weights):
     return call(
         middle_kernel,
         4,
-        [HIDDEN_BLOCK, BATCH_BLOCK, SECOND_BLOCK] + [ANYWHERE] * 6,
+        [HIDDEN_BLOCK, HIDDEN_BLOCK, BATCH_BLOCK, SECOND_BLOCK] + [ANYWHERE] * 6,
         [HIDDEN_BLOCK] + [ANYWHERE] * (len(TERMS) + len(STASH)),
         [HIDDEN] + layered(TERMS, jax.ShapeDtypeStruct) + layered(STASH, jax.ShapeDtypeStruct),
         layered(STASH, pltpu.VMEM)
         + layered(TERMS, pltpu.VMEM)[2:]
         + WEIGHT_SCRATCH
         + [semaphores(len(TERMS)), semaphores(len(STASH)), TIMES],
-        (info, *tables, hidden, cotangent, nodes, *weights),
+        (info, *tables, hidden, sent, cotangent, nodes, *weights),
         50,
     )
 
@@ -570,14 +571,14 @@
     hidden, *stash = run_forward(info, tables, nodes, weights)
     pair = ("yh", "yl")
     across, crossed = [(0, 3), (1, 2), (2, 1), (3, 0)], [(0, 2), (1, 3), (2, 0), (3, 1)]
-    first, second = lax.ppermute(hidden, pair, across), lax.ppermute(hidden, pair, crossed)
-    grad, *rest = run_middle(info, tables, first, cotangent, nodes, weights)
+    received = lax.ppermute(hidden, pair, across)
+    grad, *rest = run_middle(info, tables, received, hidden, cotangent, nodes, weights)
     terms, stash2 = rest[: len(TERMS)], rest[len(TERMS) :]
     grads = (lax.ppermute(grad, pair, across), lax.ppermute(grad, pair, crossed))
     keep, send = lax.cond(
         stage == 0,
         lambda: tuple(run_backward(info, grads, stash, stash2, weights)),
-        lambda: tuple(run_later(info, tables, second, cotangent, weights, terms)),
+        lambda: tuple(run_later(info, tables, grads[1], cotangent, weights, terms)),
     )
 
     def added(value, axis):
@@ -586,14 +587,13 @@
     def repeated(value, times):
         return jnp.broadcast_to(value, (times, *value.shape))
 
-    far, near = lax.axis_size("zh"), lax.axis_size("zl")
-    piece = D // near
+    far, pairs, near = (lax.axis_size(axis) for axis in ("zh", "za", "zb"))
     total = (keep.astype(F32) + swapped(send, "core").astype(F32)).astype(BF16)
-    total = lax.all_to_all(total.reshape(4, D, INNER), ("xl", "xh"), 0, 0, tiled=True)
-    total = added(total, 0).reshape(near, piece, INNER)
-    total = added(lax.all_to_all(total, "zl", 0, 0, tiled=True), 0)
+    total = lax.all_to_all(total.reshape(4 * near, D // near, INNER), ("xl", "xh", "zb"), 0, 0, tiled=True)
+    total = added(total.reshape(4 * near, D // near, INNER), 0).reshape(pairs, D // (near * pairs), INNER)
+    total = added(lax.all_to_all(total, "za", 0, 0, tiled=True), 0)
     total = added(lax.all_to_all(repeated(total, far), "zh", 0, 0, tiled=True), 0)
-    total = lax.all_to_all(repeated(total, 2 * near), ("xh", "zl"), 0, 0, tiled=True)
+    total = lax.all_to_all(repeated(total, 2 * near * pairs), ("xh", "zb", "za"), 0, 0, tiled=True)
     mine = total.reshape(2, D, INNER)
     grad_qkv, grad_out = run_unpack(info, mine, swapped(mine, "core"))
     return (grad_qkv, grad_out)
@@ -601,10 +601,12 @@
 
 def solution(mesh):
     depth = mesh.shape["dp"] // 4
-    near = min(depth, 4)
-    names = ("yh", "yl", "xl", "zh", "zl", "xh", "core")
-    cut = Mesh(mesh.devices.reshape(2, 2, 2, depth // near, near, 2, 2), names)
-    section, dp = P(("yh", "yl", "xl")), P(("zh", "zl", "xh", "core"))
+    near = min(depth, 2)
+    pairs = min(depth // near, 2)
+    far = depth // (near * pairs)
+    names = ("yh", "yl", "xl", "zh", "za", "zb", "xh", "core")
+    cut = Mesh(mesh.devices.reshape(2, 2, 2, far, pairs, near, 2, 2), names)
+    section, dp = P(("yh", "yl", "xl")), P(("zh", "za", "zb", "xh", "core"))
     return jax.shard_map(
         per_device,
         mesh=cut,

time: 182 us -> 178 us (0.978)
  starting transfers between devices: 49.8 us -> 46.1 us
  waiting for transfers between devices: 23.8 us -> 26.4 us
  blocking collectives: 75.1 us -> 72.5 us
    ppermute x2 -> x1, waiting for transfers between devices: 1.23 us -> 3.49 us  [per_device(): received = lax.ppermute(hidden, pair, across)]
    ppermute x2 -> x1, starting transfers between devices: 6.88 us -> 4.62 us  [per_device(): received = lax.ppermute(hidden, pair, across)]
  transfers between devices with their start and end apart: 11 -> 10, of which waited for: 7 -> 7; matrix products, arithmetic and copies ran while one was open for 0% -> 0% of each run, Pallas kernels for 3% -> 0%
where the time goes in v7:
time: 178 us; the launch traced here: 177 us
  blocking collectives  72.5 us (41%)
  starting transfers between devices  46.1 us (26%)
  Pallas kernels  27.5 us (15%)
  waiting for transfers between devices  26.4 us (15%)
  local copies, waits for them, and re-layouts  3.15 us (2%)
    all_to_all x1, blocking collectives, per_device(): lax.all_to_all(repeated(total, far), 'zh', 0, 0, tiled=True)  27.9 us
    pallas_call x5, Pallas kernels, call(): pl.pallas_call(kernel, grid_spec=pltpu.PrefetchScalarGridSpec(num_scalar_...  27.5 us
    ppermute x4, starting transfers between devices, swapped(): return lax.ppermute(value, axis, [(0, 1), (1, 0)])  20.3 us
    all_to_all x1, blocking collectives, per_device(): lax.all_to_all(total.reshape(4 * near, D // near, INNER), ('xl', 'xh', 'z...  19.8 us
    all_to_all x1, blocking collectives, per_device(): lax.all_to_all(repeated(total, 2 * near * pairs), ('xh', 'zb', 'za'), 0,...  15.8 us
    ppermute x3, waiting for transfers between devices, fetched(): return lax.ppermute(value, axes, pairs)  13.2 us
    ppermute x3, starting transfers between devices, fetched(): return lax.ppermute(value, axes, pairs)  10.3 us
    all_to_all x1, blocking collectives, per_device(): total = added(lax.all_to_all(total, 'za', 0, 0, tiled=True), 0)  8.89 us
  transfers between devices with their start and end apart: 10, of which 7 were waited for; matrix products, arithmetic and copies ran while one was open for 0% of the time, Pallas kernels for 0%

profile of v7, /device:TPU:1, one launch (start us, length us, event | category | flops | bytes accessed | tf_op | source)
XLA Modules:
  0.0 177.1 jit_solution(6342373629181340979)
XLA Ops:
  0.8 1.1 copy-done.1
  1.9 0.9 copy-done.2
  2.8 0.8 shard_map.86
  3.6 6.2 %collective-permute-start.3 = (bf16[2,512,256]{2,1,0:T(8,128)(2,1)S(1)}, bf16[2,512,256]{2,1,0:T(8,128)(2,1)S(1)}, u32[]{:S(2)}, u32[]{:S(2)}) collective-permute-start(bf16[2,512,256]{2,1,0:T(8,128)(2,1)S(1)} %get-tuple-element.148), channel_id=1, source_target_pairs={{0,192},{1,195},{2,194},{3,193},{64,128},{65,131},{66,130},{67,129... | collective-permute-start | bytes 1572872 | tf_op jit(solution)/shard_map/ppermute | solution.py:554
  9.9 2.1 %collective-permute-start.1 = (bf16[2,512,256]{2,1,0:T(8,128)(2,1)S(1)}, bf16[2,512,256]{2,1,0:T(8,128)(2,1)S(1)}, u32[]{:S(2)}, u32[]{:S(2)}) collective-permute-start(bf16[2,512,256]{2,1,0:T(8,128)(2,1)S(1)} %get-tuple-element.148), channel_id=1, source_target_pairs={{0,128},{1,129},{2,130},{3,131},{64,192},{65,193},{66,194},{67,195... | collective-permute-start | bytes 1572872 | tf_op jit(solution)/shard_map/ppermute | solution.py:554
  11.9 2.0 %collective-permute-start = (bf16[4,512,256]{2,1,0:T(8,128)(2,1)S(1)}, bf16[4,512,256]{2,1,0:T(8,128)(2,1)S(1)}, u32[]{:S(2)}, u32[]{:S(2)}) collective-permute-start(bf16[4,512,256]{2,1,0:T(8,128)(2,1)S(1)} %get-tuple-element.147.rest_0_), channel_id=1, source_target_pairs={{0,64},{1,67},{2,66},{3,65},{64,0},{65,3},{66,2},{67,1},{128,192},... | collective-permute-start | bytes 3145736 | tf_op jit(solution)/shard_map/ppermute | solution.py:554
  14.0 4.5 %collective-permute-done.3.rest_4_ = bf16[2,512,256]{2,1,0:T(8,128)(2,1)S(1)} collective-permute-done((bf16[2,512,256]{2,1,0:T(8,128)(2,1)S(1)}, bf16[2,512,256]{2,1,0:T(8,128)(2,1)S(1)}, u32[]{:S(2)}, u32[]{:S(2)}) %collective-permute-start.3) | collective-permute-done | bytes 524320 | tf_op jit(solution)/shard_map/ppermute | solution.py:554
  18.5 6.3 %collective-permute-start.4 = (bf16[2,512,256]{2,1,0:T(8,128)(2,1)S(1)}, bf16[2,512,256]{2,1,0:T(8,128)(2,1)S(1)}, u32[]{:S(2)}, u32[]{:S(2)}) collective-permute-start(bf16[2,512,256]{2,1,0:T(8,128)(2,1)S(1)} %collective-permute-done.3.rest_4_), channel_id=1, source_target_pairs={{0,1},{1,0},{2,3},{3,2},{4,5},{5,4},{6,7},{7,6},{8,9},{9,8},{10,11... | collective-permute-start | bytes 1572872 | tf_op jit(solution)/shard_map/ppermute | solution.py:540
  24.7 8.7 %collective-permute-done.1.rest_2_ = bf16[2,512,256]{2,1,0:T(8,128)(2,1)S(1)} collective-permute-done((bf16[2,512,256]{2,1,0:T(8,128)(2,1)S(1)}, bf16[2,512,256]{2,1,0:T(8,128)(2,1)S(1)}, u32[]{:S(2)}, u32[]{:S(2)}) %collective-permute-start.1) | collective-permute-done | bytes 524320 | tf_op jit(solution)/shard_map/ppermute | solution.py:554
  33.5 2.4 %collective-permute-start.2 = (bf16[2,512,256]{2,1,0:T(8,128)(2,1)S(1)}, bf16[2,512,256]{2,1,0:T(8,128)(2,1)S(1)}, u32[]{:S(2)}, u32[]{:S(2)}) collective-permute-start(bf16[2,512,256]{2,1,0:T(8,128)(2,1)S(1)} %collective-permute-done.1.rest_2_), channel_id=1, source_target_pairs={{0,1},{1,0},{2,3},{3,2},{4,5},{5,4},{6,7},{7,6},{8,9},{9,8},{10,11... | collective-permute-start | bytes 1572872 | tf_op jit(solution)/shard_map/ppermute | solution.py:540
  35.9 1.5 collective-permute-done.2.rest_3_
  37.4 7.2 %shard_map.87 = (bf16[128,512]{1,0:T(8,128)(2,1)}, bf16[4,128,512]{2,1,0:T(8,128)(2,1)}, f32[4,128,128]{2,1,0:T(8,128)}, bf16[4,3,128,256]{3,2,1,0:T(8,128)(2,1)...) custom-call(s32[6]{0:T(128)S(1)} %stack.27.info, ...), custom_call_target="tpu_custom_call" | custom-call | tf_op jit(solution)/shard_map/pallas_call | solution.py:453
  44.7 4.6 %collective-permute-start.5 = (bf16[128,512]{1,0:T(8,128)(2,1)}, bf16[128,512]{1,0:T(8,128)(2,1)S(1)}, u32[]{:S(2)}, u32[]{:S(2)}) collective-permute-start(bf16[128,512]{1,0:T(8,128)(2,1)} %get-tuple-element.149.sent), channel_id=1, source_target_pairs={{0,384},{128,256},{256,128},{384,0},{1,385},{129,257},{257,129},{3... | collective-permute-start | bytes 393224 | tf_op jit(solution)/shard_map/ppermute | solution.py:574
  49.3 3.5 %collective-permute-done.5.hidden_in = bf16[128,512]{1,0:T(8,128)(2,1)S(1)} collective-permute-done((bf16[128,512]{1,0:T(8,128)(2,1)}, bf16[128,512]{1,0:T(8,128)(2,1)S(1)}, u32[]{:S(2)}, u32[]{:S(2)}) %collective-permute-start.5) | collective-permute-done | bytes 131104 | tf_op jit(solution)/shard_map/ppermute | solution.py:574
  52.8 0.9 copy-done.3
  53.7 6.0 %shard_map.88 = (bf16[128,512]{1,0:T(8,128)(2,1)S(1)}, bf16[4,128,512]{2,1,0:T(8,128)(2,1)}, bf16[4,128,256]{2,1,0:T(8,128)(2,1)}, bf16[4,128,768]{2,1,0:T(8,128...) custom-call(s32[6]{0:T(128)S(1)} %stack.27.info, ...), custom_call_target="tpu_custom_call" | custom-call | tf_op jit(solution)/shard_map/pallas_call | solution.py:453
  59.8 8.0 %collective-permute-start.6 = (bf16[128,512]{1,0:T(8,128)(2,1)S(1)}, bf16[128,512]{1,0:T(8,128)(2,1)S(1)}, u32[]{:S(2)}, u32[]{:S(2)}) collective-permute-start(bf16[128,512]{1,0:T(8,128)(2,1)S(1)} %get-tuple-element.150), channel_id=1, source_target_pairs={{0,256},{128,384},{256,0},{384,128},{1,257},{129,385},{257,1},{385... | collective-permute-start | bytes 393224 | tf_op jit(solution)/shard_map/ppermute | solution.py:577
  67.8 2.9 %collective-permute-start.7 = (bf16[128,512]{1,0:T(8,128)(2,1)S(1)}, bf16[128,512]{1,0:T(8,128)(2,1)S(1)}, u32[]{:S(2)}, u32[]{:S(2)}) collective-permute-start(bf16[128,512]{1,0:T(8,128)(2,1)S(1)} %get-tuple-element.150), channel_id=1, source_target_pairs={{0,384},{128,256},{256,128},{384,0},{1,385},{129,257},{257,129},{3... | collective-permute-start | bytes 393224 | tf_op jit(solution)/shard_map/ppermute | solution.py:577
  70.7 4.4 %collective-permute-done.7 = bf16[128,512]{1,0:T(8,128)(2,1)S(1)} collective-permute-done((bf16[128,512]{1,0:T(8,128)(2,1)S(1)}, bf16[128,512]{1,0:T(8,128)(2,1)S(1)}, u32[]{:S(2)}, u32[]{:S(2)}) %collective-permute-start.7) | collective-permute-done | bytes 131104 | tf_op jit(solution)/shard_map/ppermute | solution.py:577
  75.1 11.9 %conditional.2 = (bf16[2,2,512,256]{3,2,1,0:T(8,128)(2,1)S(1)}, bf16[2,2,512,256]{3,2,1,0:T(8,128)(2,1)S(1)}) conditional(s32[]{:T(128)} %convert_element_type.21, (s32[6]{0:T(128)S(1)}, s32[2,2,4]{2,1,0:T(2,128)S(1)}, s32[2,4]{1,0:T(2,128)S(1)}, s32[4]{0:T(128)S(1)}, bf16[128,512]{1,0:T(8,128)(2,1)S(1)}, /*index=5*/bf16[4,128,512]{2,1,0:T(8,128)(2,1)}, ...), branch_computations={%region_0.1_spmd, %region_1.2_spmd} | conditional | bytes 16
  75.1 11.9 %branch_1_fun.1 = (bf16[2,2,512,256]{3,2,1,0:T(8,128)(2,1)S(1)}, bf16[2,2,512,256]{3,2,1,0:T(8,128)(2,1)S(1)}) custom-call(s32[6]{0:T(128)S(1)} %get-tuple-element.100.info, bf16[128,512]{1,0:T(8,128)(2,1)S(1)} %get-tuple-element.101.grad_in, bf16[128,512]{1,0:T(8,128)(2,1)S(1)} %get-tuple-element.102.grad_in2, ...), custom_call_target="tpu_custom_call" | custom-call | tf_op jit(solution)/shard_map/cond/branch_1_fun/pallas_call | solution.py:453
  87.0 4.1 %collective-permute-start.8 = (bf16[2,2,512,256]{3,2,1,0:T(8,128)(2,1)S(1)}, bf16[2,2,512,256]{3,2,1,0:T(8,128)(2,1)S(1)}, u32[]{:S(2)}, u32[]{:S(2)}) collective-permute-start(bf16[2,2,512,256]{3,2,1,0:T(8,128)(2,1)S(1)} %get-tuple-element.168), channel_id=1, source_target_pairs={{0,1},{1,0},{2,3},{3,2},{4,5},{5,4},{6,7},{7,6},{8,9},{9,8},{10,11... | collective-permute-start | bytes 3145736 | tf_op jit(solution)/shard_map/ppermute | solution.py:540
  91.1 2.3 %collective-permute-done.8 = bf16[2,2,512,256]{3,2,1,0:T(8,128)(2,1)S(1)} collective-permute-done((bf16[2,2,512,256]{3,2,1,0:T(8,128)(2,1)S(1)}, bf16[2,2,512,256]{3,2,1,0:T(8,128)(2,1)S(1)}, u32[]{:S(2)}, u32[]{:S(2)}) %collective-permute-start.8) | collective-permute-done | bytes 1048608 | tf_op jit(solution)/shard_map/ppermute | solution.py:540
  93.4 0.3 add_convert_fusion
  93.7 19.8 %all_to_all.20 = bf16[8,256,256]{2,1,0:T(8,128)(2,1)S(1)} all-to-all(bf16[8,256,256]{2,1,0:T(8,128)(2,1)S(1)} %bitcast.13), channel_id=1, replica_groups=mesh['yh'=2,'yl'=2,'xl'=2,'zh'=4,'za'=2,'zb'=2,'xh'=2,'core'=2] {'xl','x..., dimensions={0} | all-to-all | bytes 2097152 | tf_op jit(solution)/shard_map/all_to_all | solution.py:592
  113.5 0.1 reduce_sum.36
  113.6 8.9 %all_to_all.21 = bf16[2,128,256]{2,1,0:T(8,128)(2,1)S(1)} all-to-all(bf16[2,128,256]{2,1,0:T(8,128)(2,1)S(1)} %bitcast.14), channel_id=1, replica_groups=mesh['yh'=2,'yl'=2,'xl'=2,'zh'=4,'za'=2,'zb'=2,'xh'=2,'core'=2] {'za'}, dimensions={0} | all-to-all | bytes 262144 | tf_op jit(solution)/shard_map/all_to_all | solution.py:594
  122.5 27.9 %all_to_all.22 = bf16[4,128,256]{2,1,0:T(8,128)(2,1)S(1)} all-to-all(bf16[4,128,256]{2,1,0:T(8,128)(2,1)S(1)} %broadcast_in_dim.6), channel_id=1, replica_groups=mesh['yh'=2,'yl'=2,'xl'=2,'zh'=4,'za'=2,'zb'=2,'xh'=2,'core'=2] {'zh'}, dimensions={0} | all-to-all | bytes 524288 | tf_op jit(solution)/shard_map/all_to_all | solution.py:595
  150.6 15.8 %all_to_all.23 = bf16[8,128,256]{2,1,0:T(8,128)(2,1)S(1)} all-to-all(bf16[8,128,256]{2,1,0:T(8,128)(2,1)S(1)} %broadcast_in_dim.7), channel_id=1, replica_groups=mesh['yh'=2,'yl'=2,'xl'=2,'zh'=4,'za'=2,'zb'=2,'xh'=2,'core'=2] {'xh','z..., dimensions={0} | all-to-all | bytes 1048576 | tf_op jit(solution)/shard_map/all_to_all | solution.py:596
  166.4 7.5 %collective-permute-start.9 = (bf16[2,512,256]{2,1,0:T(8,128)(2,1)S(1)}, bf16[2,512,256]{2,1,0:T(8,128)(2,1)S(1)}, u32[]{:S(2)}, u32[]{:S(2)}) collective-permute-start(bf16[2,512,256]{2,1,0:T(8,128)(2,1)S(1)} %bitcast.11), channel_id=1, source_target_pairs={{0,1},{1,0},{2,3},{3,2},{4,5},{5,4},{6,7},{7,6},{8,9},{9,8},{10,11... | collective-permute-start | bytes 1572872 | tf_op jit(solution)/shard_map/ppermute | solution.py:540
  173.9 1.5 collective-permute-done.9.other
  175.4 1.6 shard_map.89
  (25 shorter events, 0.2 us)
Async XLA Ops:
  0.6 36.8 %copy-start.9 = (s32[4]{0:T(128)S(1)}, s32[4]{0:T(128)}, u32[]{:S(2)}) copy-start(s32[4]{0:T(128)} %virtual.3) | copy-start | bytes 52
  0.6 36.7 %copy-start.8 = (s32[4,2]{0,1:T(2,128)S(1)}, s32[4,2]{0,1:T(2,128)}, u32[]{:S(2)}) copy-start(s32[4,2]{0,1:T(2,128)} %param.14) | copy-start | bytes 100
  0.7 36.7 %copy-start.7 = (s32[4,2,2]{0,2,1:T(2,128)S(1)}, s32[4,2,2]{0,2,1:T(2,128)}, u32[]{:S(2)}) copy-start(s32[4,2,2]{0,2,1:T(2,128)} %param.13) | copy-start | bytes 196
  0.8 1.1 copy-start.1
  1.9 0.9 copy-start.2
  3.6 14.8 %collective-permute-start.3 = (bf16[2,512,256]{2,1,0:T(8,128)(2,1)S(1)}, bf16[2,512,256]{2,1,0:T(8,128)(2,1)S(1)}, u32[]{:S(2)}, u32[]{:S(2)}) collective-permute-start(bf16[2,512,256]{2,1,0:T(8,128)(2,1)S(1)} %get-tuple-element.148), channel_id=1, source_target_pairs={{0,192},{1,195},{2,194},{3,193},{64,128},{65,131},{66,130},{67,129... | collective-permute-start | bytes 1572872 | tf_op jit(solution)/shard_map/ppermute | solution.py:554
  9.9 23.6 %collective-permute-start.1 = (bf16[2,512,256]{2,1,0:T(8,128)(2,1)S(1)}, bf16[2,512,256]{2,1,0:T(8,128)(2,1)S(1)}, u32[]{:S(2)}, u32[]{:S(2)}) collective-permute-start(bf16[2,512,256]{2,1,0:T(8,128)(2,1)S(1)} %get-tuple-element.148), channel_id=1, source_target_pairs={{0,128},{1,129},{2,130},{3,131},{64,192},{65,193},{66,194},{67,195... | collective-permute-start | bytes 1572872 | tf_op jit(solution)/shard_map/ppermute | solution.py:554
  11.9 25.4 %collective-permute-start = (bf16[4,512,256]{2,1,0:T(8,128)(2,1)S(1)}, bf16[4,512,256]{2,1,0:T(8,128)(2,1)S(1)}, u32[]{:S(2)}, u32[]{:S(2)}) collective-permute-start(bf16[4,512,256]{2,1,0:T(8,128)(2,1)S(1)} %get-tuple-element.147.rest_0_), channel_id=1, source_target_pairs={{0,64},{1,67},{2,66},{3,65},{64,0},{65,3},{66,2},{67,1},{128,192},... | collective-permute-start | bytes 3145736 | tf_op jit(solution)/shard_map/ppermute | solution.py:554
  18.5 17.4 %collective-permute-start.4 = (bf16[2,512,256]{2,1,0:T(8,128)(2,1)S(1)}, bf16[2,512,256]{2,1,0:T(8,128)(2,1)S(1)}, u32[]{:S(2)}, u32[]{:S(2)}) collective-permute-start(bf16[2,512,256]{2,1,0:T(8,128)(2,1)S(1)} %collective-permute-done.3.rest_4_), channel_id=1, source_target_pairs={{0,1},{1,0},{2,3},{3,2},{4,5},{5,4},{6,7},{7,6},{8,9},{9,8},{10,11... | collective-permute-start | bytes 1572872 | tf_op jit(solution)/shard_map/ppermute | solution.py:540
  33.5 3.9 %collective-permute-start.2 = (bf16[2,512,256]{2,1,0:T(8,128)(2,1)S(1)}, bf16[2,512,256]{2,1,0:T(8,128)(2,1)S(1)}, u32[]{:S(2)}, u32[]{:S(2)}) collective-permute-start(bf16[2,512,256]{2,1,0:T(8,128)(2,1)S(1)} %collective-permute-done.1.rest_2_), channel_id=1, source_target_pairs={{0,1},{1,0},{2,3},{3,2},{4,5},{5,4},{6,7},{7,6},{8,9},{9,8},{10,11... | collective-permute-start | bytes 1572872 | tf_op jit(solution)/shard_map/ppermute | solution.py:540
  35.9 16.9 %copy-start.4 = (bf16[2,512,256]{2,1,0:T(8,128)(2,1)}, bf16[2,512,256]{2,1,0:T(8,128)(2,1)S(1)}, u32[]{:S(2)}) copy-start(bf16[2,512,256]{2,1,0:T(8,128)(2,1)S(1)} %collective-permute-done.4.rest_5_) | copy-start | bytes 1572868
  37.4 15.4 %copy-start.5 = (bf16[2,512,256]{2,1,0:T(8,128)(2,1)}, bf16[2,512,256]{2,1,0:T(8,128)(2,1)S(1)}, u32[]{:S(2)}) copy-start(bf16[2,512,256]{2,1,0:T(8,128)(2,1)S(1)} %collective-permute-done.2.rest_3_) | copy-start | bytes 1572868
  37.4 15.4 %copy-start = (bf16[4,128,512]{2,1,0:T(8,128)(2,1)S(1)}, bf16[4,128,512]{2,1,0:T(8,128)(2,1)}, u32[]{:S(2)}) copy-start(bf16[4,128,512]{2,1,0:T(8,128)(2,1)} %nodes_in.1) | copy-start | bytes 1572868
  37.4 15.4 %copy-start.6 = (bf16[4,128,512]{2,1,0:T(8,128)(2,1)S(1)}, bf16[4,128,512]{2,1,0:T(8,128)(2,1)}, u32[]{:S(2)}) copy-start(bf16[4,128,512]{2,1,0:T(8,128)(2,1)} %grad_in.1) | copy-start | bytes 1572868
  44.7 8.1 %collective-permute-start.5 = (bf16[128,512]{1,0:T(8,128)(2,1)}, bf16[128,512]{1,0:T(8,128)(2,1)S(1)}, u32[]{:S(2)}, u32[]{:S(2)}) collective-permute-start(bf16[128,512]{1,0:T(8,128)(2,1)} %get-tuple-element.149.sent), channel_id=1, source_target_pairs={{0,384},{128,256},{256,128},{384,0},{1,385},{129,257},{257,129},{3... | collective-permute-start | bytes 393224 | tf_op jit(solution)/shard_map/ppermute | solution.py:574
  52.8 0.9 copy-start.3
  59.8 10.9 %collective-permute-start.6 = (bf16[128,512]{1,0:T(8,128)(2,1)S(1)}, bf16[128,512]{1,0:T(8,128)(2,1)S(1)}, u32[]{:S(2)}, u32[]{:S(2)}) collective-permute-start(bf16[128,512]{1,0:T(8,128)(2,1)S(1)} %get-tuple-element.150), channel_id=1, source_target_pairs={{0,256},{128,384},{256,0},{384,128},{1,257},{129,385},{257,1},{385... | collective-permute-start | bytes 393224 | tf_op jit(solution)/shard_map/ppermute | solution.py:577
  67.8 7.4 %collective-permute-start.7 = (bf16[128,512]{1,0:T(8,128)(2,1)S(1)}, bf16[128,512]{1,0:T(8,128)(2,1)S(1)}, u32[]{:S(2)}, u32[]{:S(2)}) collective-permute-start(bf16[128,512]{1,0:T(8,128)(2,1)S(1)} %get-tuple-element.150), channel_id=1, source_target_pairs={{0,384},{128,256},{256,128},{384,0},{1,385},{129,257},{257,129},{3... | collective-permute-start | bytes 393224 | tf_op jit(solution)/shard_map/ppermute | solution.py:577
  87.0 6.4 %collective-permute-start.8 = (bf16[2,2,512,256]{3,2,1,0:T(8,128)(2,1)S(1)}, bf16[2,2,512,256]{3,2,1,0:T(8,128)(2,1)S(1)}, u32[]{:S(2)}, u32[]{:S(2)}) collective-permute-start(bf16[2,2,512,256]{3,2,1,0:T(8,128)(2,1)S(1)} %get-tuple-element.168), channel_id=1, source_target_pairs={{0,1},{1,0},{2,3},{3,2},{4,5},{5,4},{6,7},{7,6},{8,9},{9,8},{10,11... | collective-permute-start | bytes 3145736 | tf_op jit(solution)/shard_map/ppermute | solution.py:540
  166.4 9.0 %collective-permute-start.9 = (bf16[2,512,256]{2,1,0:T(8,128)(2,1)S(1)}, bf16[2,512,256]{2,1,0:T(8,128)(2,1)S(1)}, u32[]{:S(2)}, u32[]{:S(2)}) collective-permute-start(bf16[2,512,256]{2,1,0:T(8,128)(2,1)S(1)} %bitcast.11), channel_id=1, source_target_pairs={{0,1},{1,0},{2,3},{3,2},{4,5},{5,4},{6,7},{7,6},{8,9},{9,8},{10,11... | collective-permute-start | bytes 1572872 | tf_op jit(solution)/shard_map/ppermute | solution.py:540

commit v8 on v7

--- a/solution.py
+++ b/solution.py
@@ -306,7 +306,7 @@
     given, grad_out, rest = rest[:6], rest[6], rest[7:]
     terms_outside, stash_outside, inside = rest[: len(TERMS)], rest[len(TERMS) :][: len(STASH)], rest[len(TERMS) + len(STASH) :]
     stash_inside, (terms_qkv, terms_out) = inside[: len(STASH)], inside[len(STASH) :][:2]
-    place, weight_sems, terms_sems, stash_sems, times = inside[len(STASH) + 2 :]
+    place, weight_sems, terms_sems, stash_sems, times, grad_place, grad_sem = inside[len(STASH) + 2 :]
     weights = Weights(*given, place, weight_sems, info[1], info[2], range(STAGE_LAYERS))
     stash = dict(zip(STASH, stash_inside))
     weights.start()
@@ -316,9 +316,12 @@
     def _():
         times[...] = multiplicities(info[0], tile_lists, counts, virtual)
         sheets = Sheets(TERMS, terms_outside, (stash["normed"], stash["mixed"], terms_qkv, terms_out), terms_sems, False)
-        grad_out[...] = run_chain(
+        grad_place[...] = run_chain(
             hidden_in[...], grad_in[0], weights, times, masks, mean_matrix, stash, terms_qkv, terms_out, sheets.start
         )
+        copy = pltpu.make_async_copy(grad_place, grad_out, grad_sem)
+        copy.start()
+        copy.wait()
         for layer in range(STAGE_LAYERS):
             sheets.wait(layer)
 
@@ -326,7 +329,6 @@
     def _():
         times[...] = multiplicities(info[4], tile_lists, counts, virtual)
         sheets = Sheets(STASH, stash_outside, stash_inside, stash_sems, False)
-        grad_out[...] = sent[...]
         hidden = nodes_in[0]
         for layer in range(STAGE_LAYERS):
             weights.wait(layer)
@@ -449,7 +451,7 @@
     return pltpu.SemaphoreType.DMA((count, STAGE_LAYERS))
 
 
-def call(kernel, prefetched, in_specs, out_specs, out_shape, scratch, args, megabytes=48):
+def call(kernel, prefetched, in_specs, out_specs, out_shape, scratch, args, megabytes=48, aliases=None):
     return pl.pallas_call(
         kernel,
         grid_spec=pltpu.PrefetchScalarGridSpec(
@@ -461,6 +463,7 @@
         ),
         out_shape=out_shape,
         compiler_params=pltpu.CompilerParams(vmem_limit_bytes=megabytes * 2**20),
+        input_output_aliases=aliases or {},
     )(*args)
 
 
@@ -493,15 +496,16 @@
     return call(
         middle_kernel,
         4,
-        [HIDDEN_BLOCK, HIDDEN_BLOCK, BATCH_BLOCK, SECOND_BLOCK] + [ANYWHERE] * 6,
-        [HIDDEN_BLOCK] + [ANYWHERE] * (len(TERMS) + len(STASH)),
+        [HIDDEN_BLOCK, ANYWHERE, BATCH_BLOCK, SECOND_BLOCK] + [ANYWHERE] * 6,
+        [ANYWHERE] * (1 + len(TERMS) + len(STASH)),
         [HIDDEN] + layered(TERMS, jax.ShapeDtypeStruct) + layered(STASH, jax.ShapeDtypeStruct),
         layered(STASH, pltpu.VMEM)
         + layered(TERMS, pltpu.VMEM)[2:]
         + WEIGHT_SCRATCH
-        + [semaphores(len(TERMS)), semaphores(len(STASH)), TIMES],
+        + [semaphores(len(TERMS)), semaphores(len(STASH)), TIMES, pltpu.VMEM((ROWS, D), BF16), pltpu.SemaphoreType.DMA],
         (info, *tables, hidden, sent, cotangent, nodes, *weights),
         50,
+        {5: 0},
     )
 
 
@@ -589,11 +593,11 @@
 
     far, pairs, near = (lax.axis_size(axis) for axis in ("zh", "za", "zb"))
     total = (keep.astype(F32) + swapped(send, "core").astype(F32)).astype(BF16)
-    total = lax.all_to_all(total.reshape(4 * near, D // near, INNER), ("xl", "xh", "zb"), 0, 0, tiled=True)
-    total = added(total.reshape(4 * near, D // near, INNER), 0).reshape(pairs, D // (near * pairs), INNER)
-    total = added(lax.all_to_all(total, "za", 0, 0, tiled=True), 0)
+    around = near * pairs
+    total = total.reshape(4 * around, D // around, INNER)
+    total = added(lax.all_to_all(total, ("xl", "xh", "zb", "za"), 0, 0, tiled=True), 0)
     total = added(lax.all_to_all(repeated(total, far), "zh", 0, 0, tiled=True), 0)
-    total = lax.all_to_all(repeated(total, 2 * near * pairs), ("xh", "zb", "za"), 0, 0, tiled=True)
+    total = lax.all_to_all(repeated(total, 2 * around), ("xh", "zb", "za"), 0, 0, tiled=True)
     mine = total.reshape(2, D, INNER)
     grad_qkv, grad_out = run_unpack(info, mine, swapped(mine, "core"))
     return (grad_qkv, grad_out)

time: 178 us -> 184 us (1.034)
  blocking collectives: 72.5 us -> 77.1 us
    all_to_all x3 -> x2, blocking collectives: 44.5 us -> 48.3 us  [the longest x1 33.5 us: per_device(): lax.all_to_all(total, ('xl', 'xh', 'zb', 'za'), 0, 0, tiled=True)]
where the time goes in v8:
time: 184 us; the launch traced here: 183 us
  blocking collectives  77.1 us (42%)
  starting transfers between devices  46.7 us (25%)
  Pallas kernels  29 us (16%)
  waiting for transfers between devices  26.7 us (15%)
  local copies, waits for them, and re-layouts  2.26 us (1%)
    all_to_all x1, blocking collectives, per_device(): lax.all_to_all(total, ('xl', 'xh', 'zb', 'za'), 0, 0, tiled=True)  33.5 us
    pallas_call x5, Pallas kernels, call(): pl.pallas_call(kernel, grid_spec=pltpu.PrefetchScalarGridSpec(num_scalar_...  29 us
    all_to_all x1, blocking collectives, per_device(): lax.all_to_all(repeated(total, far), 'zh', 0, 0, tiled=True)  28.8 us
    ppermute x4, starting transfers between devices, swapped(): return lax.ppermute(value, axis, [(0, 1), (1, 0)])  20.6 us
    all_to_all x1, blocking collectives, per_device(): lax.all_to_all(repeated(total, 2 * around), ('xh', 'zb', 'za'), 0, 0, til...  14.8 us
    ppermute x3, waiting for transfers between devices, fetched(): return lax.ppermute(value, axes, pairs)  13.2 us
    ppermute x3, starting transfers between devices, fetched(): return lax.ppermute(value, axes, pairs)  10.3 us
    ppermute x1, starting transfers between devices, per_device(): lax.ppermute(grad, pair, crossed)  8.16 us
  transfers between devices with their start and end apart: 10, of which 7 were waited for; matrix products, arithmetic and copies ran while one was open for 0% of the time, Pallas kernels for 0%

profile of v8, /device:TPU:1, one launch (start us, length us, event | category | flops | bytes accessed | tf_op | source)
XLA Modules:
  0.0 183.3 jit_solution(15957962599476576135)
XLA Ops:
  0.7 0.1 stack.27.info
  0.8 1.1 copy-done.1
  1.9 0.9 copy-done.2
  2.8 0.8 shard_map.86
  3.6 6.2 %collective-permute-start.3 = (bf16[2,512,256]{2,1,0:T(8,128)(2,1)S(1)}, bf16[2,512,256]{2,1,0:T(8,128)(2,1)S(1)}, u32[]{:S(2)}, u32[]{:S(2)}) collective-permute-start(bf16[2,512,256]{2,1,0:T(8,128)(2,1)S(1)} %get-tuple-element.148), channel_id=1, source_target_pairs={{0,192},{1,195},{2,194},{3,193},{64,128},{65,131},{66,130},{67,129... | collective-permute-start | bytes 1572872 | tf_op jit(solution)/shard_map/ppermute | solution.py:558
  9.9 2.1 %collective-permute-start.1 = (bf16[2,512,256]{2,1,0:T(8,128)(2,1)S(1)}, bf16[2,512,256]{2,1,0:T(8,128)(2,1)S(1)}, u32[]{:S(2)}, u32[]{:S(2)}) collective-permute-start(bf16[2,512,256]{2,1,0:T(8,128)(2,1)S(1)} %get-tuple-element.148), channel_id=1, source_target_pairs={{0,128},{1,129},{2,130},{3,131},{64,192},{65,193},{66,194},{67,195... | collective-permute-start | bytes 1572872 | tf_op jit(solution)/shard_map/ppermute | solution.py:558
  11.9 2.0 %collective-permute-start = (bf16[4,512,256]{2,1,0:T(8,128)(2,1)S(1)}, bf16[4,512,256]{2,1,0:T(8,128)(2,1)S(1)}, u32[]{:S(2)}, u32[]{:S(2)}) collective-permute-start(bf16[4,512,256]{2,1,0:T(8,128)(2,1)S(1)} %get-tuple-element.147.rest_0_), channel_id=1, source_target_pairs={{0,64},{1,67},{2,66},{3,65},{64,0},{65,3},{66,2},{67,1},{128,192},... | collective-permute-start | bytes 3145736 | tf_op jit(solution)/shard_map/ppermute | solution.py:558
  14.0 4.5 %collective-permute-done.3.rest_4_ = bf16[2,512,256]{2,1,0:T(8,128)(2,1)S(1)} collective-permute-done((bf16[2,512,256]{2,1,0:T(8,128)(2,1)S(1)}, bf16[2,512,256]{2,1,0:T(8,128)(2,1)S(1)}, u32[]{:S(2)}, u32[]{:S(2)}) %collective-permute-start.3) | collective-permute-done | bytes 524320 | tf_op jit(solution)/shard_map/ppermute | solution.py:558
  18.5 6.3 %collective-permute-start.4 = (bf16[2,512,256]{2,1,0:T(8,128)(2,1)S(1)}, bf16[2,512,256]{2,1,0:T(8,128)(2,1)S(1)}, u32[]{:S(2)}, u32[]{:S(2)}) collective-permute-start(bf16[2,512,256]{2,1,0:T(8,128)(2,1)S(1)} %collective-permute-done.3.rest_4_), channel_id=1, source_target_pairs={{0,1},{1,0},{2,3},{3,2},{4,5},{5,4},{6,7},{7,6},{8,9},{9,8},{10,11... | collective-permute-start | bytes 1572872 | tf_op jit(solution)/shard_map/ppermute | solution.py:544
  24.7 8.7 %collective-permute-done.1.rest_2_ = bf16[2,512,256]{2,1,0:T(8,128)(2,1)S(1)} collective-permute-done((bf16[2,512,256]{2,1,0:T(8,128)(2,1)S(1)}, bf16[2,512,256]{2,1,0:T(8,128)(2,1)S(1)}, u32[]{:S(2)}, u32[]{:S(2)}) %collective-permute-start.1) | collective-permute-done | bytes 524320 | tf_op jit(solution)/shard_map/ppermute | solution.py:558
  33.5 2.4 %collective-permute-start.2 = (bf16[2,512,256]{2,1,0:T(8,128)(2,1)S(1)}, bf16[2,512,256]{2,1,0:T(8,128)(2,1)S(1)}, u32[]{:S(2)}, u32[]{:S(2)}) collective-permute-start(bf16[2,512,256]{2,1,0:T(8,128)(2,1)S(1)} %collective-permute-done.1.rest_2_), channel_id=1, source_target_pairs={{0,1},{1,0},{2,3},{3,2},{4,5},{5,4},{6,7},{7,6},{8,9},{9,8},{10,11... | collective-permute-start | bytes 1572872 | tf_op jit(solution)/shard_map/ppermute | solution.py:544
  35.9 1.5 collective-permute-done.2.rest_3_
  37.4 0.0 copy-start
  37.4 7.9 %shard_map.87 = (bf16[128,512]{1,0:T(8,128)(2,1)}, bf16[4,128,512]{2,1,0:T(8,128)(2,1)}, f32[4,128,128]{2,1,0:T(8,128)S(1)}, bf16[4,3,128,256]{3,2,1,0:T(8,128)(...) custom-call(s32[6]{0:T(128)S(1)} %stack.27.info, ...), custom_call_target="tpu_custom_call" | custom-call | tf_op jit(solution)/shard_map/pallas_call | solution.py:455
  45.3 4.6 %collective-permute-start.5 = (bf16[128,512]{1,0:T(8,128)(2,1)}, bf16[128,512]{1,0:T(8,128)(2,1)S(1)}, u32[]{:S(2)}, u32[]{:S(2)}) collective-permute-start(bf16[128,512]{1,0:T(8,128)(2,1)} %get-tuple-element.149.sent), channel_id=1, source_target_pairs={{0,384},{128,256},{256,128},{384,0},{1,385},{129,257},{257,129},{3... | collective-permute-start | bytes 393224 | tf_op jit(solution)/shard_map/ppermute | solution.py:578
  50.0 3.5 %collective-permute-done.5.hidden_in = bf16[128,512]{1,0:T(8,128)(2,1)S(1)} collective-permute-done((bf16[128,512]{1,0:T(8,128)(2,1)}, bf16[128,512]{1,0:T(8,128)(2,1)S(1)}, u32[]{:S(2)}, u32[]{:S(2)}) %collective-permute-start.5) | collective-permute-done | bytes 131104 | tf_op jit(solution)/shard_map/ppermute | solution.py:578
  53.5 6.1 %shard_map.88 = (bf16[128,512]{1,0:T(8,128)(2,1)}, bf16[4,128,512]{2,1,0:T(8,128)(2,1)}, bf16[4,128,256]{2,1,0:T(8,128)(2,1)}, bf16[4,128,768]{2,1,0:T(8,128)(2,...) custom-call(s32[6]{0:T(128)S(1)} %stack.27.info, ...), custom_call_target="tpu_custom_call", output_to_operand_aliasing={{0}: (5, {})} | custom-call | tf_op jit(solution)/shard_map/pallas_call | solution.py:455
  59.5 8.2 %collective-permute-start.6 = (bf16[128,512]{1,0:T(8,128)(2,1)}, bf16[128,512]{1,0:T(8,128)(2,1)S(1)}, u32[]{:S(2)}, u32[]{:S(2)}) collective-permute-start(bf16[128,512]{1,0:T(8,128)(2,1)} %get-tuple-element.150), channel_id=1, source_target_pairs={{0,256},{128,384},{256,0},{384,128},{1,257},{129,385},{257,1},{385... | collective-permute-start | bytes 393224 | tf_op jit(solution)/shard_map/ppermute | solution.py:581
  67.7 2.9 %collective-permute-start.7 = (bf16[128,512]{1,0:T(8,128)(2,1)}, bf16[128,512]{1,0:T(8,128)(2,1)}, u32[]{:S(2)}, u32[]{:S(2)}) collective-permute-start(bf16[128,512]{1,0:T(8,128)(2,1)} %get-tuple-element.150), channel_id=1, source_target_pairs={{0,384},{128,256},{256,128},{384,0},{1,385},{129,257},{257,129},{3... | collective-permute-start | bytes 393224 | tf_op jit(solution)/shard_map/ppermute | solution.py:581
  70.7 4.7 %collective-permute-done.7 = bf16[128,512]{1,0:T(8,128)(2,1)} collective-permute-done((bf16[128,512]{1,0:T(8,128)(2,1)}, bf16[128,512]{1,0:T(8,128)(2,1)}, u32[]{:S(2)}, u32[]{:S(2)}) %collective-permute-start.7) | collective-permute-done | bytes 131104 | tf_op jit(solution)/shard_map/ppermute | solution.py:581
  75.4 12.7 %conditional.2 = (bf16[2,2,512,256]{3,2,1,0:T(8,128)(2,1)S(1)}, bf16[2,2,512,256]{3,2,1,0:T(8,128)(2,1)S(1)}) conditional(s32[]{:T(128)} %convert_element_type.19, (s32[6]{0:T(128)S(1)}, s32[2,2,4]{2,1,0:T(2,128)S(1)}, s32[2,4]{1,0:T(2,128)S(1)}, s32[4]{0:T(128)S(1)}, bf16[128,512]{1,0:T(8,128)(2,1)S(1)}, /*index=5*/bf16[4,128,512]{2,1,0:T(8,128)(2,1)}, ...), branch_computations={%region_0.1_spmd, %region_1.2_spmd} | conditional | bytes 16
  75.4 12.7 %branch_1_fun.1 = (bf16[2,2,512,256]{3,2,1,0:T(8,128)(2,1)S(1)}, bf16[2,2,512,256]{3,2,1,0:T(8,128)(2,1)S(1)}) custom-call(s32[6]{0:T(128)S(1)} %get-tuple-element.100.info, bf16[128,512]{1,0:T(8,128)(2,1)} %get-tuple-element.101.grad_in, bf16[128,512]{1,0:T(8,128)(2,1)S(1)} %get-tuple-element.102.grad_in2, bf16[4,128,512]{2,1,0:T(8,128)(2,1)} %get-tuple-element.103.rest_0_, ...), custom_call_target="tpu_custom_call" | custom-call | tf_op jit(solution)/shard_map/cond/branch_1_fun/pallas_call | solution.py:455
  88.2 4.1 %collective-permute-start.8 = (bf16[2,2,512,256]{3,2,1,0:T(8,128)(2,1)S(1)}, bf16[2,2,512,256]{3,2,1,0:T(8,128)(2,1)S(1)}, u32[]{:S(2)}, u32[]{:S(2)}) collective-permute-start(bf16[2,2,512,256]{3,2,1,0:T(8,128)(2,1)S(1)} %get-tuple-element.168), channel_id=1, source_target_pairs={{0,1},{1,0},{2,3},{3,2},{4,5},{5,4},{6,7},{7,6},{8,9},{9,8},{10,11... | collective-permute-start | bytes 3145736 | tf_op jit(solution)/shard_map/ppermute | solution.py:544
  92.3 2.3 %collective-permute-done.8 = bf16[2,2,512,256]{3,2,1,0:T(8,128)(2,1)S(1)} collective-permute-done((bf16[2,2,512,256]{3,2,1,0:T(8,128)(2,1)S(1)}, bf16[2,2,512,256]{3,2,1,0:T(8,128)(2,1)S(1)}, u32[]{:S(2)}, u32[]{:S(2)}) %collective-permute-start.8) | collective-permute-done | bytes 1048608 | tf_op jit(solution)/shard_map/ppermute | solution.py:544
  94.5 0.3 add_convert_fusion
  94.8 33.5 %all_to_all.15 = bf16[16,128,256]{2,1,0:T(8,128)(2,1)S(1)} all-to-all(bf16[16,128,256]{2,1,0:T(8,128)(2,1)S(1)} %bitcast.12), channel_id=1, replica_groups=mesh['yh'=2,'yl'=2,'xl'=2,'zh'=4,'za'=2,'zb'=2,'xh'=2,'core'=2] {'xl','x..., dimensions={0} | all-to-all | bytes 2097152 | tf_op jit(solution)/shard_map/all_to_all | solution.py:598
  128.3 0.1 reduce_sum.24
  128.4 28.8 %all_to_all.16 = bf16[4,128,256]{2,1,0:T(8,128)(2,1)S(1)} all-to-all(bf16[4,128,256]{2,1,0:T(8,128)(2,1)S(1)} %broadcast_in_dim.6), channel_id=1, replica_groups=mesh['yh'=2,'yl'=2,'xl'=2,'zh'=4,'za'=2,'zb'=2,'xh'=2,'core'=2] {'zh'}, dimensions={0} | all-to-all | bytes 524288 | tf_op jit(solution)/shard_map/all_to_all | solution.py:599
  157.3 14.8 %all_to_all.17 = bf16[8,128,256]{2,1,0:T(8,128)(2,1)S(1)} all-to-all(bf16[8,128,256]{2,1,0:T(8,128)(2,1)S(1)} %broadcast_in_dim.7), channel_id=1, replica_groups=mesh['yh'=2,'yl'=2,'xl'=2,'zh'=4,'za'=2,'zb'=2,'xh'=2,'core'=2] {'xh','z..., dimensions={0} | all-to-all | bytes 1048576 | tf_op jit(solution)/shard_map/all_to_all | solution.py:600
  172.2 7.9 %collective-permute-start.9 = (bf16[2,512,256]{2,1,0:T(8,128)(2,1)S(1)}, bf16[2,512,256]{2,1,0:T(8,128)(2,1)S(1)}, u32[]{:S(2)}, u32[]{:S(2)}) collective-permute-start(bf16[2,512,256]{2,1,0:T(8,128)(2,1)S(1)} %bitcast.10), channel_id=1, source_target_pairs={{0,1},{1,0},{2,3},{3,2},{4,5},{5,4},{6,7},{7,6},{8,9},{9,8},{10,11... | collective-permute-start | bytes 1572872 | tf_op jit(solution)/shard_map/ppermute | solution.py:544
  180.1 1.5 collective-permute-done.9.other
  181.6 1.6 shard_map.89
  (21 shorter events, 0.1 us)
Async XLA Ops:
  0.6 36.8 %copy-start.8 = (s32[4]{0:T(128)S(1)}, s32[4]{0:T(128)}, u32[]{:S(2)}) copy-start(s32[4]{0:T(128)} %virtual.3) | copy-start | bytes 52
  0.6 36.7 %copy-start.7 = (s32[4,2]{0,1:T(2,128)S(1)}, s32[4,2]{0,1:T(2,128)}, u32[]{:S(2)}) copy-start(s32[4,2]{0,1:T(2,128)} %param.14) | copy-start | bytes 100
  0.7 36.7 %copy-start.6 = (s32[4,2,2]{0,2,1:T(2,128)S(1)}, s32[4,2,2]{0,2,1:T(2,128)}, u32[]{:S(2)}) copy-start(s32[4,2,2]{0,2,1:T(2,128)} %param.13) | copy-start | bytes 196
  0.8 1.1 copy-start.1
  1.9 0.9 copy-start.2
  3.6 14.8 %collective-permute-start.3 = (bf16[2,512,256]{2,1,0:T(8,128)(2,1)S(1)}, bf16[2,512,256]{2,1,0:T(8,128)(2,1)S(1)}, u32[]{:S(2)}, u32[]{:S(2)}) collective-permute-start(bf16[2,512,256]{2,1,0:T(8,128)(2,1)S(1)} %get-tuple-element.148), channel_id=1, source_target_pairs={{0,192},{1,195},{2,194},{3,193},{64,128},{65,131},{66,130},{67,129... | collective-permute-start | bytes 1572872 | tf_op jit(solution)/shard_map/ppermute | solution.py:558
  9.9 23.6 %collective-permute-start.1 = (bf16[2,512,256]{2,1,0:T(8,128)(2,1)S(1)}, bf16[2,512,256]{2,1,0:T(8,128)(2,1)S(1)}, u32[]{:S(2)}, u32[]{:S(2)}) collective-permute-start(bf16[2,512,256]{2,1,0:T(8,128)(2,1)S(1)} %get-tuple-element.148), channel_id=1, source_target_pairs={{0,128},{1,129},{2,130},{3,131},{64,192},{65,193},{66,194},{67,195... | collective-permute-start | bytes 1572872 | tf_op jit(solution)/shard_map/ppermute | solution.py:558
  11.9 25.4 %collective-permute-start = (bf16[4,512,256]{2,1,0:T(8,128)(2,1)S(1)}, bf16[4,512,256]{2,1,0:T(8,128)(2,1)S(1)}, u32[]{:S(2)}, u32[]{:S(2)}) collective-permute-start(bf16[4,512,256]{2,1,0:T(8,128)(2,1)S(1)} %get-tuple-element.147.rest_0_), channel_id=1, source_target_pairs={{0,64},{1,67},{2,66},{3,65},{64,0},{65,3},{66,2},{67,1},{128,192},... | collective-permute-start | bytes 3145736 | tf_op jit(solution)/shard_map/ppermute | solution.py:558
  18.5 17.4 %collective-permute-start.4 = (bf16[2,512,256]{2,1,0:T(8,128)(2,1)S(1)}, bf16[2,512,256]{2,1,0:T(8,128)(2,1)S(1)}, u32[]{:S(2)}, u32[]{:S(2)}) collective-permute-start(bf16[2,512,256]{2,1,0:T(8,128)(2,1)S(1)} %collective-permute-done.3.rest_4_), channel_id=1, source_target_pairs={{0,1},{1,0},{2,3},{3,2},{4,5},{5,4},{6,7},{7,6},{8,9},{9,8},{10,11... | collective-permute-start | bytes 1572872 | tf_op jit(solution)/shard_map/ppermute | solution.py:544
  33.5 3.9 %collective-permute-start.2 = (bf16[2,512,256]{2,1,0:T(8,128)(2,1)S(1)}, bf16[2,512,256]{2,1,0:T(8,128)(2,1)S(1)}, u32[]{:S(2)}, u32[]{:S(2)}) collective-permute-start(bf16[2,512,256]{2,1,0:T(8,128)(2,1)S(1)} %collective-permute-done.1.rest_2_), channel_id=1, source_target_pairs={{0,1},{1,0},{2,3},{3,2},{4,5},{5,4},{6,7},{7,6},{8,9},{9,8},{10,11... | collective-permute-start | bytes 1572872 | tf_op jit(solution)/shard_map/ppermute | solution.py:544
  35.9 17.6 %copy-start.3 = (bf16[2,512,256]{2,1,0:T(8,128)(2,1)}, bf16[2,512,256]{2,1,0:T(8,128)(2,1)S(1)}, u32[]{:S(2)}) copy-start(bf16[2,512,256]{2,1,0:T(8,128)(2,1)S(1)} %collective-permute-done.4.rest_5_) | copy-start | bytes 1572868
  37.4 16.1 %copy-start.4 = (bf16[2,512,256]{2,1,0:T(8,128)(2,1)}, bf16[2,512,256]{2,1,0:T(8,128)(2,1)S(1)}, u32[]{:S(2)}) copy-start(bf16[2,512,256]{2,1,0:T(8,128)(2,1)S(1)} %collective-permute-done.2.rest_3_) | copy-start | bytes 1572868
  37.4 16.1 %copy-start = (bf16[4,128,512]{2,1,0:T(8,128)(2,1)S(1)}, bf16[4,128,512]{2,1,0:T(8,128)(2,1)}, u32[]{:S(2)}) copy-start(bf16[4,128,512]{2,1,0:T(8,128)(2,1)} %nodes_in.1) | copy-start | bytes 1572868
  37.4 16.1 %copy-start.5 = (bf16[4,128,512]{2,1,0:T(8,128)(2,1)S(1)}, bf16[4,128,512]{2,1,0:T(8,128)(2,1)}, u32[]{:S(2)}) copy-start(bf16[4,128,512]{2,1,0:T(8,128)(2,1)} %grad_in.1) | copy-start | bytes 1572868
  45.3 8.1 %collective-permute-start.5 = (bf16[128,512]{1,0:T(8,128)(2,1)}, bf16[128,512]{1,0:T(8,128)(2,1)S(1)}, u32[]{:S(2)}, u32[]{:S(2)}) collective-permute-start(bf16[128,512]{1,0:T(8,128)(2,1)} %get-tuple-element.149.sent), channel_id=1, source_target_pairs={{0,384},{128,256},{256,128},{384,0},{1,385},{129,257},{257,129},{3... | collective-permute-start | bytes 393224 | tf_op jit(solution)/shard_map/ppermute | solution.py:578
  59.5 11.1 %collective-permute-start.6 = (bf16[128,512]{1,0:T(8,128)(2,1)}, bf16[128,512]{1,0:T(8,128)(2,1)S(1)}, u32[]{:S(2)}, u32[]{:S(2)}) collective-permute-start(bf16[128,512]{1,0:T(8,128)(2,1)} %get-tuple-element.150), channel_id=1, source_target_pairs={{0,256},{128,384},{256,0},{384,128},{1,257},{129,385},{257,1},{385... | collective-permute-start | bytes 393224 | tf_op jit(solution)/shard_map/ppermute | solution.py:581
  67.7 7.7 %collective-permute-start.7 = (bf16[128,512]{1,0:T(8,128)(2,1)}, bf16[128,512]{1,0:T(8,128)(2,1)}, u32[]{:S(2)}, u32[]{:S(2)}) collective-permute-start(bf16[128,512]{1,0:T(8,128)(2,1)} %get-tuple-element.150), channel_id=1, source_target_pairs={{0,384},{128,256},{256,128},{384,0},{1,385},{129,257},{257,129},{3... | collective-permute-start | bytes 393224 | tf_op jit(solution)/shard_map/ppermute | solution.py:581
  88.2 6.4 %collective-permute-start.8 = (bf16[2,2,512,256]{3,2,1,0:T(8,128)(2,1)S(1)}, bf16[2,2,512,256]{3,2,1,0:T(8,128)(2,1)S(1)}, u32[]{:S(2)}, u32[]{:S(2)}) collective-permute-start(bf16[2,2,512,256]{3,2,1,0:T(8,128)(2,1)S(1)} %get-tuple-element.168), channel_id=1, source_target_pairs={{0,1},{1,0},{2,3},{3,2},{4,5},{5,4},{6,7},{7,6},{8,9},{9,8},{10,11... | collective-permute-start | bytes 3145736 | tf_op jit(solution)/shard_map/ppermute | solution.py:544
  172.2 9.4 %collective-permute-start.9 = (bf16[2,512,256]{2,1,0:T(8,128)(2,1)S(1)}, bf16[2,512,256]{2,1,0:T(8,128)(2,1)S(1)}, u32[]{:S(2)}, u32[]{:S(2)}) collective-permute-start(bf16[2,512,256]{2,1,0:T(8,128)(2,1)S(1)} %bitcast.10), channel_id=1, source_target_pairs={{0,1},{1,0},{2,3},{3,2},{4,5},{5,4},{6,7},{7,6},{8,9},{9,8},{10,11... | collective-permute-start | bytes 1572872 | tf_op jit(solution)/shard_map/ppermute | solution.py:544

commit v9 on v7

--- a/solution.py
+++ b/solution.py
@@ -591,7 +591,9 @@
     total = (keep.astype(F32) + swapped(send, "core").astype(F32)).astype(BF16)
     total = lax.all_to_all(total.reshape(4 * near, D // near, INNER), ("xl", "xh", "zb"), 0, 0, tiled=True)
     total = added(total.reshape(4 * near, D // near, INNER), 0).reshape(pairs, D // (near * pairs), INNER)
-    total = added(lax.all_to_all(total, "za", 0, 0, tiled=True), 0)
+    upper = lax.axis_index("za") == 1
+    kept, given = jnp.where(upper, total[1], total[0]), jnp.where(upper, total[0], total[1])
+    total = (kept.astype(F32) + swapped(given, "za").astype(F32)).astype(BF16)
     total = added(lax.all_to_all(repeated(total, far), "zh", 0, 0, tiled=True), 0)
     total = lax.all_to_all(repeated(total, 2 * near * pairs), ("xh", "zb", "za"), 0, 0, tiled=True)
     mine = total.reshape(2, D, INNER)

time: 178 us -> 183 us (1.028)
  blocking collectives: 72.5 us -> 51.9 us
  waiting for transfers between devices: 26.4 us -> 44 us
  starting transfers between devices: 46.1 us -> 53.7 us
    all_to_all x2 -> x0, blocking collectives: 28.7 us -> none  [the longest x1 19.8 us: per_device(): lax.all_to_all(total.reshape(4 * near, D // near, INNER), ('xl', 'xh', 'z...]
    all_to_all x0 -> x1, waiting for transfers between devices: none -> 15.3 us  [per_device(): lax.all_to_all(total.reshape(4 * near, D // near, INNER), ('xl', 'xh', 'z...]
    all_to_all x1, blocking collectives: 15.8 us -> 21.9 us  [per_device(): lax.all_to_all(repeated(total, 2 * near * pairs), ('xh', 'zb', 'za'), 0,...]
    all_to_all x0 -> x1, starting transfers between devices: none -> 5.11 us  [per_device(): lax.all_to_all(total.reshape(4 * near, D // near, INNER), ('xl', 'xh', 'z...]
    ppermute x4 -> x5, starting transfers between devices: 20.3 us -> 22.7 us  [swapped(): return lax.ppermute(value, axis, [(0, 1), (1, 0)])]
    ppermute x4 -> x5, waiting for transfers between devices: 5.28 us -> 7.62 us  [swapped(): return lax.ppermute(value, axis, [(0, 1), (1, 0)])]
    all_to_all x1, blocking collectives: 27.9 us -> 30 us  [per_device(): lax.all_to_all(repeated(total, far), 'zh', 0, 0, tiled=True)]
  transfers between devices with their start and end apart: 10 -> 12, of which waited for: 7 -> 9; matrix products, arithmetic and copies ran while one was open for 0% -> 0% of each run, Pallas kernels for 0% -> 0%
where the time goes in v9:
time: 183 us
  starting transfers between devices  53.7 us (29%)
  blocking collectives  51.9 us (28%)
  waiting for transfers between devices  44 us (24%)
  Pallas kernels  27.4 us (15%)
  local copies, waits for them, and re-layouts  3.15 us (2%)
    all_to_all x1, blocking collectives, per_device(): lax.all_to_all(repeated(total, far), 'zh', 0, 0, tiled=True)  30 us
    pallas_call x5, Pallas kernels, call(): pl.pallas_call(kernel, grid_spec=pltpu.PrefetchScalarGridSpec(num_scalar_...  27.4 us
    ppermute x5, starting transfers between devices, swapped(): return lax.ppermute(value, axis, [(0, 1), (1, 0)])  22.7 us
    all_to_all x1, blocking collectives, per_device(): lax.all_to_all(repeated(total, 2 * near * pairs), ('xh', 'zb', 'za'), 0,...  21.9 us
    all_to_all x1, waiting for transfers between devices, per_device(): lax.all_to_all(total.reshape(4 * near, D // near, INNER), ('xl', 'xh', 'z...  15.3 us
    ppermute x3, waiting for transfers between devices, fetched(): return lax.ppermute(value, axes, pairs)  13.2 us
    ppermute x3, starting transfers between devices, fetched(): return lax.ppermute(value, axes, pairs)  10.3 us
    ppermute x1, starting transfers between devices, per_device(): lax.ppermute(grad, pair, crossed)  7.98 us
  transfers between devices with their start and end apart: 12, of which 9 were waited for; matrix products, arithmetic and copies ran while one was open for 0% of the time, Pallas kernels for 0%

profile of v9, /device:TPU:1, one launch (start us, length us, event | category | flops | bytes accessed | tf_op | source)
XLA Modules:
  0.0 182.8 jit_solution(10513726265779973134)
XLA Ops:
  0.8 1.1 copy-done.1
  1.9 0.9 copy-done.2
  3.6 6.2 %collective-permute-start.3 = (bf16[2,512,256]{2,1,0:T(8,128)(2,1)S(1)}, bf16[2,512,256]{2,1,0:T(8,128)(2,1)S(1)}, u32[]{:S(2)}, u32[]{:S(2)}) collective-permute-start(bf16[2,512,256]{2,1,0:T(8,128)(2,1)S(1)} %get-tuple-element.148), channel_id=1, source_target_pairs={{0,192},{1,195},{2,194},{3,193},{64,128},{65,131},{66,130},{67,129... | collective-permute-start | bytes 1572872 | tf_op jit(solution)/shard_map/ppermute | solution.py:554
  9.9 2.1 %collective-permute-start.1 = (bf16[2,512,256]{2,1,0:T(8,128)(2,1)S(1)}, bf16[2,512,256]{2,1,0:T(8,128)(2,1)S(1)}, u32[]{:S(2)}, u32[]{:S(2)}) collective-permute-start(bf16[2,512,256]{2,1,0:T(8,128)(2,1)S(1)} %get-tuple-element.148), channel_id=1, source_target_pairs={{0,128},{1,129},{2,130},{3,131},{64,192},{65,193},{66,194},{67,195... | collective-permute-start | bytes 1572872 | tf_op jit(solution)/shard_map/ppermute | solution.py:554
  11.9 2.0 %collective-permute-start = (bf16[4,512,256]{2,1,0:T(8,128)(2,1)S(1)}, bf16[4,512,256]{2,1,0:T(8,128)(2,1)S(1)}, u32[]{:S(2)}, u32[]{:S(2)}) collective-permute-start(bf16[4,512,256]{2,1,0:T(8,128)(2,1)S(1)} %get-tuple-element.147.rest_0_), channel_id=1, source_target_pairs={{0,64},{1,67},{2,66},{3,65},{64,0},{65,3},{66,2},{67,1},{128,192},... | collective-permute-start | bytes 3145736 | tf_op jit(solution)/shard_map/ppermute | solution.py:554
  14.0 4.5 %collective-permute-done.3.rest_4_ = bf16[2,512,256]{2,1,0:T(8,128)(2,1)S(1)} collective-permute-done((bf16[2,512,256]{2,1,0:T(8,128)(2,1)S(1)}, bf16[2,512,256]{2,1,0:T(8,128)(2,1)S(1)}, u32[]{:S(2)}, u32[]{:S(2)}) %collective-permute-start.3) | collective-permute-done | bytes 524320 | tf_op jit(solution)/shard_map/ppermute | solution.py:554
  18.5 6.3 %collective-permute-start.4 = (bf16[2,512,256]{2,1,0:T(8,128)(2,1)S(1)}, bf16[2,512,256]{2,1,0:T(8,128)(2,1)S(1)}, u32[]{:S(2)}, u32[]{:S(2)}) collective-permute-start(bf16[2,512,256]{2,1,0:T(8,128)(2,1)S(1)} %collective-permute-done.3.rest_4_), channel_id=1, source_target_pairs={{0,1},{1,0},{2,3},{3,2},{4,5},{5,4},{6,7},{7,6},{8,9},{9,8},{10,11... | collective-permute-start | bytes 1572872 | tf_op jit(solution)/shard_map/ppermute | solution.py:540
  24.7 8.7 %collective-permute-done.1.rest_2_ = bf16[2,512,256]{2,1,0:T(8,128)(2,1)S(1)} collective-permute-done((bf16[2,512,256]{2,1,0:T(8,128)(2,1)S(1)}, bf16[2,512,256]{2,1,0:T(8,128)(2,1)S(1)}, u32[]{:S(2)}, u32[]{:S(2)}) %collective-permute-start.1) | collective-permute-done | bytes 524320 | tf_op jit(solution)/shard_map/ppermute | solution.py:554
  33.5 2.4 %collective-permute-start.2 = (bf16[2,512,256]{2,1,0:T(8,128)(2,1)S(1)}, bf16[2,512,256]{2,1,0:T(8,128)(2,1)S(1)}, u32[]{:S(2)}, u32[]{:S(2)}) collective-permute-start(bf16[2,512,256]{2,1,0:T(8,128)(2,1)S(1)} %collective-permute-done.1.rest_2_), channel_id=1, source_target_pairs={{0,1},{1,0},{2,3},{3,2},{4,5},{5,4},{6,7},{7,6},{8,9},{9,8},{10,11... | collective-permute-start | bytes 1572872 | tf_op jit(solution)/shard_map/ppermute | solution.py:540
  35.9 1.5 collective-permute-done.2.rest_3_
  37.4 7.2 %shard_map.87 = (bf16[128,512]{1,0:T(8,128)(2,1)}, bf16[4,128,512]{2,1,0:T(8,128)(2,1)}, f32[4,128,128]{2,1,0:T(8,128)}, bf16[4,3,128,256]{3,2,1,0:T(8,128)(2,1)...) custom-call(s32[6]{0:T(128)S(1)} %stack.27.info, ...), custom_call_target="tpu_custom_call" | custom-call | tf_op jit(solution)/shard_map/pallas_call | solution.py:453
  44.7 4.6 %collective-permute-start.5 = (bf16[128,512]{1,0:T(8,128)(2,1)}, bf16[128,512]{1,0:T(8,128)(2,1)S(1)}, u32[]{:S(2)}, u32[]{:S(2)}) collective-permute-start(bf16[128,512]{1,0:T(8,128)(2,1)} %get-tuple-element.149.sent), channel_id=1, source_target_pairs={{0,384},{128,256},{256,128},{384,0},{1,385},{129,257},{257,129},{3... | collective-permute-start | bytes 393224 | tf_op jit(solution)/shard_map/ppermute | solution.py:574
  49.3 3.5 %collective-permute-done.5.hidden_in = bf16[128,512]{1,0:T(8,128)(2,1)S(1)} collective-permute-done((bf16[128,512]{1,0:T(8,128)(2,1)}, bf16[128,512]{1,0:T(8,128)(2,1)S(1)}, u32[]{:S(2)}, u32[]{:S(2)}) %collective-permute-start.5) | collective-permute-done | bytes 131104 | tf_op jit(solution)/shard_map/ppermute | solution.py:574
  52.8 0.9 copy-done.3
  53.7 6.0 %shard_map.88 = (bf16[128,512]{1,0:T(8,128)(2,1)S(1)}, bf16[4,128,512]{2,1,0:T(8,128)(2,1)}, bf16[4,128,256]{2,1,0:T(8,128)(2,1)}, bf16[4,128,768]{2,1,0:T(8,128...) custom-call(s32[6]{0:T(128)S(1)} %stack.27.info, ...), custom_call_target="tpu_custom_call" | custom-call | tf_op jit(solution)/shard_map/pallas_call | solution.py:453
  59.7 8.0 %collective-permute-start.6 = (bf16[128,512]{1,0:T(8,128)(2,1)S(1)}, bf16[128,512]{1,0:T(8,128)(2,1)S(1)}, u32[]{:S(2)}, u32[]{:S(2)}) collective-permute-start(bf16[128,512]{1,0:T(8,128)(2,1)S(1)} %get-tuple-element.150), channel_id=1, source_target_pairs={{0,256},{128,384},{256,0},{384,128},{1,257},{129,385},{257,1},{385... | collective-permute-start | bytes 393224 | tf_op jit(solution)/shard_map/ppermute | solution.py:577
  67.7 2.9 %collective-permute-start.7 = (bf16[128,512]{1,0:T(8,128)(2,1)S(1)}, bf16[128,512]{1,0:T(8,128)(2,1)S(1)}, u32[]{:S(2)}, u32[]{:S(2)}) collective-permute-start(bf16[128,512]{1,0:T(8,128)(2,1)S(1)} %get-tuple-element.150), channel_id=1, source_target_pairs={{0,384},{128,256},{256,128},{384,0},{1,385},{129,257},{257,129},{3... | collective-permute-start | bytes 393224 | tf_op jit(solution)/shard_map/ppermute | solution.py:577
  70.7 4.4 %collective-permute-done.7 = bf16[128,512]{1,0:T(8,128)(2,1)S(1)} collective-permute-done((bf16[128,512]{1,0:T(8,128)(2,1)S(1)}, bf16[128,512]{1,0:T(8,128)(2,1)S(1)}, u32[]{:S(2)}, u32[]{:S(2)}) %collective-permute-start.7) | collective-permute-done | bytes 131104 | tf_op jit(solution)/shard_map/ppermute | solution.py:577
  75.1 11.9 %conditional.2 = (bf16[2,2,512,256]{3,2,1,0:T(8,128)(2,1)S(1)}, bf16[2,2,512,256]{3,2,1,0:T(8,128)(2,1)S(1)}) conditional(s32[]{:T(128)} %convert_element_type.28, (s32[6]{0:T(128)S(1)}, s32[2,2,4]{2,1,0:T(2,128)S(1)}, s32[2,4]{1,0:T(2,128)S(1)}, s32[4]{0:T(128)S(1)}, bf16[128,512]{1,0:T(8,128)(2,1)S(1)}, /*index=5*/bf16[4,128,512]{2,1,0:T(8,128)(2,1)}, ...), branch_computations={%region_0.1_spmd, %region_1.2_spmd} | conditional | bytes 16
  75.1 11.9 %branch_1_fun.1 = (bf16[2,2,512,256]{3,2,1,0:T(8,128)(2,1)S(1)}, bf16[2,2,512,256]{3,2,1,0:T(8,128)(2,1)S(1)}) custom-call(s32[6]{0:T(128)S(1)} %get-tuple-element.100.info, bf16[128,512]{1,0:T(8,128)(2,1)S(1)} %get-tuple-element.101.grad_in, bf16[128,512]{1,0:T(8,128)(2,1)S(1)} %get-tuple-element.102.grad_in2, ...), custom_call_target="tpu_custom_call" | custom-call | tf_op jit(solution)/shard_map/cond/branch_1_fun/pallas_call | solution.py:453
  87.0 4.1 %collective-permute-start.8 = (bf16[2,2,512,256]{3,2,1,0:T(8,128)(2,1)S(1)}, bf16[2,2,512,256]{3,2,1,0:T(8,128)(2,1)S(1)}, u32[]{:S(2)}, u32[]{:S(2)}) collective-permute-start(bf16[2,2,512,256]{3,2,1,0:T(8,128)(2,1)S(1)} %get-tuple-element.168), channel_id=1, source_target_pairs={{0,1},{1,0},{2,3},{3,2},{4,5},{5,4},{6,7},{7,6},{8,9},{9,8},{10,11... | collective-permute-start | bytes 3145736 | tf_op jit(solution)/shard_map/ppermute | solution.py:540
  91.1 2.3 %collective-permute-done.8 = bf16[2,2,512,256]{3,2,1,0:T(8,128)(2,1)S(1)} collective-permute-done((bf16[2,2,512,256]{3,2,1,0:T(8,128)(2,1)S(1)}, bf16[2,2,512,256]{3,2,1,0:T(8,128)(2,1)S(1)}, u32[]{:S(2)}, u32[]{:S(2)}) %collective-permute-start.8) | collective-permute-done | bytes 1048608 | tf_op jit(solution)/shard_map/ppermute | solution.py:540
  93.3 1.3 add_convert_fusion
  94.6 5.1 %all-to-all-start = ((bf16[8,256,256]{2,1,0:T(8,128)(2,1)}), bf16[8,256,256]{2,1,0:T(8,128)(2,1)S(1)}, u32[]{:S(2)}, u32[]{:S(2)}) async-start(bf16[8,256,256]{2,1,0:T(8,128)(2,1)} %bitcast.8), calls=%async_computation | async-start | bytes 2097152 | tf_op jit(solution)/shard_map/all_to_all | solution.py:592
  99.7 15.3 %all-to-all-done = bf16[8,256,256]{2,1,0:T(8,128)(2,1)S(1)} async-done(((bf16[8,256,256]{2,1,0:T(8,128)(2,1)}), bf16[8,256,256]{2,1,0:T(8,128)(2,1)S(1)}, u32[]{:S(2)}, u32[]{:S(2)}) %all-to-all-start) | async-done | bytes 1048608 | tf_op jit(solution)/shard_map/all_to_all | solution.py:592
  115.2 4.9 %collective-permute-start.9 = (bf16[128,256]{1,0:T(8,128)(2,1)S(1)}, bf16[128,256]{1,0:T(8,128)(2,1)S(1)}, u32[]{:S(2)}, u32[]{:S(2)}) collective-permute-start(bf16[128,256]{1,0:T(8,128)(2,1)S(1)} %broadcast_select_fusion), channel_id=1, source_target_pairs={{0,8},{8,0},{1,9},{9,1},{2,10},{10,2},{3,11},{11,3},{4,12},{12,4},... | collective-permute-start | bytes 196616 | tf_op jit(solution)/shard_map/ppermute | solution.py:540
  120.1 2.3 %collective-permute-done.9 = bf16[128,256]{1,0:T(8,128)(2,1)S(1)} collective-permute-done((bf16[128,256]{1,0:T(8,128)(2,1)S(1)}, bf16[128,256]{1,0:T(8,128)(2,1)S(1)}, u32[]{:S(2)}, u32[]{:S(2)}) %collective-permute-start.9) | collective-permute-done | bytes 65568 | tf_op jit(solution)/shard_map/ppermute | solution.py:540
  122.5 30.0 %all_to_all.15 = bf16[4,128,256]{2,1,0:T(8,128)(2,1)S(1)} all-to-all(bf16[4,128,256]{2,1,0:T(8,128)(2,1)S(1)} %broadcast_in_dim.6), channel_id=1, replica_groups=mesh['yh'=2,'yl'=2,'xl'=2,'zh'=4,'za'=2,'zb'=2,'xh'=2,'core'=2] {'zh'}, dimensions={0} | all-to-all | bytes 524288 | tf_op jit(solution)/shard_map/all_to_all | solution.py:597
  152.6 21.9 %all_to_all.16 = bf16[8,128,256]{2,1,0:T(8,128)(2,1)S(1)} all-to-all(bf16[8,128,256]{2,1,0:T(8,128)(2,1)S(1)} %broadcast_in_dim.7), channel_id=1, replica_groups=mesh['yh'=2,'yl'=2,'xl'=2,'zh'=4,'za'=2,'zb'=2,'xh'=2,'core'=2] {'xh','z..., dimensions={0} | all-to-all | bytes 1048576 | tf_op jit(solution)/shard_map/all_to_all | solution.py:598
  174.5 5.0 %collective-permute-start.10 = (bf16[2,512,256]{2,1,0:T(8,128)(2,1)S(1)}, bf16[2,512,256]{2,1,0:T(8,128)(2,1)S(1)}, u32[]{:S(2)}, u32[]{:S(2)}) collective-permute-start(bf16[2,512,256]{2,1,0:T(8,128)(2,1)S(1)} %bitcast.10), channel_id=1, source_target_pairs={{0,1},{1,0},{2,3},{3,2},{4,5},{5,4},{6,7},{7,6},{8,9},{9,8},{10,11... | collective-permute-start | bytes 1572872 | tf_op jit(solution)/shard_map/ppermute | solution.py:540
  179.6 1.5 collective-permute-done.10.other
  181.1 1.6 shard_map.89
  (28 shorter events, 1.2 us)
Async XLA Ops:
  0.6 36.8 %copy-start.9 = (s32[4]{0:T(128)S(1)}, s32[4]{0:T(128)}, u32[]{:S(2)}) copy-start(s32[4]{0:T(128)} %virtual.3) | copy-start | bytes 52
  0.6 36.8 %copy-start.8 = (s32[4,2]{0,1:T(2,128)S(1)}, s32[4,2]{0,1:T(2,128)}, u32[]{:S(2)}) copy-start(s32[4,2]{0,1:T(2,128)} %param.14) | copy-start | bytes 100
  0.7 36.7 %copy-start.7 = (s32[4,2,2]{0,2,1:T(2,128)S(1)}, s32[4,2,2]{0,2,1:T(2,128)}, u32[]{:S(2)}) copy-start(s32[4,2,2]{0,2,1:T(2,128)} %param.13) | copy-start | bytes 196
  0.8 1.1 copy-start.1
  1.9 0.9 copy-start.2
  3.6 14.8 %collective-permute-start.3 = (bf16[2,512,256]{2,1,0:T(8,128)(2,1)S(1)}, bf16[2,512,256]{2,1,0:T(8,128)(2,1)S(1)}, u32[]{:S(2)}, u32[]{:S(2)}) collective-permute-start(bf16[2,512,256]{2,1,0:T(8,128)(2,1)S(1)} %get-tuple-element.148), channel_id=1, source_target_pairs={{0,192},{1,195},{2,194},{3,193},{64,128},{65,131},{66,130},{67,129... | collective-permute-start | bytes 1572872 | tf_op jit(solution)/shard_map/ppermute | solution.py:554
  9.9 23.6 %collective-permute-start.1 = (bf16[2,512,256]{2,1,0:T(8,128)(2,1)S(1)}, bf16[2,512,256]{2,1,0:T(8,128)(2,1)S(1)}, u32[]{:S(2)}, u32[]{:S(2)}) collective-permute-start(bf16[2,512,256]{2,1,0:T(8,128)(2,1)S(1)} %get-tuple-element.148), channel_id=1, source_target_pairs={{0,128},{1,129},{2,130},{3,131},{64,192},{65,193},{66,194},{67,195... | collective-permute-start | bytes 1572872 | tf_op jit(solution)/shard_map/ppermute | solution.py:554
  11.9 25.4 %collective-permute-start = (bf16[4,512,256]{2,1,0:T(8,128)(2,1)S(1)}, bf16[4,512,256]{2,1,0:T(8,128)(2,1)S(1)}, u32[]{:S(2)}, u32[]{:S(2)}) collective-permute-start(bf16[4,512,256]{2,1,0:T(8,128)(2,1)S(1)} %get-tuple-element.147.rest_0_), channel_id=1, source_target_pairs={{0,64},{1,67},{2,66},{3,65},{64,0},{65,3},{66,2},{67,1},{128,192},... | collective-permute-start | bytes 3145736 | tf_op jit(solution)/shard_map/ppermute | solution.py:554
  18.5 17.4 %collective-permute-start.4 = (bf16[2,512,256]{2,1,0:T(8,128)(2,1)S(1)}, bf16[2,512,256]{2,1,0:T(8,128)(2,1)S(1)}, u32[]{:S(2)}, u32[]{:S(2)}) collective-permute-start(bf16[2,512,256]{2,1,0:T(8,128)(2,1)S(1)} %collective-permute-done.3.rest_4_), channel_id=1, source_target_pairs={{0,1},{1,0},{2,3},{3,2},{4,5},{5,4},{6,7},{7,6},{8,9},{9,8},{10,11... | collective-permute-start | bytes 1572872 | tf_op jit(solution)/shard_map/ppermute | solution.py:540
  33.5 3.9 %collective-permute-start.2 = (bf16[2,512,256]{2,1,0:T(8,128)(2,1)S(1)}, bf16[2,512,256]{2,1,0:T(8,128)(2,1)S(1)}, u32[]{:S(2)}, u32[]{:S(2)}) collective-permute-start(bf16[2,512,256]{2,1,0:T(8,128)(2,1)S(1)} %collective-permute-done.1.rest_2_), channel_id=1, source_target_pairs={{0,1},{1,0},{2,3},{3,2},{4,5},{5,4},{6,7},{7,6},{8,9},{9,8},{10,11... | collective-permute-start | bytes 1572872 | tf_op jit(solution)/shard_map/ppermute | solution.py:540
  35.9 16.9 %copy-start.4 = (bf16[2,512,256]{2,1,0:T(8,128)(2,1)}, bf16[2,512,256]{2,1,0:T(8,128)(2,1)S(1)}, u32[]{:S(2)}) copy-start(bf16[2,512,256]{2,1,0:T(8,128)(2,1)S(1)} %collective-permute-done.4.rest_5_) | copy-start | bytes 1572868
  37.4 15.4 %copy-start.5 = (bf16[2,512,256]{2,1,0:T(8,128)(2,1)}, bf16[2,512,256]{2,1,0:T(8,128)(2,1)S(1)}, u32[]{:S(2)}) copy-start(bf16[2,512,256]{2,1,0:T(8,128)(2,1)S(1)} %collective-permute-done.2.rest_3_) | copy-start | bytes 1572868
  37.4 15.4 %copy-start = (bf16[4,128,512]{2,1,0:T(8,128)(2,1)S(1)}, bf16[4,128,512]{2,1,0:T(8,128)(2,1)}, u32[]{:S(2)}) copy-start(bf16[4,128,512]{2,1,0:T(8,128)(2,1)} %nodes_in.1) | copy-start | bytes 1572868
  37.4 15.4 %copy-start.6 = (bf16[4,128,512]{2,1,0:T(8,128)(2,1)S(1)}, bf16[4,128,512]{2,1,0:T(8,128)(2,1)}, u32[]{:S(2)}) copy-start(bf16[4,128,512]{2,1,0:T(8,128)(2,1)} %grad_in.1) | copy-start | bytes 1572868
  44.7 8.1 %collective-permute-start.5 = (bf16[128,512]{1,0:T(8,128)(2,1)}, bf16[128,512]{1,0:T(8,128)(2,1)S(1)}, u32[]{:S(2)}, u32[]{:S(2)}) collective-permute-start(bf16[128,512]{1,0:T(8,128)(2,1)} %get-tuple-element.149.sent), channel_id=1, source_target_pairs={{0,384},{128,256},{256,128},{384,0},{1,385},{129,257},{257,129},{3... | collective-permute-start | bytes 393224 | tf_op jit(solution)/shard_map/ppermute | solution.py:574
  52.8 0.9 copy-start.3
  59.7 10.9 %collective-permute-start.6 = (bf16[128,512]{1,0:T(8,128)(2,1)S(1)}, bf16[128,512]{1,0:T(8,128)(2,1)S(1)}, u32[]{:S(2)}, u32[]{:S(2)}) collective-permute-start(bf16[128,512]{1,0:T(8,128)(2,1)S(1)} %get-tuple-element.150), channel_id=1, source_target_pairs={{0,256},{128,384},{256,0},{384,128},{1,257},{129,385},{257,1},{385... | collective-permute-start | bytes 393224 | tf_op jit(solution)/shard_map/ppermute | solution.py:577
  67.7 7.4 %collective-permute-start.7 = (bf16[128,512]{1,0:T(8,128)(2,1)S(1)}, bf16[128,512]{1,0:T(8,128)(2,1)S(1)}, u32[]{:S(2)}, u32[]{:S(2)}) collective-permute-start(bf16[128,512]{1,0:T(8,128)(2,1)S(1)} %get-tuple-element.150), channel_id=1, source_target_pairs={{0,384},{128,256},{256,128},{384,0},{1,385},{129,257},{257,129},{3... | collective-permute-start | bytes 393224 | tf_op jit(solution)/shard_map/ppermute | solution.py:577
  87.0 6.4 %collective-permute-start.8 = (bf16[2,2,512,256]{3,2,1,0:T(8,128)(2,1)S(1)}, bf16[2,2,512,256]{3,2,1,0:T(8,128)(2,1)S(1)}, u32[]{:S(2)}, u32[]{:S(2)}) collective-permute-start(bf16[2,2,512,256]{3,2,1,0:T(8,128)(2,1)S(1)} %get-tuple-element.168), channel_id=1, source_target_pairs={{0,1},{1,0},{2,3},{3,2},{4,5},{5,4},{6,7},{7,6},{8,9},{9,8},{10,11... | collective-permute-start | bytes 3145736 | tf_op jit(solution)/shard_map/ppermute | solution.py:540
  94.6 20.4 %all-to-all-start = ((bf16[8,256,256]{2,1,0:T(8,128)(2,1)}), bf16[8,256,256]{2,1,0:T(8,128)(2,1)S(1)}, u32[]{:S(2)}, u32[]{:S(2)}) async-start(bf16[8,256,256]{2,1,0:T(8,128)(2,1)} %bitcast.8), calls=%async_computation | async-start | bytes 2097152 | tf_op jit(solution)/shard_map/all_to_all | solution.py:592
  115.2 7.2 %collective-permute-start.9 = (bf16[128,256]{1,0:T(8,128)(2,1)S(1)}, bf16[128,256]{1,0:T(8,128)(2,1)S(1)}, u32[]{:S(2)}, u32[]{:S(2)}) collective-permute-start(bf16[128,256]{1,0:T(8,128)(2,1)S(1)} %broadcast_select_fusion), channel_id=1, source_target_pairs={{0,8},{8,0},{1,9},{9,1},{2,10},{10,2},{3,11},{11,3},{4,12},{12,4},... | collective-permute-start | bytes 196616 | tf_op jit(solution)/shard_map/ppermute | solution.py:540
  174.5 6.6 %collective-permute-start.10 = (bf16[2,512,256]{2,1,0:T(8,128)(2,1)S(1)}, bf16[2,512,256]{2,1,0:T(8,128)(2,1)S(1)}, u32[]{:S(2)}, u32[]{:S(2)}) collective-permute-start(bf16[2,512,256]{2,1,0:T(8,128)(2,1)S(1)} %bitcast.10), channel_id=1, source_target_pairs={{0,1},{1,0},{2,3},{3,2},{4,5},{5,4},{6,7},{7,6},{8,9},{9,8},{10,11... | collective-permute-start | bytes 1572872 | tf_op jit(solution)/shard_map/ppermute | solution.py:540
